TPU v7x, 32 devices: a whole 2x2x4 slice. The times are simulated.
32 devices in a mesh: groups: 2 (over y), adapter: 8 (over z, x), fsdp: 2 (over core).
Axes of the slice: x: 2, y: 2, z: 4, core: 2. Of those that a mesh axis runs over, the one named last changes fastest.
Arguments:
- hidden: bfloat16 [3840, 8192], P(('groups', 'adapter', 'fsdp')), parts along dimension 0, may hold values from -6 to 6
- adapter_ids: int32 [3840, 1], P(('groups', 'adapter', 'fsdp')), parts along dimension 0, may hold values from 0 to 7; in each aligned block of 120 rows (0 to 119, 120 to 239, ...) at most 30 rows name the same one
- owner_map: int32 [8], replicated, may hold values from 0 to 7, each once
- down_a: bfloat16 [8, 8192, 64], P('adapter', 'fsdp'), may hold values from -0.0625 to 0.0625
- up_b: bfloat16 [8, 64, 8192], P('adapter', None, 'fsdp'), may hold values from -0.75 to 0.75
- norm_gain: bfloat16 [8192], P('fsdp'), may hold values from 0.5 to 1.5
- reward_head: bfloat16 [8192], P('fsdp'), may hold values from -0.0625 to 0.0625
Outputs:
- adapted: bfloat16 [3840, 8192], P(('groups', 'adapter', 'fsdp')), parts along dimension 0
- scores: float32 [3840], P(('groups', 'adapter', 'fsdp')), parts along dimension 0
There are 2 independent parts, one for each index of `groups`. A program takes and returns all parts, laid end to end along the dimension named above; an argument that names none is the same for every part. Nothing has to cross between parts.
Inputs may be any that keep to these rules, and one draw needn't show every extreme that they name: `adapter_ids`: the rows of one device name any one adapter at most 30 times; some adapter exactly 30 times. `owner_map`: each position appears once.
All inputs are finite; a program needn't handle non-finite values.
Results may differ from a plain program's by a relative error of at most 0.007.
Values may be sent and summed in bfloat16 or wider, within the bound.
No kernel may reach another device: no remote copies, remote signals or barrier semaphores. Data moves between devices by JAX's collectives and lax.ppermute only.
A program may use at most 64 MiB of HBM per device.

v0:
```python
import jax
import jax.numpy as jnp
from jax import lax
from jax.sharding import PartitionSpec as P


def per_device(hidden, adapter_ids, owner_map, down_a, up_b, norm_gain, reward_head):
    gain, head = (
        lax.all_gather(norm_gain, "fsdp", axis=0, tiled=True),
        lax.all_gather(reward_head, "fsdp", axis=0, tiled=True),
    )
    values = hidden.astype(jnp.float32)
    factor = lax.rsqrt(jnp.mean(values * values, axis=-1, keepdims=True) + 1e-05)
    normed = (values * factor * gain.astype(jnp.float32)).astype(jnp.bfloat16)
    row_count, width = hidden.shape
    lanes = lax.axis_size("adapter")
    capacity = max(2, (2 * row_count + lanes - 1) // lanes)
    table_size = owner_map.shape[0]
    picked = (
        adapter_ids[:, 0][:, None] == jnp.arange(table_size, dtype=jnp.int32)[None, :]
    ).astype(jnp.int32)
    owners = jnp.sum(picked * owner_map[None, :], axis=1)
    marks = (owners[:, None] == jnp.arange(lanes, dtype=jnp.int32)[None, :]).astype(jnp.int32)
    ranks = jnp.sum(jnp.cumsum(marks, axis=0) * marks, axis=1) - 1
    target = owners * capacity + ranks
    outgoing = jnp.zeros((lanes * capacity, width), jnp.bfloat16).at[target].set(normed)
    outgoing = outgoing.reshape(lanes, capacity, width)
    full_a, full_b = (
        lax.all_gather(down_a, "fsdp", axis=1, tiled=True),
        lax.all_gather(up_b, "fsdp", axis=2, tiled=True),
    )
    matrix_a = full_a[0]
    matrix_b = full_b[0]
    received = lax.all_to_all(outgoing, "adapter", split_axis=0, concat_axis=0, tiled=True)
    flat = received.reshape(-1, width)
    codes = jnp.dot(flat, matrix_a, preferred_element_type=jnp.float32).astype(jnp.bfloat16)
    delta = jnp.dot(codes, matrix_b, preferred_element_type=jnp.float32).astype(jnp.bfloat16)
    returned = lax.all_to_all(
        delta.reshape(received.shape), "adapter", split_axis=0, concat_axis=0, tiled=True
    )
    delta = returned.reshape(-1, width)[target]
    adapted = (normed.astype(jnp.float32) + 2.0 * delta.astype(jnp.float32)).astype(jnp.bfloat16)
    scores = jnp.dot(adapted, head, preferred_element_type=jnp.float32)
    return (adapted, scores)


def solution(mesh):
    placed = (
        P(("groups", "adapter", "fsdp"), None),
        P(("groups", "adapter", "fsdp"), None),
        P(),
        P("adapter", "fsdp", None),
        P("adapter", None, "fsdp"),
        P("fsdp"),
        P("fsdp"),
    )
    return jax.shard_map(
        per_device,
        mesh=mesh,
        in_specs=placed,
        out_specs=(P(("groups", "adapter", "fsdp"), None), P(("groups", "adapter", "fsdp"))),
        check_vma=False,
    )
```

profile of v0, /device:TPU:0, one launch (start us, length us, event | category | flops | bytes accessed | tf_op | source)
XLA Modules:
  0.0 261.4 jit_solution(6560783550564161433)
XLA Ops:
  7.2 0.9 select_reduce_fusion.1
  8.0 0.1 fusion.9
  8.1 0.2 reduce_window_sum.11
  8.3 0.2 select_reduce_fusion
  8.5 2.2 all_gather.12
  10.6 2.0 fusion
  12.7 6.9 %scatter_custom_fusion = bf16[240,8192]{1,0:T(8,128)(2,1)} fusion(s32[120]{0:T(128)S(1)} %fusion.10, bf16[]{:T(256)} %constant.7.clone.1, bf16[120,8192]{1,0:T(8,128)(2,1)} %param.7, f32[8192]{0:T(1024)S(1)} %convert_element_type.29, f32[120]{0:T(128)S(1)} %add_rsqrt_fusion), kind=kCustom, calls=%fused_computation.9 | custom fusion | flops 3932160 | bytes 5931522 | tf_op jit(solution)/shard_map/scatter | solution.py:26
  19.6 4.2 %reshape.58 = bf16[8,30,8192]{2,1,0:T(8,128)(2,1)} reshape(bf16[240,8192]{1,0:T(8,128)(2,1)} %scatter_custom_fusion) | data formatting | bytes 7864320 | tf_op jit(solution)/shard_map/reshape | solution.py:27
  23.7 7.1 %all-to-all-start = ((bf16[8,30,8192]{2,1,0:T(8,128)(2,1)}), bf16[8,30,8192]{2,1,0:T(8,128)(2,1)}, u32[]{:S(2)}, u32[]{:S(2)}) async-start(bf16[8,30,8192]{2,1,0:T(8,128)(2,1)} %reshape.58), calls=%async_computation | async-start | bytes 8388608 | tf_op jit(solution)/shard_map/all_to_all | solution.py:34
  30.9 0.0 all-gather.3.cloned.1.call-start
  30.9 0.7 all-gather.3.cloned.1.call-update
  31.6 0.0 all-gather.5.cloned.1.call-start
  31.6 0.7 all-gather.5.cloned.1.call-update
  32.3 92.2 %all-to-all-done = bf16[8,30,8192]{2,1,0:T(8,128)(2,1)} async-done(((bf16[8,30,8192]{2,1,0:T(8,128)(2,1)}), bf16[8,30,8192]{2,1,0:T(8,128)(2,1)}, u32[]{:S(2)}, u32[]{:S(2)}) %all-to-all-start) | async-done | bytes 3932192 | tf_op jit(solution)/shard_map/all_to_all | solution.py:34
  124.5 4.1 %reshape.59 = bf16[240,8192]{1,0:T(8,128)(2,1)} reshape(bf16[8,30,8192]{2,1,0:T(8,128)(2,1)} %all-to-all-done) | data formatting | bytes 7864320 | tf_op jit(solution)/shard_map/reshape | solution.py:35
  128.6 0.0 all-gather.3.cloned.1.call-done
  128.6 0.0 all-gather.5.cloned.1.call-done
  128.6 9.0 %convolution_convert_fusion = bf16[240,8192]{1,0:T(8,128)(2,1)} fusion(bf16[240,8192]{1,0:T(8,128)(2,1)} %reshape.59, bf16[1,64,8192]{2,1,0:T(8,128)(2,1)} %all-gather.5.cloned.1.call-done, bf16[1,8192,64]{1,2,0:T(8,128)(2,1)} %all-gather.3.cloned.1.call-done), kind=kOutput, calls=%fused_computation.2 | convolution fusion | flops 505297920 | bytes 9961472 | tf_op jit(solution)/shard_map/dot_general | solution.py:37
  137.6 4.2 %reshape.60 = bf16[8,30,8192]{2,1,0:T(8,128)(2,1)} reshape(bf16[240,8192]{1,0:T(8,128)(2,1)} %convolution_convert_fusion) | data formatting | bytes 7864320 | tf_op jit(solution)/shard_map/reshape | solution.py:39
  141.8 0.0 copy-start.2
  141.8 4.7 %all-to-all-start.1 = ((bf16[8,30,8192]{2,1,0:T(8,128)(2,1)}), bf16[8,30,8192]{2,1,0:T(8,128)(2,1)}, u32[]{:S(2)}, u32[]{:S(2)}) async-start(bf16[8,30,8192]{2,1,0:T(8,128)(2,1)} %reshape.60), calls=%async_computation.1 | async-start | bytes 8388608 | tf_op jit(solution)/shard_map/all_to_all | solution.py:38
  146.5 0.0 copy-done.2
  146.5 2.0 all_gather.15
  148.5 90.7 %all-to-all-done.1 = bf16[8,30,8192]{2,1,0:T(8,128)(2,1)} async-done(((bf16[8,30,8192]{2,1,0:T(8,128)(2,1)}), bf16[8,30,8192]{2,1,0:T(8,128)(2,1)}, u32[]{:S(2)}, u32[]{:S(2)}) %all-to-all-start.1) | async-done | bytes 3932192 | tf_op jit(solution)/shard_map/all_to_all | solution.py:38
  239.2 4.1 %reshape.61 = bf16[240,8192]{1,0:T(8,128)(2,1)} reshape(bf16[8,30,8192]{2,1,0:T(8,128)(2,1)} %all-to-all-done.1) | data formatting | bytes 7864320 | tf_op jit(solution)/shard_map/reshape | solution.py:41
  243.3 0.0 copy-start
  243.3 7.6 %gather_fusion = bf16[120,8192]{1,0:T(8,128)(2,1)} fusion(bf16[240,8192]{1,0:T(8,128)(2,1)} %reshape.61, s32[1024]{0:T(1024)S(1)} %pad_clamp_fusion), kind=kCustom, calls=%fused_computation | custom fusion | bytes 3932640 | tf_op jit(solution)/shard_map/gather | solution.py:41
  250.9 0.0 copy-done
  250.9 2.4 add_convert_fusion
  253.3 0.0 copy-start.1
  253.3 1.1 convolution_bitcast_fusion
  254.5 0.1 copy-done.1
  (5 shorter events, 0.0 us)
Async XLA Ops:
  23.7 100.8 %all-to-all-start = ((bf16[8,30,8192]{2,1,0:T(8,128)(2,1)}), bf16[8,30,8192]{2,1,0:T(8,128)(2,1)}, u32[]{:S(2)}, u32[]{:S(2)}) async-start(bf16[8,30,8192]{2,1,0:T(8,128)(2,1)} %reshape.58), calls=%async_computation | async-start | bytes 8388608 | tf_op jit(solution)/shard_map/all_to_all | solution.py:34
  30.9 97.8 %all-gather.3.cloned.1.call-start = ((), (), s32[]{:S(2)}) async-start(), calls=%async_computation.2 | async-start | bytes 1572864 | tf_op jit(solution)/shard_map/all_gather | solution.py:29
  31.6 97.0 %all-gather.5.cloned.1.call-start = ((), (), s32[]{:S(2)}) async-start(), calls=%async_computation.3 | async-start | bytes 1572864 | tf_op jit(solution)/shard_map/all_gather | solution.py:30
  141.8 4.7 %copy-start.2 = (bf16[4096]{0:T(1024)(128)(2,1)S(1)}, bf16[4096]{0:T(1024)(128)(2,1)}, u32[]{:S(2)}) copy-start(bf16[4096]{0:T(1024)(128)(2,1)} %param.13) | copy-start | bytes 24580
  141.8 97.4 %all-to-all-start.1 = ((bf16[8,30,8192]{2,1,0:T(8,128)(2,1)}), bf16[8,30,8192]{2,1,0:T(8,128)(2,1)}, u32[]{:S(2)}, u32[]{:S(2)}) async-start(bf16[8,30,8192]{2,1,0:T(8,128)(2,1)} %reshape.60), calls=%async_computation.1 | async-start | bytes 8388608 | tf_op jit(solution)/shard_map/all_to_all | solution.py:38
  243.3 7.6 %copy-start = (bf16[120,8192]{1,0:T(8,128)(2,1)S(1)}, bf16[120,8192]{1,0:T(8,128)(2,1)}, u32[]{:S(2)}) copy-start(bf16[120,8192]{1,0:T(8,128)(2,1)} %param.7) | copy-start | bytes 5898244
  253.3 1.3 copy-start.1
Sparse Core Ops, SparseCore 0:
  33.2 10.4 all-gather.2
  45.3 10.1 all-gather.4
where the time goes:
time: 262 us; the launch traced here: 261 us
  waiting for transfers between devices  184 us (70%)
  local copies, waits for them, and re-layouts  24.3 us (9%)
  between operations  14.1 us (5%)
  other arithmetic  12.6 us (5%)
  starting transfers between devices  11.9 us (5%)
  matrix products  10.1 us (4%)
  blocking collectives  4.15 us (2%)
    all_to_all x1, waiting for transfers between devices, per_device(): lax.all_to_all(outgoing, 'adapter', split_axis=0, concat_axis=0, tiled=True)  92.2 us
    all_to_all x1, waiting for transfers between devices, per_device(): lax.all_to_all(delta.reshape(received.shape), 'adapter', split_axis=0, co...  90.7 us
    dot_general x1, matrix products, per_device(): jnp.dot(codes, matrix_b, preferred_element_type=jnp.float32)  9 us
    gather x1, local copies, waits for them, and re-layouts, per_device(): delta = returned.reshape(-1, width)[target]  7.59 us
    all_to_all x1, starting transfers between devices, per_device(): lax.all_to_all(outgoing, 'adapter', split_axis=0, concat_axis=0, tiled=True)  7.12 us
    scatter x1, other arithmetic, per_device(): jnp.zeros((lanes * capacity, width), jnp.bfloat16).at[target].set(normed)  6.9 us
  transfers between devices with their start and end apart: 4, of which 2 were waited for; matrix products, arithmetic and copies ran while one was open for 2% of the time, Pallas kernels for 0%

commit v1 on v0

--- a/solution.py
+++ b/solution.py
@@ -1,10 +1,15 @@
 import jax
 import jax.numpy as jnp
 from jax import lax
+from jax.experimental import pallas as pl
+from jax.experimental.pallas import tpu as pltpu
 from jax.sharding import PartitionSpec as P
 
-
-def per_device(hidden, adapter_ids, owner_map, down_a, up_b, norm_gain, reward_head):
+GATHER_LIMIT = 12 << 20
+VMEM_LIMIT = 40 << 20
+
+
+def routed_rows(hidden, adapter_ids, owner_map, down_a, up_b, norm_gain, reward_head):
     gain, head = (
         lax.all_gather(norm_gain, "fsdp", axis=0, tiled=True),
         lax.all_gather(reward_head, "fsdp", axis=0, tiled=True),
@@ -15,11 +20,7 @@
     row_count, width = hidden.shape
     lanes = lax.axis_size("adapter")
     capacity = max(2, (2 * row_count + lanes - 1) // lanes)
-    table_size = owner_map.shape[0]
-    picked = (
-        adapter_ids[:, 0][:, None] == jnp.arange(table_size, dtype=jnp.int32)[None, :]
-    ).astype(jnp.int32)
-    owners = jnp.sum(picked * owner_map[None, :], axis=1)
+    owners = owners_of(adapter_ids, owner_map)
     marks = (owners[:, None] == jnp.arange(lanes, dtype=jnp.int32)[None, :]).astype(jnp.int32)
     ranks = jnp.sum(jnp.cumsum(marks, axis=0) * marks, axis=1) - 1
     target = owners * capacity + ranks
@@ -42,6 +43,225 @@
     adapted = (normed.astype(jnp.float32) + 2.0 * delta.astype(jnp.float32)).astype(jnp.bfloat16)
     scores = jnp.dot(adapted, head, preferred_element_type=jnp.float32)
     return (adapted, scores)
+
+
+def owners_of(adapter_ids, owner_map):
+    table_size = owner_map.shape[0]
+    picked = (
+        adapter_ids[:, 0][:, None] == jnp.arange(table_size, dtype=jnp.int32)[None, :]
+    ).astype(jnp.int32)
+    return jnp.sum(picked * owner_map[None, :], axis=1)
+
+
+def snake(count):
+    return list(range(0, count, 2)) + list(range(1, count, 2))[::-1]
+
+
+def ring_hops(count):
+    hops = []
+    for distance in range(1, count // 2 + 1):
+        hops.append((distance, 1))
+        if 2 * distance < count:
+            hops.append((distance, -1))
+    return hops
+
+
+def ring_gather(own, order):
+    count = len(order)
+    perms = {
+        way: [(order[i], order[(i + way) % count]) for i in range(count)] for way in (1, -1)
+    }
+    held = {1: own, -1: own}
+    arrived = [own]
+    for _, way in ring_hops(count):
+        held[way] = lax.ppermute(held[way], "adapter", perms[way])
+        arrived.append(held[way])
+    return arrived
+
+
+def norm_kernel(place, hidden, other, own_small, other_small, gain, own_out, other_out, send_out):
+    y = place[1]
+    half = other.shape[1]
+    quarter = half // 2
+    there = pl.multiple_of((1 - y) * quarter, quarter)
+    g = gain[...].astype(jnp.float32)
+    a = (hidden[...].astype(jnp.float32) * own_small[:, 0:1] * g).astype(jnp.bfloat16)
+    own_out[...] = a
+    b = (other[...].astype(jnp.float32) * other_small[:, 0:1] * g).astype(jnp.bfloat16)
+    other_out[...] = b
+    send_out[:, 0:quarter] = own_out[:, pl.ds(there, quarter)]
+    send_out[:, quarter:half] = other_out[:, pl.ds(there, quarter)]
+    lane = lax.broadcasted_iota(jnp.int32, (a.shape[0], 128), 1)
+    marks = jnp.where(lane == 0, own_small[:, 1:2], other_small[:, 1:2])
+    send_out[:, half:] = marks.astype(jnp.bfloat16)
+
+
+def codes_kernel(place, own, other, across, own_small, other_small, ids, *rest):
+    *downs, here_out, there_out = rest
+    quarter = downs[0].shape[1]
+    half = own.shape[1]
+    start = pl.multiple_of(place[1] * quarter, quarter)
+    wide = jnp.concatenate([d[...] for d in downs], axis=0)
+    names = ids[...]
+
+    def part(rows, slot):
+        got = lax.dot_general(
+            rows, wide, (((1,), (1,)), ((), ())), preferred_element_type=jnp.float32
+        )
+        got = jnp.where(slot == names, got, 0.0)
+        total = got[:, 0:128]
+        for i in range(128, got.shape[1], 128):
+            total = total + got[:, i : i + 128]
+        return total
+
+    slots = across[:, half:].astype(jnp.float32)
+    there_out[:, 0:128] = part(across[:, 0:quarter], slots[:, 0:1])
+    there_out[:, 128:256] = part(across[:, quarter:half], slots[:, 1:2])
+    here_out[:, 0:128] = part(own[:, pl.ds(start, quarter)], own_small[:, 1:2])
+    here_out[:, 128:256] = part(other[:, pl.ds(start, quarter)], other_small[:, 1:2])
+
+
+def delta_kernel(place, own, other, here, there, own_small, other_small, ids, head, *rest):
+    *ups, own_out, other_out, scores_out, own_codes, other_codes = rest
+    names = ids[...]
+
+    @pl.when(pl.program_id(0) == 0)
+    def _():
+        scores_out[...] = jnp.zeros_like(scores_out)
+        for total, small, out in (
+            (here[:, 0:128] + there[:, 128:256], own_small, own_codes),
+            (here[:, 128:256] + there[:, 0:128], other_small, other_codes),
+        ):
+            code = total + pltpu.roll(total, 64, 1)
+            wide = jnp.concatenate([code] * (names.shape[1] // 128), axis=1)
+            out[...] = jnp.where(small[:, 1:2] == names, wide, 0.0).astype(jnp.bfloat16)
+
+    wide = jnp.concatenate([u[...] for u in ups], axis=0)
+    weights = head[...].astype(jnp.float32)
+    lane = lax.broadcasted_iota(jnp.int32, scores_out.shape, 1)
+    for turn, (rows, codes, out) in enumerate(
+        ((own, own_codes, own_out), (other, other_codes, other_out))
+    ):
+        delta = jnp.dot(codes[...], wide, preferred_element_type=jnp.float32)
+        delta = delta.astype(jnp.bfloat16).astype(jnp.float32)
+        adapted = (rows[...].astype(jnp.float32) + 2.0 * delta).astype(jnp.bfloat16)
+        out[...] = adapted
+        part = jnp.sum(adapted.astype(jnp.float32) * weights, axis=1, keepdims=True)
+        scores_out[...] += jnp.where(lane == turn, part, 0.0)
+
+
+def gathered_matrices(hidden, adapter_ids, owner_map, down_a, up_b, norm_gain, reward_head):
+    rows, width = hidden.shape
+    count = lax.axis_size("adapter")
+    half = down_a.shape[1]
+    quarter = half // 2
+    rank = down_a.shape[2]
+    f = lax.axis_index("fsdp")
+    y = lax.axis_index("groups")
+    place = jnp.stack([f, y]).astype(jnp.int32)
+    order = snake(count)
+    swap = [(0, 1), (1, 0)]
+    params = pltpu.CompilerParams(vmem_limit_bytes=VMEM_LIMIT)
+
+    spot = [order.index(a) for a in range(count)]
+    sources = jnp.array(
+        [[a] + [order[(spot[a] - d * w) % count] for d, w in ring_hops(count)] for a in range(count)],
+        jnp.int32,
+    )[lax.axis_index("adapter")]
+    ids = jnp.repeat(sources, rank)[None, :].astype(jnp.float32)
+
+    down_own = lax.dynamic_slice_in_dim(down_a[0].T, y * quarter, quarter, 1)
+    other = lax.ppermute(
+        lax.dynamic_slice_in_dim(hidden, (1 - f) * half, half, 1), "fsdp", swap
+    )
+    downs = ring_gather(down_own, order)
+
+    values = hidden.astype(jnp.float32)
+    factor = lax.rsqrt(jnp.mean(values * values, axis=-1, keepdims=True) + 1e-05)
+    slot = owners_of(adapter_ids, owner_map)[:, None].astype(jnp.float32)
+    small = jnp.concatenate([factor, slot], axis=1)
+    other_small = lax.ppermute(small, "fsdp", swap)
+
+    whole = lambda shape: pl.BlockSpec(shape, lambda i, p: (0,) * len(shape))
+    bf = lambda *shape: jax.ShapeDtypeStruct(shape, jnp.bfloat16)
+    fl = lambda *shape: jax.ShapeDtypeStruct(shape, jnp.float32)
+    own_normed, other_normed, send = pl.pallas_call(
+        norm_kernel,
+        grid_spec=pltpu.PrefetchScalarGridSpec(
+            num_scalar_prefetch=1,
+            grid=(1,),
+            in_specs=[
+                pl.BlockSpec((rows, half), lambda i, p: (0, p[0])),
+                whole((rows, half)),
+                whole((rows, 2)),
+                whole((rows, 2)),
+                whole((1, half)),
+            ],
+            out_specs=[whole((rows, half)), whole((rows, half)), whole((rows, half + 128))],
+        ),
+        out_shape=[bf(rows, half), bf(rows, half), bf(rows, half + 128)],
+        compiler_params=params,
+        cost_estimate=pl.CostEstimate(flops=6 * rows * width, bytes_accessed=10 * rows * half, transcendentals=0),
+    )(place, hidden, other, small, other_small, norm_gain[None, :])
+    across = lax.ppermute(send, "groups", swap)
+
+    here, there = pl.pallas_call(
+        codes_kernel,
+        grid_spec=pltpu.PrefetchScalarGridSpec(
+            num_scalar_prefetch=1,
+            grid=(1,),
+            in_specs=[
+                whole((rows, half)),
+                whole((rows, half)),
+                whole((rows, half + 128)),
+                whole((rows, 2)),
+                whole((rows, 2)),
+                whole((1, count * rank)),
+            ]
+            + [whole((rank, quarter))] * count,
+            out_specs=[whole((rows, 256)), whole((rows, 256))],
+        ),
+        out_shape=[fl(rows, 256), fl(rows, 256)],
+        compiler_params=params,
+        cost_estimate=pl.CostEstimate(flops=8 * rows * quarter * count * rank, bytes_accessed=6 * rows * half + 2 * count * rank * quarter, transcendentals=0),
+    )(place, own_normed, other_normed, across, small, other_small, ids, *downs)
+    here = here + lax.ppermute(there, "groups", swap)
+    there = lax.ppermute(here, "fsdp", swap)
+
+    ups = ring_gather(up_b[0], order)
+    tile = 1024
+    column = lambda n: pl.BlockSpec((n, tile), lambda i, p: (0, i))
+    adapted, adapted_other, parts = pl.pallas_call(
+        delta_kernel,
+        grid_spec=pltpu.PrefetchScalarGridSpec(
+            num_scalar_prefetch=1,
+            grid=(half // tile,),
+            in_specs=[
+                column(rows),
+                column(rows),
+                whole((rows, 256)),
+                whole((rows, 256)),
+                whole((rows, 2)),
+                whole((rows, 2)),
+                whole((1, count * rank)),
+                column(1),
+            ]
+            + [column(rank)] * count,
+            out_specs=[
+                pl.BlockSpec((rows, tile), lambda i, p: (0, p[0] * (half // tile) + i)),
+                column(rows),
+                whole((rows, 128)),
+            ],
+            scratch_shapes=[pltpu.VMEM((rows, count * rank), jnp.bfloat16)] * 2,
+        ),
+        out_shape=[bf(rows, width), bf(rows, half), fl(rows, 128)],
+        compiler_params=params,
+        cost_estimate=pl.CostEstimate(flops=4 * rows * half * count * rank, bytes_accessed=8 * rows * half + 2 * count * rank * half, transcendentals=0),
+    )(place, own_normed, other_normed, here, there, small, other_small, ids, reward_head[None, :], *ups)
+    adapted_back = lax.ppermute(adapted_other, "fsdp", swap)
+    parts_back = lax.ppermute(parts[:, 1], "fsdp", swap)
+    adapted = lax.dynamic_update_slice_in_dim(adapted, adapted_back, (1 - f) * half, 1)
+    return (adapted, parts[:, 0] + parts_back)
 
 
 def solution(mesh):
@@ -54,6 +274,15 @@
         P("fsdp"),
         P("fsdp"),
     )
+
+    def per_device(*args):
+        down_a, up_b = args[3], args[4]
+        gathered = mesh.shape["adapter"] * 2 * (down_a.size + up_b.size)
+        square = mesh.shape["groups"] == 2 and mesh.shape["fsdp"] == 2
+        if square and down_a.shape[0] == 1 and down_a.shape[2] == 64 and gathered <= GATHER_LIMIT:
+            return gathered_matrices(*args)
+        return routed_rows(*args)
+
     return jax.shard_map(
         per_device,
         mesh=mesh,

time: 262 us -> 94.6 us (0.36)
  waiting for transfers between devices: 184 us -> 41.5 us
  between operations: 14.1 us -> 0.8 us
  Pallas kernels: 0 us -> 12.9 us
  other arithmetic: 12.6 us -> 1.87 us
  matrix products: 10.1 us -> 0 us
  starting transfers between devices: 11.9 us -> 20.4 us
  local copies, waits for them, and re-layouts: 24.3 us -> 16.5 us
  blocking collectives: 4.15 us -> 0 us
    all_to_all x2 -> x0, waiting for transfers between devices: 183 us -> none  [the longest x1 92.2 us: per_device(): lax.all_to_all(outgoing, 'adapter', split_axis=0, concat_axis=0, tiled=True)]
    ppermute x0 -> x21, waiting for transfers between devices: none -> 41.5 us  [the longest x14 34.8 us: ring_gather(): held[way] = lax.ppermute(held[way], 'adapter', perms[way])]
    ppermute x0 -> x21, starting transfers between devices: none -> 20.4 us  [the longest x14 16.4 us: ring_gather(): held[way] = lax.ppermute(held[way], 'adapter', perms[way])]
    reshape x4 -> x0, local copies, waits for them, and re-layouts: 16.6 us -> none  [the longest x1 4.15 us: per_device(): delta.reshape(received.shape)]
    pallas_call x0 -> x3, Pallas kernels: none -> 12.9 us  [the longest x1 5.63 us: gathered_matrices(): pl.pallas_call(delta_kernel, grid_spec=pltpu.PrefetchScalarGridSpec(num_s...]
    unnamed x6 -> x46, local copies, waits for them, and re-layouts: 0.13 us -> 12.8 us
    all_to_all x2 -> x0, starting transfers between devices: 11.8 us -> none  [the longest x1 7.12 us: per_device(): lax.all_to_all(outgoing, 'adapter', split_axis=0, concat_axis=0, tiled=True)]
    dot_general x2 -> x0, matrix products: 10.1 us -> none  [the longest x1 9 us: per_device(): jnp.dot(codes, matrix_b, preferred_element_type=jnp.float32)]
  transfers between devices with their start and end apart: 4 -> 21, of which waited for: 2 -> 9; matrix products, arithmetic and copies ran while one was open for 2% -> 5% of each run, Pallas kernels for 0% -> 8%
where the time goes in v1:
time: 94.6 us; the launch traced here: 94.1 us
  waiting for transfers between devices  41.5 us (44%)
  starting transfers between devices  20.4 us (22%)
  local copies, waits for them, and re-layouts  16.5 us (17%)
  Pallas kernels  12.9 us (14%)
  other arithmetic  1.87 us (2%)
    ppermute x14, waiting for transfers between devices, ring_gather(): held[way] = lax.ppermute(held[way], 'adapter', perms[way])  34.8 us
    ppermute x14, starting transfers between devices, ring_gather(): held[way] = lax.ppermute(held[way], 'adapter', perms[way])  16.4 us
    unnamed x46, local copies, waits for them, and re-layouts  12.8 us
    pallas_call x1, Pallas kernels, gathered_matrices(): pl.pallas_call(delta_kernel, grid_spec=pltpu.PrefetchScalarGridSpec(num_s...  5.63 us
    pallas_call x1, Pallas kernels, gathered_matrices(): pl.pallas_call(codes_kernel, grid_spec=pltpu.PrefetchScalarGridSpec(num_s...  4.4 us
    ppermute x1, waiting for transfers between devices, gathered_matrices(): here = here + lax.ppermute(there, 'groups', swap)  3.65 us
    pallas_call x1, Pallas kernels, gathered_matrices(): pl.pallas_call(norm_kernel, grid_spec=pltpu.PrefetchScalarGridSpec(num_sc...  2.9 us
    dynamic_slice x1, local copies, waits for them, and re-layouts, gathered_matrices(): lax.dynamic_slice_in_dim(hidden, (1 - f) * half, half, 1)  2.26 us
  transfers between devices with their start and end apart: 21, of which 9 were waited for; matrix products, arithmetic and copies ran while one was open for 5% of the time, Pallas kernels for 8%

profile of v1, /device:TPU:0, one launch (start us, length us, event | category | flops | bytes accessed | tf_op | source)
XLA Modules:
  0.0 94.1 jit_solution(3381310908238674175)
XLA Ops:
  0.7 3.1 %collective-permute-start.12 = (bf16[64,4096]{1,0:T(8,128)(2,1)}, bf16[64,4096]{1,0:T(8,128)(2,1)}, u32[]{:S(2)}, u32[]{:S(2)}) collective-permute-start(bf16[64,4096]{1,0:T(8,128)(2,1)} %bitcast.14), channel_id=1, source_target_pairs={{0,4},{4,8},{8,12},{12,14},{14,10},{10,6},{6,2},{2,0},{1,5},{5,9},... | collective-permute-start | bytes 1572872 | tf_op jit(solution)/shard_map/ppermute | solution.py:77
  3.7 2.3 %constant_dynamic-slice_fusion.1 = bf16[120,4096]{1,0:T(8,128)(2,1)} fusion(bf16[120,8192]{1,0:T(8,128)(2,1)} %hidden.1, s32[]{:T(128)S(6)} %select_n.10), kind=kLoop, calls=%fused_computation.9 | loop fusion | bytes 1966084 | tf_op jit(solution)/shard_map/dynamic_slice | solution.py:175
  7.3 8.6 %collective-permute-done.12.rest_1_ = bf16[64,4096]{1,0:T(8,128)(2,1)} collective-permute-done((bf16[64,4096]{1,0:T(8,128)(2,1)}, bf16[64,4096]{1,0:T(8,128)(2,1)}, u32[]{:S(2)}, u32[]{:S(2)}) %collective-permute-start.12) | collective-permute-done | bytes 524320 | tf_op jit(solution)/shard_map/ppermute | solution.py:77
  15.9 1.8 %collective-permute-start.14 = (bf16[64,4096]{1,0:T(8,128)(2,1)}, bf16[64,4096]{1,0:T(8,128)(2,1)S(1)}, u32[]{:S(2)}, u32[]{:S(2)}) collective-permute-start(bf16[64,4096]{1,0:T(8,128)(2,1)} %collective-permute-done.12.rest_1_), channel_id=1, source_target_pairs={{0,4},{4,8},{8,12},{12,14},{14,10},{10,6},{6,2},{2,0},{1,5},{5,9},... | collective-permute-start | bytes 1572872 | tf_op jit(solution)/shard_map/ppermute | solution.py:77
  17.7 1.6 %collective-permute-start.3 = (bf16[64,2048]{1,0:T(8,128)(2,1)S(1)}, bf16[64,2048]{1,0:T(8,128)(2,1)S(1)}, u32[]{:S(2)}, u32[]{:S(2)}) collective-permute-start(bf16[64,2048]{1,0:T(8,128)(2,1)S(1)} %dynamic-slice_bitcast_fusion.rest_0_), channel_id=1, source_target_pairs={{0,4},{4,8},{8,12},{12,14},{14,10},{10,6},{6,2},{2,0},{1,5},{5,9},... | collective-permute-start | bytes 786440 | tf_op jit(solution)/shard_map/ppermute | solution.py:77
  20.4 1.2 %copy-done.7 = bf16[120,4096]{1,0:T(8,128)(2,1)S(1)} copy-done((bf16[120,4096]{1,0:T(8,128)(2,1)S(1)}, bf16[120,4096]{1,0:T(8,128)(2,1)}, u32[]{:S(2)}) %copy-start.7) | copy-done | bytes 983064
  21.6 2.9 %shard_map.95 = (bf16[120,4096]{1,0:T(8,128)(2,1)S(1)}, bf16[120,4096]{1,0:T(8,128)(2,1)S(1)}, bf16[120,4224]{1,0:T(8,128)(2,1)}) custom-call(s32[2]{0:T(128)S(1)} %pad_add_fusion.place, bf16[120,8192]{1,0:T(8,128)(2,1)S(1)} %copy-done.1, bf16[120,4096]{1,0:T(8,128)(2,1)S(1)} %copy-done.7, f32[120,2]{1,0:T(8,128)S(1)} %copy.19.own_small, ...), custom_call_target="tpu_custom_call" | custom-call | flops 5898240 | bytes 4915200 | tf_op jit(solution)/shard_map/pallas_call | solution.py:188
  24.5 1.0 %copy-done.2 = bf16[120,4096]{1,0:T(8,128)(2,1)} copy-done((bf16[120,4096]{1,0:T(8,128)(2,1)}, bf16[120,4096]{1,0:T(8,128)(2,1)S(1)}, u32[]{:S(2)}) %copy-start.2) | copy-done | bytes 983064
  25.5 1.5 %collective-permute-start.2 = (bf16[120,4224]{1,0:T(8,128)(2,1)}, bf16[120,4224]{1,0:T(8,128)(2,1)S(1)}, u32[]{:S(2)}, u32[]{:S(2)}) collective-permute-start(bf16[120,4224]{1,0:T(8,128)(2,1)} %get-tuple-element.12), channel_id=1, source_target_pairs={{0,16},{16,0},{1,17},{17,1},{2,18},{18,2},{3,19},{19,3},{4,20},{20... | collective-permute-start | bytes 3041288 | tf_op jit(solution)/shard_map/ppermute | solution.py:206
  27.5 7.4 %collective-permute-done.3.rest_1_ = bf16[64,2048]{1,0:T(8,128)(2,1)S(1)} collective-permute-done((bf16[64,2048]{1,0:T(8,128)(2,1)S(1)}, bf16[64,2048]{1,0:T(8,128)(2,1)S(1)}, u32[]{:S(2)}, u32[]{:S(2)}) %collective-permute-start.3) | collective-permute-done | bytes 262176 | tf_op jit(solution)/shard_map/ppermute | solution.py:77
  34.8 1.5 %collective-permute-start.5 = (bf16[64,2048]{1,0:T(8,128)(2,1)S(1)}, bf16[64,2048]{1,0:T(8,128)(2,1)S(1)}, u32[]{:S(2)}, u32[]{:S(2)}) collective-permute-start(bf16[64,2048]{1,0:T(8,128)(2,1)S(1)} %collective-permute-done.3.rest_1_), channel_id=1, source_target_pairs={{0,4},{4,8},{8,12},{12,14},{14,10},{10,6},{6,2},{2,0},{1,5},{5,9},... | collective-permute-start | bytes 786440 | tf_op jit(solution)/shard_map/ppermute | solution.py:77
  37.6 1.5 %collective-permute-start.16 = (bf16[64,4096]{1,0:T(8,128)(2,1)S(1)}, bf16[64,4096]{1,0:T(8,128)(2,1)}, u32[]{:S(2)}, u32[]{:S(2)}) collective-permute-start(bf16[64,4096]{1,0:T(8,128)(2,1)S(1)} %collective-permute-done.14.rest_3_), channel_id=1, source_target_pairs={{0,4},{4,8},{8,12},{12,14},{14,10},{10,6},{6,2},{2,0},{1,5},{5,9},... | collective-permute-start | bytes 1572872 | tf_op jit(solution)/shard_map/ppermute | solution.py:77
  40.4 3.6 %collective-permute-done.5.rest_3_ = bf16[64,2048]{1,0:T(8,128)(2,1)S(1)} collective-permute-done((bf16[64,2048]{1,0:T(8,128)(2,1)S(1)}, bf16[64,2048]{1,0:T(8,128)(2,1)S(1)}, u32[]{:S(2)}, u32[]{:S(2)}) %collective-permute-start.5) | collective-permute-done | bytes 262176 | tf_op jit(solution)/shard_map/ppermute | solution.py:77
  44.1 1.5 %collective-permute-start.7 = (bf16[64,2048]{1,0:T(8,128)(2,1)S(1)}, bf16[64,2048]{1,0:T(8,128)(2,1)S(1)}, u32[]{:S(2)}, u32[]{:S(2)}) collective-permute-start(bf16[64,2048]{1,0:T(8,128)(2,1)S(1)} %collective-permute-done.5.rest_3_), channel_id=1, source_target_pairs={{0,4},{4,8},{8,12},{12,14},{14,10},{10,6},{6,2},{2,0},{1,5},{5,9},... | collective-permute-start | bytes 786440 | tf_op jit(solution)/shard_map/ppermute | solution.py:77
  46.3 8.6 %collective-permute-done.6.rest_4_ = bf16[64,2048]{1,0:T(8,128)(2,1)S(1)} collective-permute-done((bf16[64,2048]{1,0:T(8,128)(2,1)S(1)}, bf16[64,2048]{1,0:T(8,128)(2,1)S(1)}, u32[]{:S(2)}, u32[]{:S(2)}) %collective-permute-start.6) | collective-permute-done | bytes 262176 | tf_op jit(solution)/shard_map/ppermute | solution.py:77
  56.1 2.1 %collective-permute-done.7.rest_5_ = bf16[64,2048]{1,0:T(8,128)(2,1)S(1)} collective-permute-done((bf16[64,2048]{1,0:T(8,128)(2,1)S(1)}, bf16[64,2048]{1,0:T(8,128)(2,1)S(1)}, u32[]{:S(2)}, u32[]{:S(2)}) %collective-permute-start.7) | collective-permute-done | bytes 262176 | tf_op jit(solution)/shard_map/ppermute | solution.py:77
  58.3 1.3 %collective-permute-start.9 = (bf16[64,2048]{1,0:T(8,128)(2,1)S(1)}, bf16[64,2048]{1,0:T(8,128)(2,1)}, u32[]{:S(2)}, u32[]{:S(2)}) collective-permute-start(bf16[64,2048]{1,0:T(8,128)(2,1)S(1)} %collective-permute-done.7.rest_5_), channel_id=1, source_target_pairs={{0,4},{4,8},{8,12},{12,14},{14,10},{10,6},{6,2},{2,0},{1,5},{5,9},... | collective-permute-start | bytes 786440 | tf_op jit(solution)/shard_map/ppermute | solution.py:77
  61.0 1.3 %collective-permute-start.18 = (bf16[64,4096]{1,0:T(8,128)(2,1)}, bf16[64,4096]{1,0:T(8,128)(2,1)}, u32[]{:S(2)}, u32[]{:S(2)}) collective-permute-start(bf16[64,4096]{1,0:T(8,128)(2,1)} %collective-permute-done.16.rest_5_), channel_id=1, source_target_pairs={{0,4},{4,8},{8,12},{12,14},{14,10},{10,6},{6,2},{2,0},{1,5},{5,9},... | collective-permute-start | bytes 1572872 | tf_op jit(solution)/shard_map/ppermute | solution.py:77
  63.2 4.4 %collective-permute-done.9.rest_7_ = bf16[64,2048]{1,0:T(8,128)(2,1)} collective-permute-done((bf16[64,2048]{1,0:T(8,128)(2,1)S(1)}, bf16[64,2048]{1,0:T(8,128)(2,1)}, u32[]{:S(2)}, u32[]{:S(2)}) %collective-permute-start.9) | collective-permute-done | bytes 262176 | tf_op jit(solution)/shard_map/ppermute | solution.py:77
  67.6 1.2 %copy-done.3 = bf16[120,4096]{1,0:T(8,128)(2,1)S(1)} copy-done((bf16[120,4096]{1,0:T(8,128)(2,1)S(1)}, bf16[120,4096]{1,0:T(8,128)(2,1)}, u32[]{:S(2)}) %copy-start.3) | copy-done | bytes 983064
  68.8 0.9 %copy-done.5 = bf16[64,2048]{1,0:T(8,128)(2,1)S(1)} copy-done((bf16[64,2048]{1,0:T(8,128)(2,1)S(1)}, bf16[64,2048]{1,0:T(8,128)(2,1)}, u32[]{:S(2)}) %copy-start.5) | copy-done | bytes 262168
  69.8 0.9 %copy-done.12 = bf16[64,2048]{1,0:T(8,128)(2,1)S(1)} copy-done((bf16[64,2048]{1,0:T(8,128)(2,1)S(1)}, bf16[64,2048]{1,0:T(8,128)(2,1)}, u32[]{:S(2)}) %copy-start.12) | copy-done | bytes 262168
  70.7 0.9 %copy-done.14 = bf16[64,2048]{1,0:T(8,128)(2,1)S(1)} copy-done((bf16[64,2048]{1,0:T(8,128)(2,1)S(1)}, bf16[64,2048]{1,0:T(8,128)(2,1)}, u32[]{:S(2)}) %copy-start.14) | copy-done | bytes 262168
  71.7 0.9 %copy-done.16 = bf16[64,2048]{1,0:T(8,128)(2,1)S(1)} copy-done((bf16[64,2048]{1,0:T(8,128)(2,1)S(1)}, bf16[64,2048]{1,0:T(8,128)(2,1)}, u32[]{:S(2)}) %copy-start.16) | copy-done | bytes 262168
  72.6 0.9 %copy-done.18 = bf16[64,2048]{1,0:T(8,128)(2,1)S(1)} copy-done((bf16[64,2048]{1,0:T(8,128)(2,1)S(1)}, bf16[64,2048]{1,0:T(8,128)(2,1)}, u32[]{:S(2)}) %copy-start.18) | copy-done | bytes 262168
  73.6 4.4 %shard_map.96 = (f32[120,256]{1,0:T(8,128)S(1)}, f32[120,256]{1,0:T(8,128)S(1)}) custom-call(s32[2]{0:T(128)S(1)} %pad_add_fusion.place, bf16[120,4096]{1,0:T(8,128)(2,1)S(1)} %get-tuple-element.10.own, bf16[120,4096]{1,0:T(8,128)(2,1)S(1)} %copy-done.3, bf16[120,4224]{1,0:T(8,128)(2,1)S(1)} %collective-permute-done.2.across, f32[120,2]{1,0:T(8,128)S(1)} %copy.19.own_small, ...), custom_call_target="tpu_custom_call" | custom-call | flops 1006632960 | bytes 5046272 | tf_op jit(solution)/shard_map/pallas_call | solution.py:208
  78.0 1.3 %collective-permute-start.10 = (f32[120,256]{1,0:T(8,128)S(1)}, f32[120,256]{1,0:T(8,128)S(1)}, u32[]{:S(2)}, u32[]{:S(2)}) collective-permute-start(f32[120,256]{1,0:T(8,128)S(1)} %get-tuple-element.14), channel_id=1, source_target_pairs={{0,16},{16,0},{1,17},{17,1},{2,18},{18,2},{3,19},{19,3},{4,20},{20... | collective-permute-start | bytes 368648 | tf_op jit(solution)/shard_map/ppermute | solution.py:228
  79.3 3.6 %collective-permute-done.10 = f32[120,256]{1,0:T(8,128)S(1)} collective-permute-done((f32[120,256]{1,0:T(8,128)S(1)}, f32[120,256]{1,0:T(8,128)S(1)}, u32[]{:S(2)}, u32[]{:S(2)}) %collective-permute-start.10) | collective-permute-done | bytes 122912 | tf_op jit(solution)/shard_map/ppermute | solution.py:228
  83.1 1.3 %collective-permute-done.11.there = f32[120,256]{1,0:T(8,128)S(1)} collective-permute-done((f32[120,256]{1,0:T(8,128)S(1)}, f32[120,256]{1,0:T(8,128)S(1)}, u32[]{:S(2)}, u32[]{:S(2)}) %collective-permute-start.11) | collective-permute-done | bytes 122912 | tf_op jit(solution)/shard_map/ppermute | solution.py:229
  84.3 5.6 %shard_map.97 = (bf16[120,8192]{1,0:T(8,128)(2,1)}, bf16[120,4096]{1,0:T(8,128)(2,1)S(1)}, f32[120,128]{1,0:T(8,128)S(1)}) custom-call(s32[2]{0:T(128)S(1)} %pad_add_fusion.place, bf16[120,4096]{1,0:T(8,128)(2,1)S(1)} %get-tuple-element.10.own, bf16[120,4096]{1,0:T(8,128)(2,1)S(1)} %copy-done.3, f32[120,256]{1,0:T(8,128)S(1)} %add.36.here, ...), custom_call_target="tpu_custom_call" | custom-call | flops 1006632960 | bytes 8126464 | tf_op jit(solution)/shard_map/pallas_call | solution.py:234
  90.7 1.8 %collective-permute-done.20 = f32[120]{0:T(128)S(1)} collective-permute-done((f32[120]{0:T(128)S(1)}, f32[120]{0:T(128)S(1)}, u32[]{:S(2)}, u32[]{:S(2)}) %collective-permute-start.20) | collective-permute-done | bytes 512 | tf_op jit(solution)/shard_map/ppermute | solution.py:262
  93.1 1.0 %constant_dynamic-update-slice_fusion = bf16[120,8192]{1,0:T(8,128)(2,1)} fusion(bf16[120,8192]{1,0:T(8,128)(2,1)} %get-tuple-element.15, bf16[120,4096]{1,0:T(8,128)(2,1)S(1)} %collective-permute-done.19, s32[]{:T(128)S(6)} %select_n.10), kind=kLoop, calls=%fused_computation.7 | loop fusion | bytes 1966084 | tf_op jit(solution)/shard_map/dynamic_update_slice | solution.py:263
  (77 shorter events, 11.1 us)
Async XLA Ops:
  0.6 17.1 %copy-start = (bf16[1,4096,64]{1,2,0:T(8,128)(2,1)S(1)}, bf16[1,4096,64]{1,2,0:T(8,128)(2,1)}, u32[]{:S(2)}) copy-start(bf16[1,4096,64]{1,2,0:T(8,128)(2,1)} %param.11) | copy-start | bytes 1572868
  0.6 5.4 %copy-start.1 = (bf16[120,8192]{1,0:T(8,128)(2,1)S(1)}, bf16[120,8192]{1,0:T(8,128)(2,1)}, u32[]{:S(2)}) copy-start(bf16[120,8192]{1,0:T(8,128)(2,1)} %hidden.1) | copy-start | bytes 5898244
  0.7 15.2 %collective-permute-start.12 = (bf16[64,4096]{1,0:T(8,128)(2,1)}, bf16[64,4096]{1,0:T(8,128)(2,1)}, u32[]{:S(2)}, u32[]{:S(2)}) collective-permute-start(bf16[64,4096]{1,0:T(8,128)(2,1)} %bitcast.14), channel_id=1, source_target_pairs={{0,4},{4,8},{8,12},{12,14},{14,10},{10,6},{6,2},{2,0},{1,5},{5,9},... | collective-permute-start | bytes 1572872 | tf_op jit(solution)/shard_map/ppermute | solution.py:77
  3.7 33.3 %collective-permute-start.13 = (bf16[64,4096]{1,0:T(8,128)(2,1)}, bf16[64,4096]{1,0:T(8,128)(2,1)}, u32[]{:S(2)}, u32[]{:S(2)}) collective-permute-start(bf16[64,4096]{1,0:T(8,128)(2,1)} %bitcast.15), channel_id=1, source_target_pairs={{0,2},{4,0},{8,4},{12,8},{14,12},{10,14},{6,10},{2,6},{1,3},{5,1},... | collective-permute-start | bytes 1572872 | tf_op jit(solution)/shard_map/ppermute | solution.py:77
  3.7 2.7 %copy-start.21 = (s32[8]{0:T(128)S(1)}, s32[8]{0:T(128)}, u32[]{:S(2)}) copy-start(s32[8]{0:T(128)} %param.10) | copy-start | bytes 100
  3.7 2.7 %copy-start.22 = (s32[120,1]{0,1:T(1,128)S(1)}, s32[120,1]{0,1:T(1,128)}, u32[]{:S(2)}) copy-start(s32[120,1]{0,1:T(1,128)} %param.9) | copy-start | bytes 1444
  3.7 15.7 %copy-start.19 = (bf16[4096]{0:T(1024)(128)(2,1)S(1)}, bf16[4096]{0:T(1024)(128)(2,1)}, u32[]{:S(2)}) copy-start(bf16[4096]{0:T(1024)(128)(2,1)} %param.13) | copy-start | bytes 24580
  6.0 13.5 %collective-permute-start = (bf16[120,4096]{1,0:T(8,128)(2,1)}, bf16[120,4096]{1,0:T(8,128)(2,1)S(1)}, u32[]{:S(2)}, u32[]{:S(2)}) collective-permute-start(bf16[120,4096]{1,0:T(8,128)(2,1)} %constant_dynamic-slice_fusion.1), channel_id=1, source_target_pairs={{0,1},{1,0},{2,3},{3,2},{4,5},{5,4},{6,7},{7,6},{8,9},{9,8},{10,11... | collective-permute-start | bytes 2949128 | tf_op jit(solution)/shard_map/ppermute | solution.py:174
  6.7 12.8 %collective-permute-start.1 = (f32[120,2]{1,0:T(8,128)S(1)}, f32[120,2]{1,0:T(8,128)}, u32[]{:S(2)}, u32[]{:S(2)}) collective-permute-start(f32[120,2]{1,0:T(8,128)S(1)} %copy.19.own_small), channel_id=1, source_target_pairs={{0,1},{1,0},{2,3},{3,2},{4,5},{5,4},{6,7},{7,6},{8,9},{9,8},{10,11... | collective-permute-start | bytes 2888 | tf_op jit(solution)/shard_map/ppermute | solution.py:183
  15.9 21.7 %collective-permute-start.14 = (bf16[64,4096]{1,0:T(8,128)(2,1)}, bf16[64,4096]{1,0:T(8,128)(2,1)S(1)}, u32[]{:S(2)}, u32[]{:S(2)}) collective-permute-start(bf16[64,4096]{1,0:T(8,128)(2,1)} %collective-permute-done.12.rest_1_), channel_id=1, source_target_pairs={{0,4},{4,8},{8,12},{12,14},{14,10},{10,6},{6,2},{2,0},{1,5},{5,9},... | collective-permute-start | bytes 1572872 | tf_op jit(solution)/shard_map/ppermute | solution.py:77
  17.7 9.3 %copy-start.4 = (bf16[64,2048]{1,0:T(8,128)(2,1)}, bf16[64,2048]{1,0:T(8,128)(2,1)S(1)}, u32[]{:S(2)}) copy-start(bf16[64,2048]{1,0:T(8,128)(2,1)S(1)} %dynamic-slice_bitcast_fusion.rest_0_) | copy-start | bytes 786436
  17.7 17.1 %collective-permute-start.3 = (bf16[64,2048]{1,0:T(8,128)(2,1)S(1)}, bf16[64,2048]{1,0:T(8,128)(2,1)S(1)}, u32[]{:S(2)}, u32[]{:S(2)}) collective-permute-start(bf16[64,2048]{1,0:T(8,128)(2,1)S(1)} %dynamic-slice_bitcast_fusion.rest_0_), channel_id=1, source_target_pairs={{0,4},{4,8},{8,12},{12,14},{14,10},{10,6},{6,2},{2,0},{1,5},{5,9},... | collective-permute-start | bytes 786440 | tf_op jit(solution)/shard_map/ppermute | solution.py:77
  20.4 1.2 %copy-start.7 = (bf16[120,4096]{1,0:T(8,128)(2,1)S(1)}, bf16[120,4096]{1,0:T(8,128)(2,1)}, u32[]{:S(2)}) copy-start(bf16[120,4096]{1,0:T(8,128)(2,1)} %copy-done.6) | copy-start | bytes 2949124
  25.5 42.1 %collective-permute-start.2 = (bf16[120,4224]{1,0:T(8,128)(2,1)}, bf16[120,4224]{1,0:T(8,128)(2,1)S(1)}, u32[]{:S(2)}, u32[]{:S(2)}) collective-permute-start(bf16[120,4224]{1,0:T(8,128)(2,1)} %get-tuple-element.12), channel_id=1, source_target_pairs={{0,16},{16,0},{1,17},{17,1},{2,18},{18,2},{3,19},{19,3},{4,20},{20... | collective-permute-start | bytes 3041288 | tf_op jit(solution)/shard_map/ppermute | solution.py:206
  27.0 12.9 %collective-permute-start.4 = (bf16[64,2048]{1,0:T(8,128)(2,1)S(1)}, bf16[64,2048]{1,0:T(8,128)(2,1)S(1)}, u32[]{:S(2)}, u32[]{:S(2)}) collective-permute-start(bf16[64,2048]{1,0:T(8,128)(2,1)S(1)} %dynamic-slice_bitcast_fusion.rest_0_), channel_id=1, source_target_pairs={{0,2},{4,0},{8,4},{12,8},{14,12},{10,14},{6,10},{2,6},{1,3},{5,1},... | collective-permute-start | bytes 786440 | tf_op jit(solution)/shard_map/ppermute | solution.py:77
  34.8 9.2 %collective-permute-start.5 = (bf16[64,2048]{1,0:T(8,128)(2,1)S(1)}, bf16[64,2048]{1,0:T(8,128)(2,1)S(1)}, u32[]{:S(2)}, u32[]{:S(2)}) collective-permute-start(bf16[64,2048]{1,0:T(8,128)(2,1)S(1)} %collective-permute-done.3.rest_1_), channel_id=1, source_target_pairs={{0,4},{4,8},{8,12},{12,14},{14,10},{10,6},{6,2},{2,0},{1,5},{5,9},... | collective-permute-start | bytes 786440 | tf_op jit(solution)/shard_map/ppermute | solution.py:77
  37.1 23.2 %collective-permute-start.15 = (bf16[64,4096]{1,0:T(8,128)(2,1)}, bf16[64,4096]{1,0:T(8,128)(2,1)}, u32[]{:S(2)}, u32[]{:S(2)}) collective-permute-start(bf16[64,4096]{1,0:T(8,128)(2,1)} %collective-permute-done.13.rest_2_), channel_id=1, source_target_pairs={{0,2},{4,0},{8,4},{12,8},{14,12},{10,14},{6,10},{2,6},{1,3},{5,1},... | collective-permute-start | bytes 1572872 | tf_op jit(solution)/shard_map/ppermute | solution.py:77
  37.6 23.4 %collective-permute-start.16 = (bf16[64,4096]{1,0:T(8,128)(2,1)S(1)}, bf16[64,4096]{1,0:T(8,128)(2,1)}, u32[]{:S(2)}, u32[]{:S(2)}) collective-permute-start(bf16[64,4096]{1,0:T(8,128)(2,1)S(1)} %collective-permute-done.14.rest_3_), channel_id=1, source_target_pairs={{0,4},{4,8},{8,12},{12,14},{14,10},{10,6},{6,2},{2,0},{1,5},{5,9},... | collective-permute-start | bytes 1572872 | tf_op jit(solution)/shard_map/ppermute | solution.py:77
  39.9 15.0 %collective-permute-start.6 = (bf16[64,2048]{1,0:T(8,128)(2,1)S(1)}, bf16[64,2048]{1,0:T(8,128)(2,1)S(1)}, u32[]{:S(2)}, u32[]{:S(2)}) collective-permute-start(bf16[64,2048]{1,0:T(8,128)(2,1)S(1)} %collective-permute-done.4.rest_2_), channel_id=1, source_target_pairs={{0,2},{4,0},{8,4},{12,8},{14,12},{10,14},{6,10},{2,6},{1,3},{5,1},... | collective-permute-start | bytes 786440 | tf_op jit(solution)/shard_map/ppermute | solution.py:77
  44.1 14.2 %collective-permute-start.7 = (bf16[64,2048]{1,0:T(8,128)(2,1)S(1)}, bf16[64,2048]{1,0:T(8,128)(2,1)S(1)}, u32[]{:S(2)}, u32[]{:S(2)}) collective-permute-start(bf16[64,2048]{1,0:T(8,128)(2,1)S(1)} %collective-permute-done.5.rest_3_), channel_id=1, source_target_pairs={{0,4},{4,8},{8,12},{12,14},{14,10},{10,6},{6,2},{2,0},{1,5},{5,9},... | collective-permute-start | bytes 786440 | tf_op jit(solution)/shard_map/ppermute | solution.py:77
  54.9 8.3 %collective-permute-start.8 = (bf16[64,2048]{1,0:T(8,128)(2,1)S(1)}, bf16[64,2048]{1,0:T(8,128)(2,1)}, u32[]{:S(2)}, u32[]{:S(2)}) collective-permute-start(bf16[64,2048]{1,0:T(8,128)(2,1)S(1)} %collective-permute-done.6.rest_4_), channel_id=1, source_target_pairs={{0,2},{4,0},{8,4},{12,8},{14,12},{10,14},{6,10},{2,6},{1,3},{5,1},... | collective-permute-start | bytes 786440 | tf_op jit(solution)/shard_map/ppermute | solution.py:77
  58.3 9.3 %collective-permute-start.9 = (bf16[64,2048]{1,0:T(8,128)(2,1)S(1)}, bf16[64,2048]{1,0:T(8,128)(2,1)}, u32[]{:S(2)}, u32[]{:S(2)}) collective-permute-start(bf16[64,2048]{1,0:T(8,128)(2,1)S(1)} %collective-permute-done.7.rest_5_), channel_id=1, source_target_pairs={{0,4},{4,8},{8,12},{12,14},{14,10},{10,6},{6,2},{2,0},{1,5},{5,9},... | collective-permute-start | bytes 786440 | tf_op jit(solution)/shard_map/ppermute | solution.py:77
  60.3 22.8 %collective-permute-start.17 = (bf16[64,4096]{1,0:T(8,128)(2,1)}, bf16[64,4096]{1,0:T(8,128)(2,1)}, u32[]{:S(2)}, u32[]{:S(2)}) collective-permute-start(bf16[64,4096]{1,0:T(8,128)(2,1)} %collective-permute-done.15.rest_4_), channel_id=1, source_target_pairs={{0,2},{4,0},{8,4},{12,8},{14,12},{10,14},{6,10},{2,6},{1,3},{5,1},... | collective-permute-start | bytes 1572872 | tf_op jit(solution)/shard_map/ppermute | solution.py:77
  61.0 22.0 %collective-permute-start.18 = (bf16[64,4096]{1,0:T(8,128)(2,1)}, bf16[64,4096]{1,0:T(8,128)(2,1)}, u32[]{:S(2)}, u32[]{:S(2)}) collective-permute-start(bf16[64,4096]{1,0:T(8,128)(2,1)} %collective-permute-done.16.rest_5_), channel_id=1, source_target_pairs={{0,4},{4,8},{8,12},{12,14},{14,10},{10,6},{6,2},{2,0},{1,5},{5,9},... | collective-permute-start | bytes 1572872 | tf_op jit(solution)/shard_map/ppermute | solution.py:77
  67.6 1.2 %copy-start.3 = (bf16[120,4096]{1,0:T(8,128)(2,1)S(1)}, bf16[120,4096]{1,0:T(8,128)(2,1)}, u32[]{:S(2)}) copy-start(bf16[120,4096]{1,0:T(8,128)(2,1)} %copy-done.2) | copy-start | bytes 2949124
  73.6 9.5 %copy-start.20 = (bf16[4096]{0:T(1024)(128)(2,1)S(1)}, bf16[4096]{0:T(1024)(128)(2,1)}, u32[]{:S(2)}) copy-start(bf16[4096]{0:T(1024)(128)(2,1)} %param.14) | copy-start | bytes 24580
  73.6 10.8 %copy-start.8 = (bf16[1,64,4096]{2,1,0:T(8,128)(2,1)S(1)}, bf16[1,64,4096]{2,1,0:T(8,128)(2,1)}, u32[]{:S(2)}) copy-start(bf16[1,64,4096]{2,1,0:T(8,128)(2,1)} %param.12) | copy-start | bytes 1572868
  73.6 10.8 %copy-start.10 = (bf16[64,4096]{1,0:T(8,128)(2,1)S(1)}, bf16[64,4096]{1,0:T(8,128)(2,1)}, u32[]{:S(2)}) copy-start(bf16[64,4096]{1,0:T(8,128)(2,1)} %copy-done.9) | copy-start | bytes 1572868
  78.0 4.9 %collective-permute-start.10 = (f32[120,256]{1,0:T(8,128)S(1)}, f32[120,256]{1,0:T(8,128)S(1)}, u32[]{:S(2)}, u32[]{:S(2)}) collective-permute-start(f32[120,256]{1,0:T(8,128)S(1)} %get-tuple-element.14), channel_id=1, source_target_pairs={{0,16},{16,0},{1,17},{17,1},{2,18},{18,2},{3,19},{19,3},{4,20},{20... | collective-permute-start | bytes 368648 | tf_op jit(solution)/shard_map/ppermute | solution.py:228
  82.9 1.4 %collective-permute-start.11 = (f32[120,256]{1,0:T(8,128)S(1)}, f32[120,256]{1,0:T(8,128)S(1)}, u32[]{:S(2)}, u32[]{:S(2)}) collective-permute-start(f32[120,256]{1,0:T(8,128)S(1)} %add.36.here), channel_id=1, source_target_pairs={{0,1},{1,0},{2,3},{3,2},{4,5},{5,4},{6,7},{7,6},{8,9},{9,8},{10,11... | collective-permute-start | bytes 368648 | tf_op jit(solution)/shard_map/ppermute | solution.py:229
  90.0 3.1 %collective-permute-start.19 = (bf16[120,4096]{1,0:T(8,128)(2,1)S(1)}, bf16[120,4096]{1,0:T(8,128)(2,1)S(1)}, u32[]{:S(2)}, u32[]{:S(2)}) collective-permute-start(bf16[120,4096]{1,0:T(8,128)(2,1)S(1)} %get-tuple-element.16), channel_id=1, source_target_pairs={{0,1},{1,0},{2,3},{3,2},{4,5},{5,4},{6,7},{7,6},{8,9},{9,8},{10,11... | collective-permute-start | bytes 2949128 | tf_op jit(solution)/shard_map/ppermute | solution.py:261
  90.3 2.2 %collective-permute-start.20 = (f32[120]{0:T(128)S(1)}, f32[120]{0:T(128)S(1)}, u32[]{:S(2)}, u32[]{:S(2)}) collective-permute-start(f32[120]{0:T(128)S(1)} %get-tuple-element.18), channel_id=1, source_target_pairs={{0,1},{1,0},{2,3},{3,2},{4,5},{5,4},{6,7},{7,6},{8,9},{9,8},{10,11... | collective-permute-start | bytes 1448 | tf_op jit(solution)/shard_map/ppermute | solution.py:262
  (12 other events, 10.3 us)

commit v2 on v0

--- a/solution.py
+++ b/solution.py
@@ -1,10 +1,15 @@
 import jax
 import jax.numpy as jnp
 from jax import lax
+from jax.experimental import pallas as pl
+from jax.experimental.pallas import tpu as pltpu
 from jax.sharding import PartitionSpec as P
 
-
-def per_device(hidden, adapter_ids, owner_map, down_a, up_b, norm_gain, reward_head):
+GATHER_LIMIT = 12 << 20
+VMEM_LIMIT = 60 << 20
+
+
+def routed_rows(hidden, adapter_ids, owner_map, down_a, up_b, norm_gain, reward_head):
     gain, head = (
         lax.all_gather(norm_gain, "fsdp", axis=0, tiled=True),
         lax.all_gather(reward_head, "fsdp", axis=0, tiled=True),
@@ -15,11 +20,7 @@
     row_count, width = hidden.shape
     lanes = lax.axis_size("adapter")
     capacity = max(2, (2 * row_count + lanes - 1) // lanes)
-    table_size = owner_map.shape[0]
-    picked = (
-        adapter_ids[:, 0][:, None] == jnp.arange(table_size, dtype=jnp.int32)[None, :]
-    ).astype(jnp.int32)
-    owners = jnp.sum(picked * owner_map[None, :], axis=1)
+    owners = owners_of(adapter_ids, owner_map)
     marks = (owners[:, None] == jnp.arange(lanes, dtype=jnp.int32)[None, :]).astype(jnp.int32)
     ranks = jnp.sum(jnp.cumsum(marks, axis=0) * marks, axis=1) - 1
     target = owners * capacity + ranks
@@ -42,6 +43,271 @@
     adapted = (normed.astype(jnp.float32) + 2.0 * delta.astype(jnp.float32)).astype(jnp.bfloat16)
     scores = jnp.dot(adapted, head, preferred_element_type=jnp.float32)
     return (adapted, scores)
+
+
+def owners_of(adapter_ids, owner_map):
+    table_size = owner_map.shape[0]
+    picked = (
+        adapter_ids[:, 0][:, None] == jnp.arange(table_size, dtype=jnp.int32)[None, :]
+    ).astype(jnp.int32)
+    return jnp.sum(picked * owner_map[None, :], axis=1)
+
+
+def snake(count):
+    return list(range(0, count, 2)) + list(range(1, count, 2))[::-1]
+
+
+def ring_hops(count):
+    hops = []
+    for distance in range(1, count // 2 + 1):
+        hops.append((distance, 1))
+        if 2 * distance < count:
+            hops.append((distance, -1))
+    return hops
+
+
+def slots_of(lengths, first):
+    left, last, order = list(lengths), [-2] * len(lengths), []
+    while any(left):
+        ready = [c for c in first if left[c] and last[c] <= len(order) - 2]
+        ready = ready or [c for c in first if left[c]]
+        chain = ready[0]
+        last[chain] = len(order)
+        order.append((chain, lengths[chain] - left[chain] + 1))
+        left[chain] -= 1
+    return order
+
+
+def after(array, *others):
+    return lax.optimization_barrier((array, *others))[0]
+
+
+def padded(x, rows):
+    return jnp.concatenate([x, jnp.zeros((rows - x.shape[0], x.shape[1]), x.dtype)], axis=0)
+
+
+def norm_kernel(place, hidden, other, own_small, other_small, gain, out):
+    rows, quarter = hidden.shape
+    full = own_small.shape[0]
+    g = gain[...].astype(jnp.float32)
+    for turn, (raw, small) in enumerate(((hidden, own_small), (other, other_small))):
+        normed = raw[...].astype(jnp.float32) * small[0:rows, 0:1] * g
+        spot = turn * full
+        out[spot : spot + full, 0:quarter] = padded(normed, full).astype(jnp.bfloat16)
+        out[spot : spot + full, quarter:] = jnp.broadcast_to(small[:, 1:2], (full, 128)).astype(jnp.bfloat16)
+
+
+def codes_kernel(here, across, ids, *rest):
+    *downs, here_out, there_out = rest
+    quarter = downs[0].shape[1]
+    wide = jnp.concatenate([d[...] for d in downs], axis=0)
+    names = ids[...]
+    rows = jnp.concatenate([here[:, 0:quarter], across[:, 0:quarter]], axis=0)
+    slot = jnp.concatenate([here[:, quarter:], across[:, quarter:]], axis=0).astype(jnp.float32)
+    got = lax.dot_general(rows, wide, (((1,), (1,)), ((), ())), preferred_element_type=jnp.float32)
+    total = 0.0
+    for i in range(0, got.shape[1], 128):
+        total = total + jnp.where(slot == names[:, i : i + 128], got[:, i : i + 128], 0.0)
+    here_out[...] = total[0 : here.shape[0]]
+    there_out[...] = total[here.shape[0] :]
+
+
+def delta_kernel(place, mine, theirs, here, crossed, beside, beyond, own_small, other_small, ids, head, *rest):
+    *ups, own_out, other_out, own_scores, other_scores, codes, sums = rest
+    names = ids[...]
+    full = own_small.shape[0]
+    rows = own_out.shape[0]
+
+    @pl.when(pl.program_id(0) == 0)
+    def _():
+        sums[...] = jnp.zeros_like(sums)
+        for part, swapped, small in ((0, full, own_small), (full, 0, other_small)):
+            total = here[part : part + full] + crossed[part : part + full]
+            total += beside[swapped : swapped + full] + beyond[swapped : swapped + full]
+            code = total + pltpu.roll(total, 64, 1)
+            turned = jnp.where(place[1] == 1, pltpu.roll(code, 32, 1), code)
+            lane = lax.broadcasted_iota(jnp.int32, code.shape, 1)
+            first = jnp.where(lane < 64, code, turned)
+            wide = jnp.concatenate([first] + [turned] * (names.shape[1] // 128 - 1), axis=1)
+            wide = jnp.where(small[:, 1:2] == names, wide, 0.0)
+            codes[part : part + full] = wide.astype(jnp.bfloat16)
+
+    wide = jnp.concatenate([u[...] for u in ups], axis=0)
+    weights = head[...].astype(jnp.float32)
+    lane = lax.broadcasted_iota(jnp.int32, (full, 128), 1)
+    deltas = jnp.dot(codes[...], wide, preferred_element_type=jnp.float32)
+    is_mine = 2 * pl.program_id(0) // pl.num_programs(0) == place[1]
+    for turn, out in enumerate((own_out, other_out)):
+        span = slice(turn * full, (turn + 1) * full)
+        normed = jnp.where(is_mine, mine[span].astype(jnp.float32), theirs[span].astype(jnp.float32))
+        delta = deltas[span].astype(jnp.bfloat16).astype(jnp.float32)
+        adapted = normed + 2.0 * delta
+        adapted = adapted.astype(jnp.bfloat16).astype(jnp.float32)
+        out[...] = adapted[0:rows].astype(jnp.bfloat16)
+        part = jnp.sum(adapted * weights, axis=1, keepdims=True)
+        sums[...] += jnp.where(lane == turn, part, 0.0)
+
+    @pl.when(pl.program_id(0) == pl.num_programs(0) - 1)
+    def _():
+        turned = sums[...].T
+        own_scores[...] = turned[0:1]
+        other_scores[...] = turned[1:2]
+
+
+def gathered_matrices(hidden, adapter_ids, owner_map, down_a, up_b, norm_gain, reward_head):
+    rows, width = hidden.shape
+    full = -(-rows // 128) * 128
+    count = lax.axis_size("adapter")
+    half = down_a.shape[1]
+    quarter = half // 2
+    rank = down_a.shape[2]
+    f = lax.axis_index("fsdp")
+    y = lax.axis_index("groups")
+    place = jnp.stack([f, y]).astype(jnp.int32)
+    order = snake(count)
+    hops = ring_hops(count)
+    swap = [(0, 1), (1, 0)]
+    params = pltpu.CompilerParams(vmem_limit_bytes=VMEM_LIMIT)
+
+    spot = [order.index(a) for a in range(count)]
+    sources = jnp.array(
+        [[a] + [order[(spot[a] - d * w) % count] for d, w in hops] for a in range(count)],
+        jnp.int32,
+    )[lax.axis_index("adapter")]
+    ids = jnp.repeat(sources, rank)[None, :].astype(jnp.float32)
+    gain, head = norm_gain[None, :], reward_head[None, :]
+
+    cost = pl.CostEstimate(flops=1, bytes_accessed=1, transcendentals=0)
+    whole = lambda shape: pl.BlockSpec(shape, lambda i, p: (0,) * len(shape))
+    bf = lambda *shape: jax.ShapeDtypeStruct(shape, jnp.bfloat16)
+    fl = lambda *shape: jax.ShapeDtypeStruct(shape, jnp.float32)
+    tile = 1024
+    each = quarter // tile
+    column = lambda n: pl.BlockSpec((n, tile), lambda i, p: (0, i))
+    half_column = pl.BlockSpec((rows, tile), lambda i, p: (0, p[0] * (half // tile) + i))
+
+    perms = {
+        way: [(order[i], order[(i + way) % count]) for i in range(count)] for way in (1, -1)
+    }
+    down_own = lax.dynamic_slice_in_dim(down_a[0].T, y * quarter, quarter, 1)
+    far = count // 2
+    near = far // 2
+    lengths = {1: (far, count - 1 - far, near), -1: (count - 1 - far, far, near)}
+    slots = {way: slots_of(lengths[way], (1, 0, 2)) for way in (1, -1)}
+    held = {}
+    for way in (1, -1):
+        held[0, 0, way] = down_own
+        for c, side in ((1, y), (2, 1 - y)):
+            held[c, 0, way] = lax.dynamic_slice_in_dim(up_b[0], side * (rank // 2), rank // 2, 0)
+    arrived = []
+
+    def send_slot(k, *gates):
+        now = []
+        for way in (1, -1):
+            if k >= len(slots[way]):
+                continue
+            chain, distance = slots[way][k]
+            piece = held[chain, distance - 1, way]
+            wait = list(gates) + (arrived[k - 2] if k >= 2 else [])
+            if wait:
+                piece = after(piece, *wait)
+            held[chain, distance, way] = lax.ppermute(piece, "adapter", perms[way])
+            now.append(held[chain, distance, way])
+        arrived.append(now)
+
+    send_slot(0)
+    other = lax.ppermute(hidden, "fsdp", swap)
+    values = hidden.astype(jnp.float32)
+    factor = lax.rsqrt(jnp.mean(values * values, axis=-1, keepdims=True) + 1e-05)
+    slot = owners_of(adapter_ids, owner_map)[:, None].astype(jnp.float32)
+    small = padded(jnp.concatenate([factor, slot], axis=1), full)
+    other_small = lax.ppermute(small, "fsdp", swap)
+    send_slot(1)
+    send_slot(2)
+
+    def normed(gain, side):
+        piece = pl.BlockSpec((rows, quarter), lambda i, p: (0, 2 * p[0] + side(p[1])))
+        return pl.pallas_call(
+            norm_kernel,
+            grid_spec=pltpu.PrefetchScalarGridSpec(
+                num_scalar_prefetch=1,
+                grid=(1,),
+                in_specs=[
+                    piece,
+                    piece,
+                    whole((full, 2)),
+                    whole((full, 2)),
+                    pl.BlockSpec((1, quarter), lambda i, p: (0, side(p[1]))),
+                ],
+                out_specs=whole((2 * full, quarter + 128)),
+            ),
+            out_shape=bf(2 * full, quarter + 128),
+            compiler_params=params,
+            cost_estimate=cost,
+        )(place, hidden, other, small, other_small, gain)
+
+    theirs = normed(gain, lambda y: 1 - y)
+    across = lax.ppermute(after(theirs, *arrived[1]), "groups", swap)
+    gain, head, ids, *_ = lax.optimization_barrier((gain, head, ids, theirs, *arrived[2]))
+    mine = normed(gain, lambda y: y)
+
+    last_down = max(k for way in (1, -1) for k, (c, _) in enumerate(slots[way]) if c == 0)
+    for k in range(3, last_down + 3):
+        send_slot(k, *([mine] if k == 5 else []))
+    across_far = {
+        (d, w): lax.ppermute(held[1, d, w if d < far else -1], "groups", swap)
+        for d, w in hops
+        if near < d < far
+    }
+    here, there = pl.pallas_call(
+        codes_kernel,
+        out_shape=[fl(2 * full, 128), fl(2 * full, 128)],
+        compiler_params=params,
+        cost_estimate=cost,
+    )(mine, across, ids, down_own, *[held[0, d, w] for d, w in hops])
+    crossed = lax.ppermute(after(there, *across_far.values()), "groups", swap)
+    for k in range(last_down + 3, max(len(slots[1]), len(slots[-1]))):
+        send_slot(k, there)
+    across_far[far, 1] = lax.ppermute(after(held[1, far, -1], there), "groups", swap)
+    beside = lax.ppermute(here, "fsdp", swap)
+    beyond = lax.ppermute(crossed, "fsdp", swap)
+
+    ups = []
+    for distance, way in hops:
+        first = held[1, distance, way if distance < far else -1]
+        ups += [first, held[2, distance, way] if distance <= near else across_far[distance, way]]
+    adapted, adapted_other, own_part, other_part = pl.pallas_call(
+        delta_kernel,
+        grid_spec=pltpu.PrefetchScalarGridSpec(
+            num_scalar_prefetch=1,
+            grid=(half // tile,),
+            in_specs=[
+                pl.BlockSpec((2 * full, tile), lambda i, p: (0, jnp.clip(i - p[1] * each, 0, each - 1))),
+                pl.BlockSpec((2 * full, tile), lambda i, p: (0, jnp.clip(i - (1 - p[1]) * each, 0, each - 1))),
+            ]
+            + [whole((2 * full, 128))] * 4
+            + [
+                whole((full, 2)),
+                whole((full, 2)),
+                whole((1, count * rank)),
+                column(1),
+                column(rank),
+            ]
+            + [column(rank // 2)] * len(ups),
+            out_specs=[half_column, column(rows), whole((1, full)), whole((1, full))],
+            scratch_shapes=[
+                pltpu.VMEM((2 * full, count * rank), jnp.bfloat16),
+                pltpu.VMEM((full, 128), jnp.float32),
+            ],
+        ),
+        out_shape=[bf(rows, width), bf(rows, half), fl(1, full), fl(1, full)],
+        compiler_params=params,
+        cost_estimate=cost,
+    )(place, mine, theirs, here, crossed, beside, beyond, small, other_small, ids, head, up_b[0], *ups)
+    adapted_back = lax.ppermute(adapted_other, "fsdp", swap)
+    part_back = lax.ppermute(other_part.reshape(-1), "fsdp", swap)
+    adapted = lax.dynamic_update_slice_in_dim(adapted, adapted_back, (1 - f) * half, 1)
+    return (adapted, (own_part.reshape(-1) + part_back)[:rows])
 
 
 def solution(mesh):
@@ -54,6 +320,15 @@
         P("fsdp"),
         P("fsdp"),
     )
+
+    def per_device(*args):
+        down_a, up_b = args[3], args[4]
+        gathered = mesh.shape["adapter"] * 2 * (down_a.size + up_b.size)
+        square = mesh.shape["groups"] == 2 and mesh.shape["fsdp"] == 2
+        if square and down_a.shape[2] == 64 and gathered <= GATHER_LIMIT:
+            return gathered_matrices(*args)
+        return routed_rows(*args)
+
     return jax.shard_map(
         per_device,
         mesh=mesh,

time: 262 us -> 84.6 us (0.32)
  waiting for transfers between devices: 184 us -> 25.7 us
  Pallas kernels: 0 us -> 17.9 us
  local copies, waits for them, and re-layouts: 24.3 us -> 7.63 us
  starting transfers between devices: 11.9 us -> 26.9 us
  between operations: 14.1 us -> 0.95 us
  matrix products: 10.1 us -> 0 us
  other arithmetic: 12.6 us -> 5.29 us
  blocking collectives: 4.15 us -> 0 us
    all_to_all x2 -> x0, waiting for transfers between devices: 183 us -> none  [the longest x1 92.2 us: per_device(): lax.all_to_all(outgoing, 'adapter', split_axis=0, concat_axis=0, tiled=True)]
    ppermute x0 -> x29, starting transfers between devices: none -> 26.9 us  [the longest x18 19.7 us: send_slot(): held[chain, distance, way] = lax.ppermute(piece, 'adapter', perms[way])]
    ppermute x0 -> x29, waiting for transfers between devices: none -> 25.7 us  [the longest x18 17.5 us: send_slot(): held[chain, distance, way] = lax.ppermute(piece, 'adapter', perms[way])]
    pallas_call x0 -> x4, Pallas kernels: none -> 17.9 us  [the longest x1 7.2 us: gathered_matrices(): pl.pallas_call(delta_kernel, grid_spec=pltpu.PrefetchScalarGridSpec(num_s...]
    reshape x4 -> x0, local copies, waits for them, and re-layouts: 16.6 us -> none  [the longest x1 4.15 us: per_device(): delta.reshape(received.shape)]
    all_to_all x2 -> x0, starting transfers between devices: 11.8 us -> none  [the longest x1 7.12 us: per_device(): lax.all_to_all(outgoing, 'adapter', split_axis=0, concat_axis=0, tiled=True)]
    dot_general x2 -> x0, matrix products: 10.1 us -> none  [the longest x1 9 us: per_device(): jnp.dot(codes, matrix_b, preferred_element_type=jnp.float32)]
    gather x1 -> x0, local copies, waits for them, and re-layouts: 7.59 us -> none  [per_device(): delta = returned.reshape(-1, width)[target]]
  transfers between devices with their start and end apart: 4 -> 29, of which waited for: 2 -> 14; matrix products, arithmetic and copies ran while one was open for 2% -> 10% of each run, Pallas kernels for 0% -> 13%
where the time goes in v2:
time: 84.6 us; the launch traced here: 84.2 us
  starting transfers between devices  26.9 us (32%)
  waiting for transfers between devices  25.7 us (30%)
  Pallas kernels  17.9 us (21%)
  local copies, waits for them, and re-layouts  7.63 us (9%)
  other arithmetic  5.29 us (6%)
  between operations  0.95 us (1%)
    ppermute x18, starting transfers between devices, send_slot(): held[chain, distance, way] = lax.ppermute(piece, 'adapter', perms[way])  19.7 us
    ppermute x18, waiting for transfers between devices, send_slot(): held[chain, distance, way] = lax.ppermute(piece, 'adapter', perms[way])  17.5 us
    pallas_call x1, Pallas kernels, gathered_matrices(): pl.pallas_call(delta_kernel, grid_spec=pltpu.PrefetchScalarGridSpec(num_s...  7.2 us
    pallas_call x2, Pallas kernels, normed(): pl.pallas_call(norm_kernel, grid_spec=pltpu.PrefetchScalarGridSpec(num_sc...  6.56 us
    pallas_call x1, Pallas kernels, gathered_matrices(): pl.pallas_call(codes_kernel, out_shape=[fl(2 * full, 128), fl(2 * full, 1...  4.11 us
    unnamed x60, local copies, waits for them, and re-layouts  3.66 us
    ppermute x1, waiting for transfers between devices, gathered_matrices(): crossed = lax.ppermute(after(there, *across_far.values()), 'groups', swap)  3.15 us
    ppermute x1, waiting for transfers between devices, gathered_matrices(): part_back = lax.ppermute(other_part.reshape(-1), 'fsdp', swap)  2.27 us
  transfers between devices with their start and end apart: 29, of which 14 were waited for; matrix products, arithmetic and copies ran while one was open for 10% of the time, Pallas kernels for 13%

profile of v2, /device:TPU:0, one launch (start us, length us, event | category | flops | bytes accessed | tf_op | source)
XLA Modules:
  0.0 84.2 jit_solution(5207843370790287503)
XLA Ops:
  1.7 3.0 %collective-permute-start.7 = (bf16[64,2048]{1,0:T(8,128)(2,1)S(1)}, bf16[64,2048]{1,0:T(8,128)(2,1)}, u32[]{:S(2)}, u32[]{:S(2)}) collective-permute-start(bf16[64,2048]{1,0:T(8,128)(2,1)S(1)} %dynamic-slice_bitcast_fusion.1.rest_0_), channel_id=1, source_target_pairs={{0,2},{4,0},{8,4},{12,8},{14,12},{10,14},{6,10},{2,6},{1,3},{5,1},... | collective-permute-start | bytes 786440 | tf_op jit(solution)/shard_map/ppermute | solution.py:214
  5.6 2.0 %multiply_reduce_fusion = f32[120]{0:T(128)S(1)} fusion(bf16[120,8192]{1,0:T(8,128)(2,1)} %hidden.3), kind=kLoop, calls=%fused_computation | loop fusion | flops 2949000 | bytes 1966560 | tf_op jit(solution)/shard_map/reduce_sum | solution.py:221
  8.8 1.9 %collective-permute-start.3 = (bf16[32,4096]{1,0:T(8,128)(2,1)}, bf16[32,4096]{1,0:T(8,128)(2,1)S(1)}, u32[]{:S(2)}, u32[]{:S(2)}) collective-permute-start(bf16[32,4096]{1,0:T(8,128)(2,1)} %get-tuple-element.55), channel_id=1, source_target_pairs={{0,2},{4,0},{8,4},{12,8},{14,12},{10,14},{6,10},{2,6},{1,3},{5,1},... | collective-permute-start | bytes 786440 | tf_op jit(solution)/shard_map/ppermute | solution.py:214
  12.4 1.3 %copy-done.1 = bf16[120,8192]{1,0:T(8,128)(2,1)} copy-done((bf16[120,8192]{1,0:T(8,128)(2,1)}, bf16[120,8192]{1,0:T(8,128)(2,1)S(1)}, u32[]{:S(2)}) %copy-start.1) | copy-done | bytes 1966104
  13.6 3.2 %shard_map.95.theirs = bf16[256,2176]{1,0:T(8,128)(2,1)} custom-call(s32[2]{0:T(128)} %pad_add_fusion.place, bf16[120,8192]{1,0:T(8,128)(2,1)} %hidden.3, bf16[120,8192]{1,0:T(8,128)(2,1)} %copy-done.1, f32[128,2]{1,0:T(8,128)} %copy-done.4, f32[128,2]{1,0:T(8,128)} %copy-done.6, bf16[1,4096]{1,0:T(2,128)(2,1)} %broadcast_in_dim.6.gain), custom_call_target="tpu_custom_call" | custom-call | flops 1 | bytes 1 | tf_op jit(solution)/shard_map/pallas_call | solution.py:230
  16.9 1.7 %collective-permute-start.8 = (bf16[256,2176]{1,0:T(8,128)(2,1)}, bf16[256,2176]{1,0:T(8,128)(2,1)S(1)}, u32[]{:S(2)}, u32[]{:S(2)}) collective-permute-start(bf16[256,2176]{1,0:T(8,128)(2,1)} %shard_map.95.theirs), channel_id=1, source_target_pairs={{0,16},{16,0},{1,17},{17,1},{2,18},{18,2},{3,19},{19,3},{4,20},{20... | collective-permute-start | bytes 3342344 | tf_op jit(solution)/shard_map/ppermute | solution.py:250
  20.2 1.1 %collective-permute-start.5 = (bf16[32,4096]{1,0:T(8,128)(2,1)S(1)}, bf16[32,4096]{1,0:T(8,128)(2,1)S(1)}, u32[]{:S(2)}, u32[]{:S(2)}) collective-permute-start(bf16[32,4096]{1,0:T(8,128)(2,1)S(1)} %collective-permute-done.3.rest_3_), channel_id=1, source_target_pairs={{0,2},{4,0},{8,4},{12,8},{14,12},{10,14},{6,10},{2,6},{1,3},{5,1},... | collective-permute-start | bytes 786440 | tf_op jit(solution)/shard_map/ppermute | solution.py:214
  22.2 1.1 %collective-permute-start.10 = (bf16[64,2048]{1,0:T(8,128)(2,1)}, bf16[64,2048]{1,0:T(8,128)(2,1)}, u32[]{:S(2)}, u32[]{:S(2)}) collective-permute-start(bf16[64,2048]{1,0:T(8,128)(2,1)} %collective-permute-done.7.rest_2_), channel_id=1, source_target_pairs={{0,2},{4,0},{8,4},{12,8},{14,12},{10,14},{6,10},{2,6},{1,3},{5,1},... | collective-permute-start | bytes 786440 | tf_op jit(solution)/shard_map/ppermute | solution.py:214
  23.3 5.2 %collective-permute-done.4.rest_5_ = bf16[32,4096]{1,0:T(8,128)(2,1)S(1)} collective-permute-done((bf16[32,4096]{1,0:T(8,128)(2,1)S(1)}, bf16[32,4096]{1,0:T(8,128)(2,1)S(1)}, u32[]{:S(2)}, u32[]{:S(2)}) %collective-permute-start.4) | collective-permute-done | bytes 262176 | tf_op jit(solution)/shard_map/ppermute | solution.py:214
  29.4 1.6 %collective-permute-start.14 = (bf16[32,4096]{1,0:T(8,128)(2,1)S(1)}, bf16[32,4096]{1,0:T(8,128)(2,1)S(1)}, u32[]{:S(2)}, u32[]{:S(2)}) collective-permute-start(bf16[32,4096]{1,0:T(8,128)(2,1)S(1)} %collective-permute-done.4.rest_5_), channel_id=1, source_target_pairs={{0,4},{4,8},{8,12},{12,14},{14,10},{10,6},{6,2},{2,0},{1,5},{5,9},... | collective-permute-start | bytes 786440 | tf_op jit(solution)/shard_map/ppermute | solution.py:214
  33.5 3.3 %shard_map.96.here.mine = bf16[256,2176]{1,0:T(8,128)(2,1)} custom-call(s32[2]{0:T(128)} %pad_add_fusion.place, bf16[120,8192]{1,0:T(8,128)(2,1)} %hidden.3, bf16[120,8192]{1,0:T(8,128)(2,1)} %copy-done.1, f32[128,2]{1,0:T(8,128)} %copy-done.4, f32[128,2]{1,0:T(8,128)} %copy-done.6, bf16[1,4096]{1,0:T(2,128)(2,1)} %broadcast_in_dim.6.gain), custom_call_target="tpu_custom_call" | custom-call | flops 1 | bytes 1 | tf_op jit(solution)/shard_map/pallas_call | solution.py:230
  36.9 1.6 %collective-permute-start.11 = (bf16[64,2048]{1,0:T(8,128)(2,1)S(1)}, bf16[64,2048]{1,0:T(8,128)(2,1)S(1)}, u32[]{:S(2)}, u32[]{:S(2)}) collective-permute-start(bf16[64,2048]{1,0:T(8,128)(2,1)S(1)} %collective-permute-done.9.rest_3_), channel_id=1, source_target_pairs={{0,4},{4,8},{8,12},{12,14},{14,10},{10,6},{6,2},{2,0},{1,5},{5,9},... | collective-permute-start | bytes 786440 | tf_op jit(solution)/shard_map/ppermute | solution.py:214
  40.7 1.6 %collective-permute-start.21 = (bf16[32,4096]{1,0:T(8,128)(2,1)S(1)}, bf16[32,4096]{1,0:T(8,128)(2,1)S(1)}, u32[]{:S(2)}, u32[]{:S(2)}) collective-permute-start(bf16[32,4096]{1,0:T(8,128)(2,1)S(1)} %copy-done.7), channel_id=1, source_target_pairs={{0,4},{4,8},{8,12},{12,14},{14,10},{10,6},{6,2},{2,0},{1,5},{5,9},... | collective-permute-start | bytes 786440 | tf_op jit(solution)/shard_map/ppermute | solution.py:214
  42.7 3.5 %collective-permute-done.11.rest_5_ = bf16[64,2048]{1,0:T(8,128)(2,1)S(1)} collective-permute-done((bf16[64,2048]{1,0:T(8,128)(2,1)S(1)}, bf16[64,2048]{1,0:T(8,128)(2,1)S(1)}, u32[]{:S(2)}, u32[]{:S(2)}) %collective-permute-start.11) | collective-permute-done | bytes 262176 | tf_op jit(solution)/shard_map/ppermute | solution.py:214
  46.2 1.8 %collective-permute-done.12.rest_6_ = bf16[64,2048]{1,0:T(8,128)(2,1)S(1)} collective-permute-done((bf16[64,2048]{1,0:T(8,128)(2,1)}, bf16[64,2048]{1,0:T(8,128)(2,1)S(1)}, u32[]{:S(2)}, u32[]{:S(2)}) %collective-permute-start.12) | collective-permute-done | bytes 262176 | tf_op jit(solution)/shard_map/ppermute | solution.py:214
  48.4 1.6 %collective-permute-start.13 = (bf16[64,2048]{1,0:T(8,128)(2,1)S(1)}, bf16[64,2048]{1,0:T(8,128)(2,1)S(1)}, u32[]{:S(2)}, u32[]{:S(2)}) collective-permute-start(bf16[64,2048]{1,0:T(8,128)(2,1)S(1)} %collective-permute-done.11.rest_5_), channel_id=1, source_target_pairs={{0,4},{4,8},{8,12},{12,14},{14,10},{10,6},{6,2},{2,0},{1,5},{5,9},... | collective-permute-start | bytes 786440 | tf_op jit(solution)/shard_map/ppermute | solution.py:214
  50.0 1.8 %collective-permute-done.21.rest_2_ = bf16[32,4096]{1,0:T(8,128)(2,1)S(1)} collective-permute-done((bf16[32,4096]{1,0:T(8,128)(2,1)S(1)}, bf16[32,4096]{1,0:T(8,128)(2,1)S(1)}, u32[]{:S(2)}, u32[]{:S(2)}) %collective-permute-start.21) | collective-permute-done | bytes 262176 | tf_op jit(solution)/shard_map/ppermute | solution.py:214
  51.8 1.1 %collective-permute-start.15 = (bf16[32,4096]{1,0:T(8,128)(2,1)S(1)}, bf16[32,4096]{1,0:T(8,128)(2,1)S(1)}, u32[]{:S(2)}, u32[]{:S(2)}) collective-permute-start(bf16[32,4096]{1,0:T(8,128)(2,1)S(1)} %collective-permute-done.14.rest_9_), channel_id=1, source_target_pairs={{0,16},{16,0},{1,17},{17,1},{2,18},{18,2},{3,19},{19,3},{4,20},{20... | collective-permute-start | bytes 786440 | tf_op jit(solution)/shard_map/ppermute | solution.py:258
  53.1 1.1 %collective-permute-start.17 = (bf16[32,4096]{1,0:T(8,128)(2,1)S(1)}, bf16[32,4096]{1,0:T(8,128)(2,1)S(1)}, u32[]{:S(2)}, u32[]{:S(2)}) collective-permute-start(bf16[32,4096]{1,0:T(8,128)(2,1)S(1)} %collective-permute-done.16.rest_11_), channel_id=1, source_target_pairs={{0,16},{16,0},{1,17},{17,1},{2,18},{18,2},{3,19},{19,3},{4,20},{20... | collective-permute-start | bytes 786440 | tf_op jit(solution)/shard_map/ppermute | solution.py:258
  54.1 1.8 %collective-permute-done.22.rest_4_ = bf16[32,4096]{1,0:T(8,128)(2,1)S(1)} collective-permute-done((bf16[32,4096]{1,0:T(8,128)(2,1)S(1)}, bf16[32,4096]{1,0:T(8,128)(2,1)S(1)}, u32[]{:S(2)}, u32[]{:S(2)}) %collective-permute-start.22) | collective-permute-done | bytes 262176 | tf_op jit(solution)/shard_map/ppermute | solution.py:214
  55.9 1.6 %collective-permute-start.24 = (bf16[32,4096]{1,0:T(8,128)(2,1)S(1)}, bf16[32,4096]{1,0:T(8,128)(2,1)S(1)}, u32[]{:S(2)}, u32[]{:S(2)}) collective-permute-start(bf16[32,4096]{1,0:T(8,128)(2,1)S(1)} %collective-permute-done.21.rest_2_), channel_id=1, source_target_pairs={{0,4},{4,8},{8,12},{12,14},{14,10},{10,6},{6,2},{2,0},{1,5},{5,9},... | collective-permute-start | bytes 786440 | tf_op jit(solution)/shard_map/ppermute | solution.py:214
  58.2 1.0 %copy-done.3 = bf16[256,2176]{1,0:T(8,128)(2,1)} copy-done((bf16[256,2176]{1,0:T(8,128)(2,1)}, bf16[256,2176]{1,0:T(8,128)(2,1)S(1)}, u32[]{:S(2)}) %copy-start.3) | copy-done | bytes 1114136
  59.2 4.1 %shard_map.97 = (f32[256,128]{1,0:T(8,128)}, f32[256,128]{1,0:T(8,128)}) custom-call(bf16[256,2176]{1,0:T(8,128)(2,1)} %shard_map.96.here.mine, bf16[256,2176]{1,0:T(8,128)(2,1)} %copy-done.3, f32[1,512]{1,0:T(1,128)} %convert_element_type.41.ids, bf16[64,2048]{1,0:T(8,128)(2,1)} %copy-done.5, bf16[64,2048]{1,0:T(8,128)(2,1)} %collective-permute-done.6.rest_1_, ...), custom_call_target="tpu_custom_call" | custom-call | flops 1 | bytes 1 | tf_op jit(solution)/shard_map/pallas_call | solution.py:262
  63.3 1.1 %collective-permute-start.18 = (f32[256,128]{1,0:T(8,128)}, f32[256,128]{1,0:T(8,128)S(1)}, u32[]{:S(2)}, u32[]{:S(2)}) collective-permute-start(f32[256,128]{1,0:T(8,128)} %get-tuple-element.42), channel_id=1, source_target_pairs={{0,16},{16,0},{1,17},{17,1},{2,18},{18,2},{3,19},{19,3},{4,20},{20... | collective-permute-start | bytes 393224 | tf_op jit(solution)/shard_map/ppermute | solution.py:268
  64.4 1.0 %collective-permute-start.26 = (bf16[32,4096]{1,0:T(8,128)(2,1)S(1)}, bf16[32,4096]{1,0:T(8,128)(2,1)S(1)}, u32[]{:S(2)}, u32[]{:S(2)}) collective-permute-start(bf16[32,4096]{1,0:T(8,128)(2,1)S(1)} %collective-permute-done.23.rest_13_), channel_id=1, source_target_pairs={{0,16},{16,0},{1,17},{17,1},{2,18},{18,2},{3,19},{19,3},{4,20},{20... | collective-permute-start | bytes 786440 | tf_op jit(solution)/shard_map/ppermute | solution.py:271
  65.4 3.1 %collective-permute-done.18.crossed = f32[256,128]{1,0:T(8,128)S(1)} collective-permute-done((f32[256,128]{1,0:T(8,128)}, f32[256,128]{1,0:T(8,128)S(1)}, u32[]{:S(2)}, u32[]{:S(2)}) %collective-permute-start.18) | collective-permute-done | bytes 131104 | tf_op jit(solution)/shard_map/ppermute | solution.py:268
  68.6 1.3 %collective-permute-done.20.beyond = f32[256,128]{1,0:T(8,128)S(1)} collective-permute-done((f32[256,128]{1,0:T(8,128)S(1)}, f32[256,128]{1,0:T(8,128)S(1)}, u32[]{:S(2)}, u32[]{:S(2)}) %collective-permute-start.20) | collective-permute-done | bytes 131104 | tf_op jit(solution)/shard_map/ppermute | solution.py:273
  69.9 1.5 %collective-permute-done.26.rest_14_ = bf16[32,4096]{1,0:T(8,128)(2,1)S(1)} collective-permute-done((bf16[32,4096]{1,0:T(8,128)(2,1)S(1)}, bf16[32,4096]{1,0:T(8,128)(2,1)S(1)}, u32[]{:S(2)}, u32[]{:S(2)}) %collective-permute-start.26) | collective-permute-done | bytes 262176 | tf_op jit(solution)/shard_map/ppermute | solution.py:271
  72.0 7.2 %shard_map.98 = (bf16[120,8192]{1,0:T(8,128)(2,1)}, bf16[120,4096]{1,0:T(8,128)(2,1)}, f32[1,128]{1,0:T(1,128)}, f32[1,128]{1,0:T(1,128)}) custom-call(s32[2]{0:T(128)} %pad_add_fusion.place, bf16[256,2176]{1,0:T(8,128)(2,1)} %shard_map.96.here.mine, bf16[256,2176]{1,0:T(8,128)(2,1)} %shard_map.95.theirs, f32[256,128]{1,0:T(8,128)} %get-tuple-element.38.here, ...), custom_call_target="tpu_custom_call" | custom-call | flops 1 | bytes 1 | tf_op jit(solution)/shard_map/pallas_call | solution.py:279
  79.8 2.3 %collective-permute-done.28 = f32[128]{0:T(128)S(1)} collective-permute-done((f32[128]{0:T(128)}, f32[128]{0:T(128)S(1)}, u32[]{:S(2)}, u32[]{:S(2)}) %collective-permute-start.28) | collective-permute-done | bytes 544 | tf_op jit(solution)/shard_map/ppermute | solution.py:308
  82.1 1.1 %bitcast_add_fusion = f32[128]{0:T(128)} fusion(f32[128]{0:T(128)S(1)} %collective-permute-done.28, f32[1,128]{1,0:T(1,128)} %get-tuple-element.52), kind=kLoop, calls=%fused_computation.12 | loop fusion | flops 128 | bytes 1536 | tf_op jit(solution)/shard_map/add | solution.py:310
  83.2 1.0 %constant_dynamic-update-slice_fusion = bf16[120,8192]{1,0:T(8,128)(2,1)} fusion(bf16[120,8192]{1,0:T(8,128)(2,1)} %get-tuple-element.50, bf16[120,4096]{1,0:T(8,128)(2,1)S(1)} %collective-permute-done.27, s32[]{:T(128)S(6)} %select_n.21), kind=kLoop, calls=%fused_computation.6 | loop fusion | bytes 1966084 | tf_op jit(solution)/shard_map/dynamic_update_slice | solution.py:309
  (107 shorter events, 15.9 us)
Async XLA Ops:
  0.7 11.7 %collective-permute-start = (bf16[120,8192]{1,0:T(8,128)(2,1)}, bf16[120,8192]{1,0:T(8,128)(2,1)S(1)}, u32[]{:S(2)}, u32[]{:S(2)}) collective-permute-start(bf16[120,8192]{1,0:T(8,128)(2,1)} %hidden.3), channel_id=1, source_target_pairs={{0,1},{1,0},{2,3},{3,2},{4,5},{5,4},{6,7},{7,6},{8,9},{9,8},{10,11... | collective-permute-start | bytes 5898248 | tf_op jit(solution)/shard_map/ppermute | solution.py:219
  1.7 15.2 %collective-permute-start.7 = (bf16[64,2048]{1,0:T(8,128)(2,1)S(1)}, bf16[64,2048]{1,0:T(8,128)(2,1)}, u32[]{:S(2)}, u32[]{:S(2)}) collective-permute-start(bf16[64,2048]{1,0:T(8,128)(2,1)S(1)} %dynamic-slice_bitcast_fusion.1.rest_0_), channel_id=1, source_target_pairs={{0,2},{4,0},{8,4},{12,8},{14,12},{10,14},{6,10},{2,6},{1,3},{5,1},... | collective-permute-start | bytes 786440 | tf_op jit(solution)/shard_map/ppermute | solution.py:214
  4.7 12.2 %collective-permute-start.6 = (bf16[64,2048]{1,0:T(8,128)(2,1)S(1)}, bf16[64,2048]{1,0:T(8,128)(2,1)}, u32[]{:S(2)}, u32[]{:S(2)}) collective-permute-start(bf16[64,2048]{1,0:T(8,128)(2,1)S(1)} %dynamic-slice_bitcast_fusion.1.rest_0_), channel_id=1, source_target_pairs={{0,4},{4,8},{8,12},{12,14},{14,10},{10,6},{6,2},{2,0},{1,5},{5,9},... | collective-permute-start | bytes 786440 | tf_op jit(solution)/shard_map/ppermute | solution.py:214
  7.8 2.8 %collective-permute-start.1 = (f32[128,2]{1,0:T(8,128)S(1)}, f32[128,2]{1,0:T(8,128)S(1)}, u32[]{:S(2)}, u32[]{:S(2)}) collective-permute-start(f32[128,2]{1,0:T(8,128)S(1)} %concatenate.7.own_small), channel_id=1, source_target_pairs={{0,1},{1,0},{2,3},{3,2},{4,5},{5,4},{6,7},{7,6},{8,9},{9,8},{10,11... | collective-permute-start | bytes 3080 | tf_op jit(solution)/shard_map/ppermute | solution.py:224
  8.8 9.8 %collective-permute-start.3 = (bf16[32,4096]{1,0:T(8,128)(2,1)}, bf16[32,4096]{1,0:T(8,128)(2,1)S(1)}, u32[]{:S(2)}, u32[]{:S(2)}) collective-permute-start(bf16[32,4096]{1,0:T(8,128)(2,1)} %get-tuple-element.55), channel_id=1, source_target_pairs={{0,2},{4,0},{8,4},{12,8},{14,12},{10,14},{6,10},{2,6},{1,3},{5,1},... | collective-permute-start | bytes 786440 | tf_op jit(solution)/shard_map/ppermute | solution.py:214
  10.6 8.6 %collective-permute-start.2 = (bf16[32,4096]{1,0:T(8,128)(2,1)}, bf16[32,4096]{1,0:T(8,128)(2,1)S(1)}, u32[]{:S(2)}, u32[]{:S(2)}) collective-permute-start(bf16[32,4096]{1,0:T(8,128)(2,1)} %get-tuple-element.55), channel_id=1, source_target_pairs={{0,4},{4,8},{8,12},{12,14},{14,10},{10,6},{6,2},{2,0},{1,5},{5,9},... | collective-permute-start | bytes 786440 | tf_op jit(solution)/shard_map/ppermute | solution.py:214
  16.9 41.3 %collective-permute-start.8 = (bf16[256,2176]{1,0:T(8,128)(2,1)}, bf16[256,2176]{1,0:T(8,128)(2,1)S(1)}, u32[]{:S(2)}, u32[]{:S(2)}) collective-permute-start(bf16[256,2176]{1,0:T(8,128)(2,1)} %shard_map.95.theirs), channel_id=1, source_target_pairs={{0,16},{16,0},{1,17},{17,1},{2,18},{18,2},{3,19},{19,3},{4,20},{20... | collective-permute-start | bytes 3342344 | tf_op jit(solution)/shard_map/ppermute | solution.py:250
  19.3 9.2 %collective-permute-start.4 = (bf16[32,4096]{1,0:T(8,128)(2,1)S(1)}, bf16[32,4096]{1,0:T(8,128)(2,1)S(1)}, u32[]{:S(2)}, u32[]{:S(2)}) collective-permute-start(bf16[32,4096]{1,0:T(8,128)(2,1)S(1)} %collective-permute-done.2.rest_1_), channel_id=1, source_target_pairs={{0,4},{4,8},{8,12},{12,14},{14,10},{10,6},{6,2},{2,0},{1,5},{5,9},... | collective-permute-start | bytes 786440 | tf_op jit(solution)/shard_map/ppermute | solution.py:214
  20.2 9.2 %collective-permute-start.5 = (bf16[32,4096]{1,0:T(8,128)(2,1)S(1)}, bf16[32,4096]{1,0:T(8,128)(2,1)S(1)}, u32[]{:S(2)}, u32[]{:S(2)}) collective-permute-start(bf16[32,4096]{1,0:T(8,128)(2,1)S(1)} %collective-permute-done.3.rest_3_), channel_id=1, source_target_pairs={{0,2},{4,0},{8,4},{12,8},{14,12},{10,14},{6,10},{2,6},{1,3},{5,1},... | collective-permute-start | bytes 786440 | tf_op jit(solution)/shard_map/ppermute | solution.py:214
  21.3 15.6 %collective-permute-start.9 = (bf16[64,2048]{1,0:T(8,128)(2,1)}, bf16[64,2048]{1,0:T(8,128)(2,1)S(1)}, u32[]{:S(2)}, u32[]{:S(2)}) collective-permute-start(bf16[64,2048]{1,0:T(8,128)(2,1)} %collective-permute-done.6.rest_1_), channel_id=1, source_target_pairs={{0,4},{4,8},{8,12},{12,14},{14,10},{10,6},{6,2},{2,0},{1,5},{5,9},... | collective-permute-start | bytes 786440 | tf_op jit(solution)/shard_map/ppermute | solution.py:214
  22.2 14.7 %collective-permute-start.10 = (bf16[64,2048]{1,0:T(8,128)(2,1)}, bf16[64,2048]{1,0:T(8,128)(2,1)}, u32[]{:S(2)}, u32[]{:S(2)}) collective-permute-start(bf16[64,2048]{1,0:T(8,128)(2,1)} %collective-permute-done.7.rest_2_), channel_id=1, source_target_pairs={{0,2},{4,0},{8,4},{12,8},{14,12},{10,14},{6,10},{2,6},{1,3},{5,1},... | collective-permute-start | bytes 786440 | tf_op jit(solution)/shard_map/ppermute | solution.py:214
  29.4 10.3 %collective-permute-start.14 = (bf16[32,4096]{1,0:T(8,128)(2,1)S(1)}, bf16[32,4096]{1,0:T(8,128)(2,1)S(1)}, u32[]{:S(2)}, u32[]{:S(2)}) collective-permute-start(bf16[32,4096]{1,0:T(8,128)(2,1)S(1)} %collective-permute-done.4.rest_5_), channel_id=1, source_target_pairs={{0,4},{4,8},{8,12},{12,14},{14,10},{10,6},{6,2},{2,0},{1,5},{5,9},... | collective-permute-start | bytes 786440 | tf_op jit(solution)/shard_map/ppermute | solution.py:214
  31.0 9.7 %collective-permute-start.16 = (bf16[32,4096]{1,0:T(8,128)(2,1)S(1)}, bf16[32,4096]{1,0:T(8,128)(2,1)S(1)}, u32[]{:S(2)}, u32[]{:S(2)}) collective-permute-start(bf16[32,4096]{1,0:T(8,128)(2,1)S(1)} %collective-permute-done.5.rest_7_), channel_id=1, source_target_pairs={{0,2},{4,0},{8,4},{12,8},{14,12},{10,14},{6,10},{2,6},{1,3},{5,1},... | collective-permute-start | bytes 786440 | tf_op jit(solution)/shard_map/ppermute | solution.py:214
  36.9 21.3 %copy-start.14 = (bf16[64,2048]{1,0:T(8,128)(2,1)}, bf16[64,2048]{1,0:T(8,128)(2,1)S(1)}, u32[]{:S(2)}) copy-start(bf16[64,2048]{1,0:T(8,128)(2,1)S(1)} %collective-permute-done.9.rest_3_) | copy-start | bytes 786436
  36.9 9.3 %collective-permute-start.11 = (bf16[64,2048]{1,0:T(8,128)(2,1)S(1)}, bf16[64,2048]{1,0:T(8,128)(2,1)S(1)}, u32[]{:S(2)}, u32[]{:S(2)}) collective-permute-start(bf16[64,2048]{1,0:T(8,128)(2,1)S(1)} %collective-permute-done.9.rest_3_), channel_id=1, source_target_pairs={{0,4},{4,8},{8,12},{12,14},{14,10},{10,6},{6,2},{2,0},{1,5},{5,9},... | collective-permute-start | bytes 786440 | tf_op jit(solution)/shard_map/ppermute | solution.py:214
  38.5 9.5 %collective-permute-start.12 = (bf16[64,2048]{1,0:T(8,128)(2,1)}, bf16[64,2048]{1,0:T(8,128)(2,1)S(1)}, u32[]{:S(2)}, u32[]{:S(2)}) collective-permute-start(bf16[64,2048]{1,0:T(8,128)(2,1)} %collective-permute-done.10.rest_4_), channel_id=1, source_target_pairs={{0,2},{4,0},{8,4},{12,8},{14,12},{10,14},{6,10},{2,6},{1,3},{5,1},... | collective-permute-start | bytes 786440 | tf_op jit(solution)/shard_map/ppermute | solution.py:214
  39.8 31.6 %copy-start.12 = (bf16[32,4096]{1,0:T(8,128)(2,1)}, bf16[32,4096]{1,0:T(8,128)(2,1)S(1)}, u32[]{:S(2)}) copy-start(bf16[32,4096]{1,0:T(8,128)(2,1)S(1)} %collective-permute-done.14.rest_9_) | copy-start | bytes 786436
  40.7 30.7 %copy-start.13 = (bf16[32,4096]{1,0:T(8,128)(2,1)}, bf16[32,4096]{1,0:T(8,128)(2,1)S(1)}, u32[]{:S(2)}) copy-start(bf16[32,4096]{1,0:T(8,128)(2,1)S(1)} %collective-permute-done.16.rest_11_) | copy-start | bytes 786436
  40.7 11.1 %collective-permute-start.21 = (bf16[32,4096]{1,0:T(8,128)(2,1)S(1)}, bf16[32,4096]{1,0:T(8,128)(2,1)S(1)}, u32[]{:S(2)}, u32[]{:S(2)}) collective-permute-start(bf16[32,4096]{1,0:T(8,128)(2,1)S(1)} %copy-done.7), channel_id=1, source_target_pairs={{0,4},{4,8},{8,12},{12,14},{14,10},{10,6},{6,2},{2,0},{1,5},{5,9},... | collective-permute-start | bytes 786440 | tf_op jit(solution)/shard_map/ppermute | solution.py:214
  42.3 10.8 %collective-permute-start.23 = (bf16[32,4096]{1,0:T(8,128)(2,1)S(1)}, bf16[32,4096]{1,0:T(8,128)(2,1)S(1)}, u32[]{:S(2)}, u32[]{:S(2)}) collective-permute-start(bf16[32,4096]{1,0:T(8,128)(2,1)S(1)} %collective-permute-done.16.rest_11_), channel_id=1, source_target_pairs={{0,2},{4,0},{8,4},{12,8},{14,12},{10,14},{6,10},{2,6},{1,3},{5,1},... | collective-permute-start | bytes 786440 | tf_op jit(solution)/shard_map/ppermute | solution.py:214
  48.0 7.9 %collective-permute-start.22 = (bf16[32,4096]{1,0:T(8,128)(2,1)S(1)}, bf16[32,4096]{1,0:T(8,128)(2,1)S(1)}, u32[]{:S(2)}, u32[]{:S(2)}) collective-permute-start(bf16[32,4096]{1,0:T(8,128)(2,1)S(1)} %copy-done.7), channel_id=1, source_target_pairs={{0,2},{4,0},{8,4},{12,8},{14,12},{10,14},{6,10},{2,6},{1,3},{5,1},... | collective-permute-start | bytes 786440 | tf_op jit(solution)/shard_map/ppermute | solution.py:214
  48.4 9.0 %collective-permute-start.13 = (bf16[64,2048]{1,0:T(8,128)(2,1)S(1)}, bf16[64,2048]{1,0:T(8,128)(2,1)S(1)}, u32[]{:S(2)}, u32[]{:S(2)}) collective-permute-start(bf16[64,2048]{1,0:T(8,128)(2,1)S(1)} %collective-permute-done.11.rest_5_), channel_id=1, source_target_pairs={{0,4},{4,8},{8,12},{12,14},{14,10},{10,6},{6,2},{2,0},{1,5},{5,9},... | collective-permute-start | bytes 786440 | tf_op jit(solution)/shard_map/ppermute | solution.py:214
  51.8 11.4 %collective-permute-start.15 = (bf16[32,4096]{1,0:T(8,128)(2,1)S(1)}, bf16[32,4096]{1,0:T(8,128)(2,1)S(1)}, u32[]{:S(2)}, u32[]{:S(2)}) collective-permute-start(bf16[32,4096]{1,0:T(8,128)(2,1)S(1)} %collective-permute-done.14.rest_9_), channel_id=1, source_target_pairs={{0,16},{16,0},{1,17},{17,1},{2,18},{18,2},{3,19},{19,3},{4,20},{20... | collective-permute-start | bytes 786440 | tf_op jit(solution)/shard_map/ppermute | solution.py:258
  53.1 10.2 %collective-permute-start.17 = (bf16[32,4096]{1,0:T(8,128)(2,1)S(1)}, bf16[32,4096]{1,0:T(8,128)(2,1)S(1)}, u32[]{:S(2)}, u32[]{:S(2)}) collective-permute-start(bf16[32,4096]{1,0:T(8,128)(2,1)S(1)} %collective-permute-done.16.rest_11_), channel_id=1, source_target_pairs={{0,16},{16,0},{1,17},{17,1},{2,18},{18,2},{3,19},{19,3},{4,20},{20... | collective-permute-start | bytes 786440 | tf_op jit(solution)/shard_map/ppermute | solution.py:258
  55.9 12.7 %collective-permute-start.24 = (bf16[32,4096]{1,0:T(8,128)(2,1)S(1)}, bf16[32,4096]{1,0:T(8,128)(2,1)S(1)}, u32[]{:S(2)}, u32[]{:S(2)}) collective-permute-start(bf16[32,4096]{1,0:T(8,128)(2,1)S(1)} %collective-permute-done.21.rest_2_), channel_id=1, source_target_pairs={{0,4},{4,8},{8,12},{12,14},{14,10},{10,6},{6,2},{2,0},{1,5},{5,9},... | collective-permute-start | bytes 786440 | tf_op jit(solution)/shard_map/ppermute | solution.py:214
  57.4 11.1 %collective-permute-start.25 = (bf16[32,4096]{1,0:T(8,128)(2,1)S(1)}, bf16[32,4096]{1,0:T(8,128)(2,1)}, u32[]{:S(2)}, u32[]{:S(2)}) collective-permute-start(bf16[32,4096]{1,0:T(8,128)(2,1)S(1)} %collective-permute-done.22.rest_4_), channel_id=1, source_target_pairs={{0,2},{4,0},{8,4},{12,8},{14,12},{10,14},{6,10},{2,6},{1,3},{5,1},... | collective-permute-start | bytes 786440 | tf_op jit(solution)/shard_map/ppermute | solution.py:214
  63.3 5.2 %collective-permute-start.18 = (f32[256,128]{1,0:T(8,128)}, f32[256,128]{1,0:T(8,128)S(1)}, u32[]{:S(2)}, u32[]{:S(2)}) collective-permute-start(f32[256,128]{1,0:T(8,128)} %get-tuple-element.42), channel_id=1, source_target_pairs={{0,16},{16,0},{1,17},{17,1},{2,18},{18,2},{3,19},{19,3},{4,20},{20... | collective-permute-start | bytes 393224 | tf_op jit(solution)/shard_map/ppermute | solution.py:268
  64.4 6.9 %collective-permute-start.26 = (bf16[32,4096]{1,0:T(8,128)(2,1)S(1)}, bf16[32,4096]{1,0:T(8,128)(2,1)S(1)}, u32[]{:S(2)}, u32[]{:S(2)}) collective-permute-start(bf16[32,4096]{1,0:T(8,128)(2,1)S(1)} %collective-permute-done.23.rest_13_), channel_id=1, source_target_pairs={{0,16},{16,0},{1,17},{17,1},{2,18},{18,2},{3,19},{19,3},{4,20},{20... | collective-permute-start | bytes 786440 | tf_op jit(solution)/shard_map/ppermute | solution.py:271
  65.4 3.2 %collective-permute-start.19 = (f32[256,128]{1,0:T(8,128)}, f32[256,128]{1,0:T(8,128)S(1)}, u32[]{:S(2)}, u32[]{:S(2)}) collective-permute-start(f32[256,128]{1,0:T(8,128)} %get-tuple-element.38.here), channel_id=1, source_target_pairs={{0,1},{1,0},{2,3},{3,2},{4,5},{5,4},{6,7},{7,6},{8,9},{9,8},{10,11... | collective-permute-start | bytes 393224 | tf_op jit(solution)/shard_map/ppermute | solution.py:272
  68.5 1.3 %collective-permute-start.20 = (f32[256,128]{1,0:T(8,128)S(1)}, f32[256,128]{1,0:T(8,128)S(1)}, u32[]{:S(2)}, u32[]{:S(2)}) collective-permute-start(f32[256,128]{1,0:T(8,128)S(1)} %collective-permute-done.18.crossed), channel_id=1, source_target_pairs={{0,1},{1,0},{2,3},{3,2},{4,5},{5,4},{6,7},{7,6},{8,9},{9,8},{10,11... | collective-permute-start | bytes 393224 | tf_op jit(solution)/shard_map/ppermute | solution.py:273
  79.2 4.0 %collective-permute-start.27 = (bf16[120,4096]{1,0:T(8,128)(2,1)}, bf16[120,4096]{1,0:T(8,128)(2,1)S(1)}, u32[]{:S(2)}, u32[]{:S(2)}) collective-permute-start(bf16[120,4096]{1,0:T(8,128)(2,1)} %get-tuple-element.51), channel_id=1, source_target_pairs={{0,1},{1,0},{2,3},{3,2},{4,5},{5,4},{6,7},{7,6},{8,9},{9,8},{10,11... | collective-permute-start | bytes 2949128 | tf_op jit(solution)/shard_map/ppermute | solution.py:307
  79.3 2.8 %collective-permute-start.28 = (f32[128]{0:T(128)}, f32[128]{0:T(128)S(1)}, u32[]{:S(2)}, u32[]{:S(2)}) collective-permute-start(f32[128]{0:T(128)} %bitcast.24), channel_id=1, source_target_pairs={{0,1},{1,0},{2,3},{3,2},{4,5},{5,4},{6,7},{7,6},{8,9},{9,8},{10,11... | collective-permute-start | bytes 1544 | tf_op jit(solution)/shard_map/ppermute | solution.py:308
  (27 other events, 216.2 us)

commit v3 on v2

--- a/solution.py
+++ b/solution.py
@@ -6,7 +6,7 @@
 from jax.sharding import PartitionSpec as P
 
 GATHER_LIMIT = 12 << 20
-VMEM_LIMIT = 60 << 20
+VMEM_LIMIT = 32 << 20
 
 
 def routed_rows(hidden, adapter_ids, owner_map, down_a, up_b, norm_gain, reward_head):

time: 84.6 us -> 81.7 us (0.966)
  waiting for transfers between devices: 25.7 us -> 33.6 us
  local copies, waits for them, and re-layouts: 7.63 us -> 2.69 us
  Pallas kernels: 17.9 us -> 13.7 us
  other arithmetic: 5.29 us -> 4.08 us
    ppermute x18, waiting for transfers between devices: 17.5 us -> 22.9 us  [send_slot(): held[chain, distance, way] = lax.ppermute(piece, 'adapter', perms[way])]
    unnamed x60 -> x12, local copies, waits for them, and re-layouts: 3.66 us -> 0.51 us
    ppermute x2, waiting for transfers between devices: 0.01 us -> 2.6 us  [gathered_matrices(): lax.ppermute(held[1, d, w if d < far else -1], 'groups', swap)]
    pallas_call x2, Pallas kernels: 6.56 us -> 4.83 us  [normed(): pl.pallas_call(norm_kernel, grid_spec=pltpu.PrefetchScalarGridSpec(num_sc...]
    pallas_call x1, Pallas kernels: 4.11 us -> 2.81 us  [gathered_matrices(): pl.pallas_call(codes_kernel, out_shape=[fl(2 * full, 128), fl(2 * full, 1...]
    broadcast_in_dim x2, local copies, waits for them, and re-layouts: 1.21 us -> 0.02 us  [gathered_matrices(): gain, head = (norm_gain[None, :], reward_head[None, :])]
    pallas_call x1, Pallas kernels: 7.2 us -> 6.08 us  [gathered_matrices(): pl.pallas_call(delta_kernel, grid_spec=pltpu.PrefetchScalarGridSpec(num_s...]
  transfers between devices with their start and end apart: 29 -> 29, of which waited for: 14 -> 17; matrix products, arithmetic and copies ran while one was open for 10% -> 6% of each run, Pallas kernels for 13% -> 9%
where the time goes in v3:
time: 81.7 us; the launch traced here: 81.3 us
  waiting for transfers between devices  33.6 us (41%)
  starting transfers between devices  26.4 us (32%)
  Pallas kernels  13.7 us (17%)
  other arithmetic  4.08 us (5%)
  local copies, waits for them, and re-layouts  2.69 us (3%)
    ppermute x18, waiting for transfers between devices, send_slot(): held[chain, distance, way] = lax.ppermute(piece, 'adapter', perms[way])  22.9 us
    ppermute x18, starting transfers between devices, send_slot(): held[chain, distance, way] = lax.ppermute(piece, 'adapter', perms[way])  19.7 us
    pallas_call x1, Pallas kernels, gathered_matrices(): pl.pallas_call(delta_kernel, grid_spec=pltpu.PrefetchScalarGridSpec(num_s...  6.08 us
    pallas_call x2, Pallas kernels, normed(): pl.pallas_call(norm_kernel, grid_spec=pltpu.PrefetchScalarGridSpec(num_sc...  4.83 us
    ppermute x1, waiting for transfers between devices, gathered_matrices(): crossed = lax.ppermute(after(there, *across_far.values()), 'groups', swap)  2.94 us
    pallas_call x1, Pallas kernels, gathered_matrices(): pl.pallas_call(codes_kernel, out_shape=[fl(2 * full, 128), fl(2 * full, 1...  2.81 us
    ppermute x2, waiting for transfers between devices, gathered_matrices(): lax.ppermute(held[1, d, w if d < far else -1], 'groups', swap)  2.6 us
    ppermute x1, waiting for transfers between devices, gathered_matrices(): part_back = lax.ppermute(other_part.reshape(-1), 'fsdp', swap)  2.06 us
  transfers between devices with their start and end apart: 29, of which 17 were waited for; matrix products, arithmetic and copies ran while one was open for 6% of the time, Pallas kernels for 9%

profile of v3, /device:TPU:0, one launch (start us, length us, event | category | flops | bytes accessed | tf_op | source)
XLA Modules:
  0.0 81.3 jit_solution(11148950863390769060)
XLA Ops:
  1.7 3.0 %collective-permute-start.7 = (bf16[64,2048]{1,0:T(8,128)(2,1)S(1)}, bf16[64,2048]{1,0:T(8,128)(2,1)}, u32[]{:S(2)}, u32[]{:S(2)}) collective-permute-start(bf16[64,2048]{1,0:T(8,128)(2,1)S(1)} %dynamic-slice_bitcast_fusion.1.rest_0_), channel_id=1, source_target_pairs={{0,2},{4,0},{8,4},{12,8},{14,12},{10,14},{6,10},{2,6},{1,3},{5,1},... | collective-permute-start | bytes 786440 | tf_op jit(solution)/shard_map/ppermute | solution.py:214
  4.8 0.8 select_reduce_fusion
  5.6 2.0 %multiply_reduce_fusion = f32[120]{0:T(128)S(1)} fusion(bf16[120,8192]{1,0:T(8,128)(2,1)} %hidden.3), kind=kLoop, calls=%fused_computation | loop fusion | flops 2949000 | bytes 1966560 | tf_op jit(solution)/shard_map/reduce_sum | solution.py:221
  7.9 0.9 %dynamic-slice_bitcast_fusion = (bf16[32,4096]{1,0:T(8,128)(2,1)}, bf16[32,4096]{1,0:T(8,128)(2,1)}) fusion(bf16[1,64,4096]{2,1,0:T(8,128)(2,1)S(1)} %copy-done.2, s32[]{:T(128)S(6)} %select_n.20, s32[]{:T(128)S(6)} %select_n.18), kind=kLoop, calls=%fused_computation.1 | loop fusion | bytes 1048584 | tf_op jit(solution)/shard_map/dynamic_slice | solution.py:201
  8.7 1.9 %collective-permute-start.3 = (bf16[32,4096]{1,0:T(8,128)(2,1)}, bf16[32,4096]{1,0:T(8,128)(2,1)}, u32[]{:S(2)}, u32[]{:S(2)}) collective-permute-start(bf16[32,4096]{1,0:T(8,128)(2,1)} %get-tuple-element.55), channel_id=1, source_target_pairs={{0,2},{4,0},{8,4},{12,8},{14,12},{10,14},{6,10},{2,6},{1,3},{5,1},... | collective-permute-start | bytes 786440 | tf_op jit(solution)/shard_map/ppermute | solution.py:214
  11.2 2.9 %shard_map.95.theirs = bf16[256,2176]{1,0:T(8,128)(2,1)} custom-call(s32[2]{0:T(128)S(1)} %pad_add_fusion.place, bf16[120,8192]{1,0:T(8,128)(2,1)S(1)} %copy-done.1, bf16[120,8192]{1,0:T(8,128)(2,1)} %collective-permute-done.other, f32[128,2]{1,0:T(8,128)S(1)} %concatenate.7.own_small, f32[128,2]{1,0:T(8,128)S(1)} %collective-permute-done.1.other_small, ...), custom_call_target="tpu_custom_call" | custom-call | flops 1 | bytes 1 | tf_op jit(solution)/shard_map/pallas_call | solution.py:230
  14.1 1.6 %collective-permute-start.8 = (bf16[256,2176]{1,0:T(8,128)(2,1)}, bf16[256,2176]{1,0:T(8,128)(2,1)}, u32[]{:S(2)}, u32[]{:S(2)}) collective-permute-start(bf16[256,2176]{1,0:T(8,128)(2,1)} %shard_map.95.theirs), channel_id=1, source_target_pairs={{0,16},{16,0},{1,17},{17,1},{2,18},{18,2},{3,19},{19,3},{4,20},{20... | collective-permute-start | bytes 3342344 | tf_op jit(solution)/shard_map/ppermute | solution.py:250
  15.7 2.3 %collective-permute-done.3.rest_3_ = bf16[32,4096]{1,0:T(8,128)(2,1)} collective-permute-done((bf16[32,4096]{1,0:T(8,128)(2,1)}, bf16[32,4096]{1,0:T(8,128)(2,1)}, u32[]{:S(2)}, u32[]{:S(2)}) %collective-permute-start.3) | collective-permute-done | bytes 262176 | tf_op jit(solution)/shard_map/ppermute | solution.py:214
  18.0 1.4 %collective-permute-done.2.rest_1_ = bf16[32,4096]{1,0:T(8,128)(2,1)} collective-permute-done((bf16[32,4096]{1,0:T(8,128)(2,1)}, bf16[32,4096]{1,0:T(8,128)(2,1)}, u32[]{:S(2)}, u32[]{:S(2)}) %collective-permute-start.2) | collective-permute-done | bytes 262176 | tf_op jit(solution)/shard_map/ppermute | solution.py:214
  19.8 1.6 %collective-permute-start.5 = (bf16[32,4096]{1,0:T(8,128)(2,1)}, bf16[32,4096]{1,0:T(8,128)(2,1)}, u32[]{:S(2)}, u32[]{:S(2)}) collective-permute-start(bf16[32,4096]{1,0:T(8,128)(2,1)} %collective-permute-done.3.rest_3_), channel_id=1, source_target_pairs={{0,2},{4,0},{8,4},{12,8},{14,12},{10,14},{6,10},{2,6},{1,3},{5,1},... | collective-permute-start | bytes 786440 | tf_op jit(solution)/shard_map/ppermute | solution.py:214
  21.8 1.6 %collective-permute-start.10 = (bf16[64,2048]{1,0:T(8,128)(2,1)}, bf16[64,2048]{1,0:T(8,128)(2,1)}, u32[]{:S(2)}, u32[]{:S(2)}) collective-permute-start(bf16[64,2048]{1,0:T(8,128)(2,1)} %collective-permute-done.7.rest_2_), channel_id=1, source_target_pairs={{0,2},{4,0},{8,4},{12,8},{14,12},{10,14},{6,10},{2,6},{1,3},{5,1},... | collective-permute-start | bytes 786440 | tf_op jit(solution)/shard_map/ppermute | solution.py:214
  23.4 5.5 %collective-permute-done.4.rest_5_ = bf16[32,4096]{1,0:T(8,128)(2,1)} collective-permute-done((bf16[32,4096]{1,0:T(8,128)(2,1)}, bf16[32,4096]{1,0:T(8,128)(2,1)}, u32[]{:S(2)}, u32[]{:S(2)}) %collective-permute-start.4) | collective-permute-done | bytes 262176 | tf_op jit(solution)/shard_map/ppermute | solution.py:214
  29.3 1.7 %collective-permute-start.14 = (bf16[32,4096]{1,0:T(8,128)(2,1)}, bf16[32,4096]{1,0:T(8,128)(2,1)}, u32[]{:S(2)}, u32[]{:S(2)}) collective-permute-start(bf16[32,4096]{1,0:T(8,128)(2,1)} %collective-permute-done.4.rest_5_), channel_id=1, source_target_pairs={{0,4},{4,8},{8,12},{12,14},{14,10},{10,6},{6,2},{2,0},{1,5},{5,9},... | collective-permute-start | bytes 786440 | tf_op jit(solution)/shard_map/ppermute | solution.py:214
  32.2 1.9 %shard_map.96.here.mine = bf16[256,2176]{1,0:T(8,128)(2,1)S(1)} custom-call(s32[2]{0:T(128)S(1)} %pad_add_fusion.place, bf16[120,8192]{1,0:T(8,128)(2,1)S(1)} %copy-done.1, bf16[120,8192]{1,0:T(8,128)(2,1)} %collective-permute-done.other, f32[128,2]{1,0:T(8,128)S(1)} %concatenate.7.own_small, f32[128,2]{1,0:T(8,128)S(1)} %collective-permute-done.1.other_small, ...), custom_call_target="tpu_custom_call" | custom-call | flops 1 | bytes 1 | tf_op jit(solution)/shard_map/pallas_call | solution.py:230
  34.9 1.7 %collective-permute-start.11 = (bf16[64,2048]{1,0:T(8,128)(2,1)}, bf16[64,2048]{1,0:T(8,128)(2,1)S(1)}, u32[]{:S(2)}, u32[]{:S(2)}) collective-permute-start(bf16[64,2048]{1,0:T(8,128)(2,1)} %collective-permute-done.9.rest_3_), channel_id=1, source_target_pairs={{0,4},{4,8},{8,12},{12,14},{14,10},{10,6},{6,2},{2,0},{1,5},{5,9},... | collective-permute-start | bytes 786440 | tf_op jit(solution)/shard_map/ppermute | solution.py:214
  37.0 3.2 %collective-permute-done.14.rest_9_ = bf16[32,4096]{1,0:T(8,128)(2,1)} collective-permute-done((bf16[32,4096]{1,0:T(8,128)(2,1)}, bf16[32,4096]{1,0:T(8,128)(2,1)}, u32[]{:S(2)}, u32[]{:S(2)}) %collective-permute-start.14) | collective-permute-done | bytes 262176 | tf_op jit(solution)/shard_map/ppermute | solution.py:214
  40.6 1.7 %collective-permute-start.21 = (bf16[32,4096]{1,0:T(8,128)(2,1)S(1)}, bf16[32,4096]{1,0:T(8,128)(2,1)S(1)}, u32[]{:S(2)}, u32[]{:S(2)}) collective-permute-start(bf16[32,4096]{1,0:T(8,128)(2,1)S(1)} %copy-done.3), channel_id=1, source_target_pairs={{0,4},{4,8},{8,12},{12,14},{14,10},{10,6},{6,2},{2,0},{1,5},{5,9},... | collective-permute-start | bytes 786440 | tf_op jit(solution)/shard_map/ppermute | solution.py:214
  42.6 3.1 %collective-permute-done.11.rest_5_ = bf16[64,2048]{1,0:T(8,128)(2,1)S(1)} collective-permute-done((bf16[64,2048]{1,0:T(8,128)(2,1)}, bf16[64,2048]{1,0:T(8,128)(2,1)S(1)}, u32[]{:S(2)}, u32[]{:S(2)}) %collective-permute-start.11) | collective-permute-done | bytes 262176 | tf_op jit(solution)/shard_map/ppermute | solution.py:214
  46.1 1.6 %collective-permute-start.22 = (bf16[32,4096]{1,0:T(8,128)(2,1)S(1)}, bf16[32,4096]{1,0:T(8,128)(2,1)S(1)}, u32[]{:S(2)}, u32[]{:S(2)}) collective-permute-start(bf16[32,4096]{1,0:T(8,128)(2,1)S(1)} %copy-done.3), channel_id=1, source_target_pairs={{0,2},{4,0},{8,4},{12,8},{14,12},{10,14},{6,10},{2,6},{1,3},{5,1},... | collective-permute-start | bytes 786440 | tf_op jit(solution)/shard_map/ppermute | solution.py:214
  48.1 3.2 %collective-permute-done.21.rest_2_ = bf16[32,4096]{1,0:T(8,128)(2,1)S(1)} collective-permute-done((bf16[32,4096]{1,0:T(8,128)(2,1)S(1)}, bf16[32,4096]{1,0:T(8,128)(2,1)S(1)}, u32[]{:S(2)}, u32[]{:S(2)}) %collective-permute-start.21) | collective-permute-done | bytes 262176 | tf_op jit(solution)/shard_map/ppermute | solution.py:214
  51.3 1.5 %collective-permute-start.15 = (bf16[32,4096]{1,0:T(8,128)(2,1)}, bf16[32,4096]{1,0:T(8,128)(2,1)S(1)}, u32[]{:S(2)}, u32[]{:S(2)}) collective-permute-start(bf16[32,4096]{1,0:T(8,128)(2,1)} %collective-permute-done.14.rest_9_), channel_id=1, source_target_pairs={{0,16},{16,0},{1,17},{17,1},{2,18},{18,2},{3,19},{19,3},{4,20},{20... | collective-permute-start | bytes 786440 | tf_op jit(solution)/shard_map/ppermute | solution.py:258
  53.3 2.3 %collective-permute-done.22.rest_4_ = bf16[32,4096]{1,0:T(8,128)(2,1)S(1)} collective-permute-done((bf16[32,4096]{1,0:T(8,128)(2,1)S(1)}, bf16[32,4096]{1,0:T(8,128)(2,1)S(1)}, u32[]{:S(2)}, u32[]{:S(2)}) %collective-permute-start.22) | collective-permute-done | bytes 262176 | tf_op jit(solution)/shard_map/ppermute | solution.py:214
  55.6 1.6 %collective-permute-start.24 = (bf16[32,4096]{1,0:T(8,128)(2,1)S(1)}, bf16[32,4096]{1,0:T(8,128)(2,1)S(1)}, u32[]{:S(2)}, u32[]{:S(2)}) collective-permute-start(bf16[32,4096]{1,0:T(8,128)(2,1)S(1)} %collective-permute-done.21.rest_2_), channel_id=1, source_target_pairs={{0,4},{4,8},{8,12},{12,14},{14,10},{10,6},{6,2},{2,0},{1,5},{5,9},... | collective-permute-start | bytes 786440 | tf_op jit(solution)/shard_map/ppermute | solution.py:214
  57.7 2.8 %shard_map.97 = (f32[256,128]{1,0:T(8,128)S(1)}, f32[256,128]{1,0:T(8,128)S(1)}) custom-call(bf16[256,2176]{1,0:T(8,128)(2,1)S(1)} %shard_map.96.here.mine, bf16[256,2176]{1,0:T(8,128)(2,1)} %collective-permute-done.8.across, f32[1,512]{1,0:T(1,128)S(1)} %convert_element_type.41.ids, bf16[64,2048]{1,0:T(8,128)(2,1)S(1)} %dynamic-slice_bitcast_fusion.1.rest_0_, ...), custom_call_target="tpu_custom_call" | custom-call | flops 1 | bytes 1 | tf_op jit(solution)/shard_map/pallas_call | solution.py:262
  60.5 2.6 %collective-permute-done.17.rest_12_ = bf16[32,4096]{1,0:T(8,128)(2,1)S(1)} collective-permute-done((bf16[32,4096]{1,0:T(8,128)(2,1)}, bf16[32,4096]{1,0:T(8,128)(2,1)S(1)}, u32[]{:S(2)}, u32[]{:S(2)}) %collective-permute-start.17) | collective-permute-done | bytes 262176 | tf_op jit(solution)/shard_map/ppermute | solution.py:258
  63.1 1.6 %collective-permute-start.18 = (f32[256,128]{1,0:T(8,128)S(1)}, f32[256,128]{1,0:T(8,128)S(1)}, u32[]{:S(2)}, u32[]{:S(2)}) collective-permute-start(f32[256,128]{1,0:T(8,128)S(1)} %get-tuple-element.42), channel_id=1, source_target_pairs={{0,16},{16,0},{1,17},{17,1},{2,18},{18,2},{3,19},{19,3},{4,20},{20... | collective-permute-start | bytes 393224 | tf_op jit(solution)/shard_map/ppermute | solution.py:268
  65.1 2.9 %collective-permute-done.18.crossed = f32[256,128]{1,0:T(8,128)S(1)} collective-permute-done((f32[256,128]{1,0:T(8,128)S(1)}, f32[256,128]{1,0:T(8,128)S(1)}, u32[]{:S(2)}, u32[]{:S(2)}) %collective-permute-start.18) | collective-permute-done | bytes 131104 | tf_op jit(solution)/shard_map/ppermute | solution.py:268
  68.1 1.3 %collective-permute-done.20.beyond = f32[256,128]{1,0:T(8,128)S(1)} collective-permute-done((f32[256,128]{1,0:T(8,128)S(1)}, f32[256,128]{1,0:T(8,128)S(1)}, u32[]{:S(2)}, u32[]{:S(2)}) %collective-permute-start.20) | collective-permute-done | bytes 131104 | tf_op jit(solution)/shard_map/ppermute | solution.py:273
  69.4 1.7 %collective-permute-done.26.rest_14_ = bf16[32,4096]{1,0:T(8,128)(2,1)S(1)} collective-permute-done((bf16[32,4096]{1,0:T(8,128)(2,1)S(1)}, bf16[32,4096]{1,0:T(8,128)(2,1)S(1)}, u32[]{:S(2)}, u32[]{:S(2)}) %collective-permute-start.26) | collective-permute-done | bytes 262176 | tf_op jit(solution)/shard_map/ppermute | solution.py:271
  71.1 6.1 %shard_map.98 = (bf16[120,8192]{1,0:T(8,128)(2,1)}, bf16[120,4096]{1,0:T(8,128)(2,1)S(1)}, f32[1,128]{1,0:T(1,128)S(1)}, f32[1,128]{1,0:T(1,128)S(1)}) custom-call(s32[2]{0:T(128)S(1)} %pad_add_fusion.place, bf16[256,2176]{1,0:T(8,128)(2,1)S(1)} %shard_map.96.here.mine, bf16[256,2176]{1,0:T(8,128)(2,1)} %shard_map.95.theirs, ...), custom_call_target="tpu_custom_call" | custom-call | flops 1 | bytes 1 | tf_op jit(solution)/shard_map/pallas_call | solution.py:279
  77.7 2.1 %collective-permute-done.28 = f32[128]{0:T(128)S(1)} collective-permute-done((f32[128]{0:T(128)S(1)}, f32[128]{0:T(128)S(1)}, u32[]{:S(2)}, u32[]{:S(2)}) %collective-permute-start.28) | collective-permute-done | bytes 544 | tf_op jit(solution)/shard_map/ppermute | solution.py:308
  80.3 1.0 %constant_dynamic-update-slice_fusion = bf16[120,8192]{1,0:T(8,128)(2,1)} fusion(bf16[120,8192]{1,0:T(8,128)(2,1)} %get-tuple-element.50, bf16[120,4096]{1,0:T(8,128)(2,1)S(1)} %collective-permute-done.27, s32[]{:T(128)S(6)} %select_n.21), kind=kLoop, calls=%fused_computation.6 | loop fusion | bytes 1966084 | tf_op jit(solution)/shard_map/dynamic_update_slice | solution.py:309
  (59 shorter events, 9.5 us)
Async XLA Ops:
  0.6 10.5 %copy-start.1 = (bf16[120,8192]{1,0:T(8,128)(2,1)S(1)}, bf16[120,8192]{1,0:T(8,128)(2,1)}, u32[]{:S(2)}) copy-start(bf16[120,8192]{1,0:T(8,128)(2,1)} %hidden.3) | copy-start | bytes 5898244
  0.7 10.4 %copy-start.4 = (bf16[4096]{0:T(1024)(128)(2,1)S(1)}, bf16[4096]{0:T(1024)(128)(2,1)}, u32[]{:S(2)}) copy-start(bf16[4096]{0:T(1024)(128)(2,1)} %param.13) | copy-start | bytes 24580
  0.7 10.5 %collective-permute-start = (bf16[120,8192]{1,0:T(8,128)(2,1)}, bf16[120,8192]{1,0:T(8,128)(2,1)}, u32[]{:S(2)}, u32[]{:S(2)}) collective-permute-start(bf16[120,8192]{1,0:T(8,128)(2,1)} %hidden.3), channel_id=1, source_target_pairs={{0,1},{1,0},{2,3},{3,2},{4,5},{5,4},{6,7},{7,6},{8,9},{9,8},{10,11... | collective-permute-start | bytes 5898248 | tf_op jit(solution)/shard_map/ppermute | solution.py:219
  1.7 12.4 %collective-permute-start.7 = (bf16[64,2048]{1,0:T(8,128)(2,1)S(1)}, bf16[64,2048]{1,0:T(8,128)(2,1)}, u32[]{:S(2)}, u32[]{:S(2)}) collective-permute-start(bf16[64,2048]{1,0:T(8,128)(2,1)S(1)} %dynamic-slice_bitcast_fusion.1.rest_0_), channel_id=1, source_target_pairs={{0,2},{4,0},{8,4},{12,8},{14,12},{10,14},{6,10},{2,6},{1,3},{5,1},... | collective-permute-start | bytes 786440 | tf_op jit(solution)/shard_map/ppermute | solution.py:214
  4.7 9.4 %collective-permute-start.6 = (bf16[64,2048]{1,0:T(8,128)(2,1)S(1)}, bf16[64,2048]{1,0:T(8,128)(2,1)}, u32[]{:S(2)}, u32[]{:S(2)}) collective-permute-start(bf16[64,2048]{1,0:T(8,128)(2,1)S(1)} %dynamic-slice_bitcast_fusion.1.rest_0_), channel_id=1, source_target_pairs={{0,4},{4,8},{8,12},{12,14},{14,10},{10,6},{6,2},{2,0},{1,5},{5,9},... | collective-permute-start | bytes 786440 | tf_op jit(solution)/shard_map/ppermute | solution.py:214
  7.8 2.8 %collective-permute-start.1 = (f32[128,2]{1,0:T(8,128)S(1)}, f32[128,2]{1,0:T(8,128)S(1)}, u32[]{:S(2)}, u32[]{:S(2)}) collective-permute-start(f32[128,2]{1,0:T(8,128)S(1)} %concatenate.7.own_small), channel_id=1, source_target_pairs={{0,1},{1,0},{2,3},{3,2},{4,5},{5,4},{6,7},{7,6},{8,9},{9,8},{10,11... | collective-permute-start | bytes 3080 | tf_op jit(solution)/shard_map/ppermute | solution.py:224
  8.7 9.2 %collective-permute-start.3 = (bf16[32,4096]{1,0:T(8,128)(2,1)}, bf16[32,4096]{1,0:T(8,128)(2,1)}, u32[]{:S(2)}, u32[]{:S(2)}) collective-permute-start(bf16[32,4096]{1,0:T(8,128)(2,1)} %get-tuple-element.55), channel_id=1, source_target_pairs={{0,2},{4,0},{8,4},{12,8},{14,12},{10,14},{6,10},{2,6},{1,3},{5,1},... | collective-permute-start | bytes 786440 | tf_op jit(solution)/shard_map/ppermute | solution.py:214
  10.6 8.7 %collective-permute-start.2 = (bf16[32,4096]{1,0:T(8,128)(2,1)}, bf16[32,4096]{1,0:T(8,128)(2,1)}, u32[]{:S(2)}, u32[]{:S(2)}) collective-permute-start(bf16[32,4096]{1,0:T(8,128)(2,1)} %get-tuple-element.55), channel_id=1, source_target_pairs={{0,4},{4,8},{8,12},{12,14},{14,10},{10,6},{6,2},{2,0},{1,5},{5,9},... | collective-permute-start | bytes 786440 | tf_op jit(solution)/shard_map/ppermute | solution.py:214
  11.2 21.0 %copy-start.5 = (bf16[4096]{0:T(1024)(128)(2,1)S(1)}, bf16[4096]{0:T(1024)(128)(2,1)}, u32[]{:S(2)}) copy-start(bf16[4096]{0:T(1024)(128)(2,1)} %param.14) | copy-start | bytes 24580
  14.1 43.6 %collective-permute-start.8 = (bf16[256,2176]{1,0:T(8,128)(2,1)}, bf16[256,2176]{1,0:T(8,128)(2,1)}, u32[]{:S(2)}, u32[]{:S(2)}) collective-permute-start(bf16[256,2176]{1,0:T(8,128)(2,1)} %shard_map.95.theirs), channel_id=1, source_target_pairs={{0,16},{16,0},{1,17},{17,1},{2,18},{18,2},{3,19},{19,3},{4,20},{20... | collective-permute-start | bytes 3342344 | tf_op jit(solution)/shard_map/ppermute | solution.py:250
  19.3 9.6 %collective-permute-start.4 = (bf16[32,4096]{1,0:T(8,128)(2,1)}, bf16[32,4096]{1,0:T(8,128)(2,1)}, u32[]{:S(2)}, u32[]{:S(2)}) collective-permute-start(bf16[32,4096]{1,0:T(8,128)(2,1)} %collective-permute-done.2.rest_1_), channel_id=1, source_target_pairs={{0,4},{4,8},{8,12},{12,14},{14,10},{10,6},{6,2},{2,0},{1,5},{5,9},... | collective-permute-start | bytes 786440 | tf_op jit(solution)/shard_map/ppermute | solution.py:214
  19.8 9.6 %collective-permute-start.5 = (bf16[32,4096]{1,0:T(8,128)(2,1)}, bf16[32,4096]{1,0:T(8,128)(2,1)}, u32[]{:S(2)}, u32[]{:S(2)}) collective-permute-start(bf16[32,4096]{1,0:T(8,128)(2,1)} %collective-permute-done.3.rest_3_), channel_id=1, source_target_pairs={{0,2},{4,0},{8,4},{12,8},{14,12},{10,14},{6,10},{2,6},{1,3},{5,1},... | collective-permute-start | bytes 786440 | tf_op jit(solution)/shard_map/ppermute | solution.py:214
  21.4 13.1 %collective-permute-start.9 = (bf16[64,2048]{1,0:T(8,128)(2,1)}, bf16[64,2048]{1,0:T(8,128)(2,1)}, u32[]{:S(2)}, u32[]{:S(2)}) collective-permute-start(bf16[64,2048]{1,0:T(8,128)(2,1)} %collective-permute-done.6.rest_1_), channel_id=1, source_target_pairs={{0,4},{4,8},{8,12},{12,14},{14,10},{10,6},{6,2},{2,0},{1,5},{5,9},... | collective-permute-start | bytes 786440 | tf_op jit(solution)/shard_map/ppermute | solution.py:214
  21.8 13.2 %collective-permute-start.10 = (bf16[64,2048]{1,0:T(8,128)(2,1)}, bf16[64,2048]{1,0:T(8,128)(2,1)}, u32[]{:S(2)}, u32[]{:S(2)}) collective-permute-start(bf16[64,2048]{1,0:T(8,128)(2,1)} %collective-permute-done.7.rest_2_), channel_id=1, source_target_pairs={{0,2},{4,0},{8,4},{12,8},{14,12},{10,14},{6,10},{2,6},{1,3},{5,1},... | collective-permute-start | bytes 786440 | tf_op jit(solution)/shard_map/ppermute | solution.py:214
  29.3 10.8 %collective-permute-start.14 = (bf16[32,4096]{1,0:T(8,128)(2,1)}, bf16[32,4096]{1,0:T(8,128)(2,1)}, u32[]{:S(2)}, u32[]{:S(2)}) collective-permute-start(bf16[32,4096]{1,0:T(8,128)(2,1)} %collective-permute-done.4.rest_5_), channel_id=1, source_target_pairs={{0,4},{4,8},{8,12},{12,14},{14,10},{10,6},{6,2},{2,0},{1,5},{5,9},... | collective-permute-start | bytes 786440 | tf_op jit(solution)/shard_map/ppermute | solution.py:214
  31.0 9.5 %collective-permute-start.16 = (bf16[32,4096]{1,0:T(8,128)(2,1)}, bf16[32,4096]{1,0:T(8,128)(2,1)}, u32[]{:S(2)}, u32[]{:S(2)}) collective-permute-start(bf16[32,4096]{1,0:T(8,128)(2,1)} %collective-permute-done.5.rest_7_), channel_id=1, source_target_pairs={{0,2},{4,0},{8,4},{12,8},{14,12},{10,14},{6,10},{2,6},{1,3},{5,1},... | collective-permute-start | bytes 786440 | tf_op jit(solution)/shard_map/ppermute | solution.py:214
  34.9 10.7 %collective-permute-start.11 = (bf16[64,2048]{1,0:T(8,128)(2,1)}, bf16[64,2048]{1,0:T(8,128)(2,1)S(1)}, u32[]{:S(2)}, u32[]{:S(2)}) collective-permute-start(bf16[64,2048]{1,0:T(8,128)(2,1)} %collective-permute-done.9.rest_3_), channel_id=1, source_target_pairs={{0,4},{4,8},{8,12},{12,14},{14,10},{10,6},{6,2},{2,0},{1,5},{5,9},... | collective-permute-start | bytes 786440 | tf_op jit(solution)/shard_map/ppermute | solution.py:214
  36.6 9.4 %collective-permute-start.12 = (bf16[64,2048]{1,0:T(8,128)(2,1)}, bf16[64,2048]{1,0:T(8,128)(2,1)S(1)}, u32[]{:S(2)}, u32[]{:S(2)}) collective-permute-start(bf16[64,2048]{1,0:T(8,128)(2,1)} %collective-permute-done.10.rest_4_), channel_id=1, source_target_pairs={{0,2},{4,0},{8,4},{12,8},{14,12},{10,14},{6,10},{2,6},{1,3},{5,1},... | collective-permute-start | bytes 786440 | tf_op jit(solution)/shard_map/ppermute | solution.py:214
  40.6 10.7 %collective-permute-start.21 = (bf16[32,4096]{1,0:T(8,128)(2,1)S(1)}, bf16[32,4096]{1,0:T(8,128)(2,1)S(1)}, u32[]{:S(2)}, u32[]{:S(2)}) collective-permute-start(bf16[32,4096]{1,0:T(8,128)(2,1)S(1)} %copy-done.3), channel_id=1, source_target_pairs={{0,4},{4,8},{8,12},{12,14},{14,10},{10,6},{6,2},{2,0},{1,5},{5,9},... | collective-permute-start | bytes 786440 | tf_op jit(solution)/shard_map/ppermute | solution.py:214
  42.3 10.5 %collective-permute-start.23 = (bf16[32,4096]{1,0:T(8,128)(2,1)}, bf16[32,4096]{1,0:T(8,128)(2,1)S(1)}, u32[]{:S(2)}, u32[]{:S(2)}) collective-permute-start(bf16[32,4096]{1,0:T(8,128)(2,1)} %collective-permute-done.16.rest_11_), channel_id=1, source_target_pairs={{0,2},{4,0},{8,4},{12,8},{14,12},{10,14},{6,10},{2,6},{1,3},{5,1},... | collective-permute-start | bytes 786440 | tf_op jit(solution)/shard_map/ppermute | solution.py:214
  46.1 9.6 %collective-permute-start.22 = (bf16[32,4096]{1,0:T(8,128)(2,1)S(1)}, bf16[32,4096]{1,0:T(8,128)(2,1)S(1)}, u32[]{:S(2)}, u32[]{:S(2)}) collective-permute-start(bf16[32,4096]{1,0:T(8,128)(2,1)S(1)} %copy-done.3), channel_id=1, source_target_pairs={{0,2},{4,0},{8,4},{12,8},{14,12},{10,14},{6,10},{2,6},{1,3},{5,1},... | collective-permute-start | bytes 786440 | tf_op jit(solution)/shard_map/ppermute | solution.py:214
  47.7 9.5 %collective-permute-start.13 = (bf16[64,2048]{1,0:T(8,128)(2,1)S(1)}, bf16[64,2048]{1,0:T(8,128)(2,1)S(1)}, u32[]{:S(2)}, u32[]{:S(2)}) collective-permute-start(bf16[64,2048]{1,0:T(8,128)(2,1)S(1)} %collective-permute-done.11.rest_5_), channel_id=1, source_target_pairs={{0,4},{4,8},{8,12},{12,14},{14,10},{10,6},{6,2},{2,0},{1,5},{5,9},... | collective-permute-start | bytes 786440 | tf_op jit(solution)/shard_map/ppermute | solution.py:214
  51.3 9.2 %collective-permute-start.15 = (bf16[32,4096]{1,0:T(8,128)(2,1)}, bf16[32,4096]{1,0:T(8,128)(2,1)S(1)}, u32[]{:S(2)}, u32[]{:S(2)}) collective-permute-start(bf16[32,4096]{1,0:T(8,128)(2,1)} %collective-permute-done.14.rest_9_), channel_id=1, source_target_pairs={{0,16},{16,0},{1,17},{17,1},{2,18},{18,2},{3,19},{19,3},{4,20},{20... | collective-permute-start | bytes 786440 | tf_op jit(solution)/shard_map/ppermute | solution.py:258
  52.8 10.3 %collective-permute-start.17 = (bf16[32,4096]{1,0:T(8,128)(2,1)}, bf16[32,4096]{1,0:T(8,128)(2,1)S(1)}, u32[]{:S(2)}, u32[]{:S(2)}) collective-permute-start(bf16[32,4096]{1,0:T(8,128)(2,1)} %collective-permute-done.16.rest_11_), channel_id=1, source_target_pairs={{0,16},{16,0},{1,17},{17,1},{2,18},{18,2},{3,19},{19,3},{4,20},{20... | collective-permute-start | bytes 786440 | tf_op jit(solution)/shard_map/ppermute | solution.py:258
  55.6 12.4 %collective-permute-start.24 = (bf16[32,4096]{1,0:T(8,128)(2,1)S(1)}, bf16[32,4096]{1,0:T(8,128)(2,1)S(1)}, u32[]{:S(2)}, u32[]{:S(2)}) collective-permute-start(bf16[32,4096]{1,0:T(8,128)(2,1)S(1)} %collective-permute-done.21.rest_2_), channel_id=1, source_target_pairs={{0,4},{4,8},{8,12},{12,14},{14,10},{10,6},{6,2},{2,0},{1,5},{5,9},... | collective-permute-start | bytes 786440 | tf_op jit(solution)/shard_map/ppermute | solution.py:214
  57.2 10.9 %collective-permute-start.25 = (bf16[32,4096]{1,0:T(8,128)(2,1)S(1)}, bf16[32,4096]{1,0:T(8,128)(2,1)S(1)}, u32[]{:S(2)}, u32[]{:S(2)}) collective-permute-start(bf16[32,4096]{1,0:T(8,128)(2,1)S(1)} %collective-permute-done.22.rest_4_), channel_id=1, source_target_pairs={{0,2},{4,0},{8,4},{12,8},{14,12},{10,14},{6,10},{2,6},{1,3},{5,1},... | collective-permute-start | bytes 786440 | tf_op jit(solution)/shard_map/ppermute | solution.py:214
  63.1 5.0 %collective-permute-start.18 = (f32[256,128]{1,0:T(8,128)S(1)}, f32[256,128]{1,0:T(8,128)S(1)}, u32[]{:S(2)}, u32[]{:S(2)}) collective-permute-start(f32[256,128]{1,0:T(8,128)S(1)} %get-tuple-element.42), channel_id=1, source_target_pairs={{0,16},{16,0},{1,17},{17,1},{2,18},{18,2},{3,19},{19,3},{4,20},{20... | collective-permute-start | bytes 393224 | tf_op jit(solution)/shard_map/ppermute | solution.py:268
  64.7 6.4 %collective-permute-start.26 = (bf16[32,4096]{1,0:T(8,128)(2,1)S(1)}, bf16[32,4096]{1,0:T(8,128)(2,1)S(1)}, u32[]{:S(2)}, u32[]{:S(2)}) collective-permute-start(bf16[32,4096]{1,0:T(8,128)(2,1)S(1)} %collective-permute-done.23.rest_13_), channel_id=1, source_target_pairs={{0,16},{16,0},{1,17},{17,1},{2,18},{18,2},{3,19},{19,3},{4,20},{20... | collective-permute-start | bytes 786440 | tf_op jit(solution)/shard_map/ppermute | solution.py:271
  65.1 3.0 %collective-permute-start.19 = (f32[256,128]{1,0:T(8,128)S(1)}, f32[256,128]{1,0:T(8,128)S(1)}, u32[]{:S(2)}, u32[]{:S(2)}) collective-permute-start(f32[256,128]{1,0:T(8,128)S(1)} %get-tuple-element.38.here), channel_id=1, source_target_pairs={{0,1},{1,0},{2,3},{3,2},{4,5},{5,4},{6,7},{7,6},{8,9},{9,8},{10,11... | collective-permute-start | bytes 393224 | tf_op jit(solution)/shard_map/ppermute | solution.py:272
  68.1 1.3 %collective-permute-start.20 = (f32[256,128]{1,0:T(8,128)S(1)}, f32[256,128]{1,0:T(8,128)S(1)}, u32[]{:S(2)}, u32[]{:S(2)}) collective-permute-start(f32[256,128]{1,0:T(8,128)S(1)} %collective-permute-done.18.crossed), channel_id=1, source_target_pairs={{0,1},{1,0},{2,3},{3,2},{4,5},{5,4},{6,7},{7,6},{8,9},{9,8},{10,11... | collective-permute-start | bytes 393224 | tf_op jit(solution)/shard_map/ppermute | solution.py:273
  77.2 3.1 %collective-permute-start.27 = (bf16[120,4096]{1,0:T(8,128)(2,1)S(1)}, bf16[120,4096]{1,0:T(8,128)(2,1)S(1)}, u32[]{:S(2)}, u32[]{:S(2)}) collective-permute-start(bf16[120,4096]{1,0:T(8,128)(2,1)S(1)} %get-tuple-element.51), channel_id=1, source_target_pairs={{0,1},{1,0},{2,3},{3,2},{4,5},{5,4},{6,7},{7,6},{8,9},{9,8},{10,11... | collective-permute-start | bytes 2949128 | tf_op jit(solution)/shard_map/ppermute | solution.py:307
  77.2 2.6 %collective-permute-start.28 = (f32[128]{0:T(128)S(1)}, f32[128]{0:T(128)S(1)}, u32[]{:S(2)}, u32[]{:S(2)}) collective-permute-start(f32[128]{0:T(128)S(1)} %bitcast.23), channel_id=1, source_target_pairs={{0,1},{1,0},{2,3},{3,2},{4,5},{5,4},{6,7},{7,6},{8,9},{9,8},{10,11... | collective-permute-start | bytes 1544 | tf_op jit(solution)/shard_map/ppermute | solution.py:308
  (3 other events, 16.6 us)

commit v4 on v3

--- a/solution.py
+++ b/solution.py
@@ -181,7 +181,7 @@
     whole = lambda shape: pl.BlockSpec(shape, lambda i, p: (0,) * len(shape))
     bf = lambda *shape: jax.ShapeDtypeStruct(shape, jnp.bfloat16)
     fl = lambda *shape: jax.ShapeDtypeStruct(shape, jnp.float32)
-    tile = 1024
+    tile = 2048
     each = quarter // tile
     column = lambda n: pl.BlockSpec((n, tile), lambda i, p: (0, i))
     half_column = pl.BlockSpec((rows, tile), lambda i, p: (0, p[0] * (half // tile) + i))
@@ -252,23 +252,22 @@
     mine = normed(gain, lambda y: y)
 
     last_down = max(k for way in (1, -1) for k, (c, _) in enumerate(slots[way]) if c == 0)
-    for k in range(3, last_down + 3):
+    across_far = {}
+    for k in range(3, last_down + 1):
         send_slot(k, *([mine] if k == 5 else []))
-    across_far = {
-        (d, w): lax.ppermute(held[1, d, w if d < far else -1], "groups", swap)
-        for d, w in hops
-        if near < d < far
-    }
+    for d, w in hops:
+        if near < d < far:
+            across_far[d, w] = lax.ppermute(held[1, d, w], "groups", swap)
+    for k in range(last_down + 1, max(len(slots[1]), len(slots[-1]))):
+        send_slot(k, *across_far.values())
     here, there = pl.pallas_call(
         codes_kernel,
         out_shape=[fl(2 * full, 128), fl(2 * full, 128)],
         compiler_params=params,
         cost_estimate=cost,
     )(mine, across, ids, down_own, *[held[0, d, w] for d, w in hops])
-    crossed = lax.ppermute(after(there, *across_far.values()), "groups", swap)
-    for k in range(last_down + 3, max(len(slots[1]), len(slots[-1]))):
-        send_slot(k, there)
-    across_far[far, 1] = lax.ppermute(after(held[1, far, -1], there), "groups", swap)
+    across_far[far, 1] = lax.ppermute(held[1, far, -1], "groups", swap)
+    crossed = lax.ppermute(after(there, across_far[far, 1]), "groups", swap)
     beside = lax.ppermute(here, "fsdp", swap)
     beyond = lax.ppermute(crossed, "fsdp", swap)
 

time: 81.7 us -> 78.4 us (0.960)
  waiting for transfers between devices: 33.6 us -> 26.8 us
  starting transfers between devices: 26.4 us -> 30.7 us
    ppermute x18, waiting for transfers between devices: 22.9 us -> 19.5 us  [send_slot(): held[chain, distance, way] = lax.ppermute(piece, 'adapter', perms[way])]
    ppermute x4, waiting for transfers between devices: 7.24 us -> 3.97 us  [the longest x1 3.57 us: gathered_matrices(): crossed = lax.ppermute(after(there, across_far[far, 1]), 'groups', swap)]
    ppermute x4, starting transfers between devices: 4.08 us -> 6.26 us  [the longest x2 3.28 us: gathered_matrices(): across_far[d, w] = lax.ppermute(held[1, d, w], 'groups', swap)]
    ppermute x18, starting transfers between devices: 19.7 us -> 21.8 us  [send_slot(): held[chain, distance, way] = lax.ppermute(piece, 'adapter', perms[way])]
  transfers between devices with their start and end apart: 29 -> 29, of which waited for: 17 -> 15; matrix products, arithmetic and copies ran while one was open for 6% -> 7% of each run, Pallas kernels for 9% -> 10%
where the time goes in v4:
time: 78.4 us; the launch traced here: 78.1 us
  starting transfers between devices  30.7 us (39%)
  waiting for transfers between devices  26.8 us (34%)
  Pallas kernels  13 us (17%)
  other arithmetic  4.08 us (5%)
  local copies, waits for them, and re-layouts  2.69 us (3%)
  between operations  0.8 us (1%)
    ppermute x18, starting transfers between devices, send_slot(): held[chain, distance, way] = lax.ppermute(piece, 'adapter', perms[way])  21.8 us
    ppermute x18, waiting for transfers between devices, send_slot(): held[chain, distance, way] = lax.ppermute(piece, 'adapter', perms[way])  19.5 us
    pallas_call x1, Pallas kernels, gathered_matrices(): pl.pallas_call(delta_kernel, grid_spec=pltpu.PrefetchScalarGridSpec(num_s...  5.32 us
    pallas_call x2, Pallas kernels, normed(): pl.pallas_call(norm_kernel, grid_spec=pltpu.PrefetchScalarGridSpec(num_sc...  4.82 us
    ppermute x1, waiting for transfers between devices, gathered_matrices(): crossed = lax.ppermute(after(there, across_far[far, 1]), 'groups', swap)  3.57 us
    ppermute x2, starting transfers between devices, gathered_matrices(): across_far[d, w] = lax.ppermute(held[1, d, w], 'groups', swap)  3.28 us
    pallas_call x1, Pallas kernels, gathered_matrices(): pl.pallas_call(codes_kernel, out_shape=[fl(2 * full, 128), fl(2 * full, 1...  2.81 us
    ppermute x1, waiting for transfers between devices, gathered_matrices(): part_back = lax.ppermute(other_part.reshape(-1), 'fsdp', swap)  2.06 us
  transfers between devices with their start and end apart: 29, of which 15 were waited for; matrix products, arithmetic and copies ran while one was open for 7% of the time, Pallas kernels for 10%

profile of v4, /device:TPU:0, one launch (start us, length us, event | category | flops | bytes accessed | tf_op | source)
XLA Modules:
  0.0 78.1 jit_solution(15278265656140120688)
XLA Ops:
  1.7 3.0 %collective-permute-start.7 = (bf16[64,2048]{1,0:T(8,128)(2,1)S(1)}, bf16[64,2048]{1,0:T(8,128)(2,1)}, u32[]{:S(2)}, u32[]{:S(2)}) collective-permute-start(bf16[64,2048]{1,0:T(8,128)(2,1)S(1)} %dynamic-slice_bitcast_fusion.1.rest_0_), channel_id=1, source_target_pairs={{0,2},{4,0},{8,4},{12,8},{14,12},{10,14},{6,10},{2,6},{1,3},{5,1},... | collective-permute-start | bytes 786440 | tf_op jit(solution)/shard_map/ppermute | solution.py:214
  5.6 2.0 %multiply_reduce_fusion = f32[120]{0:T(128)S(1)} fusion(bf16[120,8192]{1,0:T(8,128)(2,1)} %hidden.3), kind=kLoop, calls=%fused_computation | loop fusion | flops 2949000 | bytes 1966560 | tf_op jit(solution)/shard_map/reduce_sum | solution.py:221
  8.7 1.9 %collective-permute-start.3 = (bf16[32,4096]{1,0:T(8,128)(2,1)}, bf16[32,4096]{1,0:T(8,128)(2,1)}, u32[]{:S(2)}, u32[]{:S(2)}) collective-permute-start(bf16[32,4096]{1,0:T(8,128)(2,1)} %get-tuple-element.53), channel_id=1, source_target_pairs={{0,2},{4,0},{8,4},{12,8},{14,12},{10,14},{6,10},{2,6},{1,3},{5,1},... | collective-permute-start | bytes 786440 | tf_op jit(solution)/shard_map/ppermute | solution.py:214
  11.2 2.9 %shard_map.95.theirs = bf16[256,2176]{1,0:T(8,128)(2,1)} custom-call(s32[2]{0:T(128)S(1)} %pad_add_fusion.place, bf16[120,8192]{1,0:T(8,128)(2,1)S(1)} %copy-done.1, bf16[120,8192]{1,0:T(8,128)(2,1)} %collective-permute-done.other, f32[128,2]{1,0:T(8,128)S(1)} %concatenate.7.own_small, f32[128,2]{1,0:T(8,128)S(1)} %collective-permute-done.1.other_small, ...), custom_call_target="tpu_custom_call" | custom-call | flops 1 | bytes 1 | tf_op jit(solution)/shard_map/pallas_call | solution.py:230
  14.1 1.6 %collective-permute-start.8 = (bf16[256,2176]{1,0:T(8,128)(2,1)}, bf16[256,2176]{1,0:T(8,128)(2,1)}, u32[]{:S(2)}, u32[]{:S(2)}) collective-permute-start(bf16[256,2176]{1,0:T(8,128)(2,1)} %shard_map.95.theirs), channel_id=1, source_target_pairs={{0,16},{16,0},{1,17},{17,1},{2,18},{18,2},{3,19},{19,3},{4,20},{20... | collective-permute-start | bytes 3342344 | tf_op jit(solution)/shard_map/ppermute | solution.py:250
  15.7 2.3 %collective-permute-done.3.rest_3_ = bf16[32,4096]{1,0:T(8,128)(2,1)} collective-permute-done((bf16[32,4096]{1,0:T(8,128)(2,1)}, bf16[32,4096]{1,0:T(8,128)(2,1)}, u32[]{:S(2)}, u32[]{:S(2)}) %collective-permute-start.3) | collective-permute-done | bytes 262176 | tf_op jit(solution)/shard_map/ppermute | solution.py:214
  18.0 1.4 %collective-permute-done.2.rest_1_ = bf16[32,4096]{1,0:T(8,128)(2,1)} collective-permute-done((bf16[32,4096]{1,0:T(8,128)(2,1)}, bf16[32,4096]{1,0:T(8,128)(2,1)}, u32[]{:S(2)}, u32[]{:S(2)}) %collective-permute-start.2) | collective-permute-done | bytes 262176 | tf_op jit(solution)/shard_map/ppermute | solution.py:214
  19.8 1.6 %collective-permute-start.5 = (bf16[32,4096]{1,0:T(8,128)(2,1)}, bf16[32,4096]{1,0:T(8,128)(2,1)}, u32[]{:S(2)}, u32[]{:S(2)}) collective-permute-start(bf16[32,4096]{1,0:T(8,128)(2,1)} %collective-permute-done.3.rest_3_), channel_id=1, source_target_pairs={{0,2},{4,0},{8,4},{12,8},{14,12},{10,14},{6,10},{2,6},{1,3},{5,1},... | collective-permute-start | bytes 786440 | tf_op jit(solution)/shard_map/ppermute | solution.py:214
  21.8 1.6 %collective-permute-start.10 = (bf16[64,2048]{1,0:T(8,128)(2,1)}, bf16[64,2048]{1,0:T(8,128)(2,1)}, u32[]{:S(2)}, u32[]{:S(2)}) collective-permute-start(bf16[64,2048]{1,0:T(8,128)(2,1)} %collective-permute-done.7.rest_2_), channel_id=1, source_target_pairs={{0,2},{4,0},{8,4},{12,8},{14,12},{10,14},{6,10},{2,6},{1,3},{5,1},... | collective-permute-start | bytes 786440 | tf_op jit(solution)/shard_map/ppermute | solution.py:214
  24.3 4.6 %collective-permute-done.4.rest_5_ = bf16[32,4096]{1,0:T(8,128)(2,1)} collective-permute-done((bf16[32,4096]{1,0:T(8,128)(2,1)}, bf16[32,4096]{1,0:T(8,128)(2,1)}, u32[]{:S(2)}, u32[]{:S(2)}) %collective-permute-start.4) | collective-permute-done | bytes 262176 | tf_op jit(solution)/shard_map/ppermute | solution.py:214
  29.3 1.6 %collective-permute-start.14 = (bf16[32,4096]{1,0:T(8,128)(2,1)}, bf16[32,4096]{1,0:T(8,128)(2,1)S(1)}, u32[]{:S(2)}, u32[]{:S(2)}) collective-permute-start(bf16[32,4096]{1,0:T(8,128)(2,1)} %collective-permute-done.5.rest_7_), channel_id=1, source_target_pairs={{0,2},{4,0},{8,4},{12,8},{14,12},{10,14},{6,10},{2,6},{1,3},{5,1},... | collective-permute-start | bytes 786440 | tf_op jit(solution)/shard_map/ppermute | solution.py:214
  31.3 1.9 %shard_map.96.here.mine = bf16[256,2176]{1,0:T(8,128)(2,1)S(1)} custom-call(s32[2]{0:T(128)S(1)} %pad_add_fusion.place, bf16[120,8192]{1,0:T(8,128)(2,1)S(1)} %copy-done.1, bf16[120,8192]{1,0:T(8,128)(2,1)} %collective-permute-done.other, f32[128,2]{1,0:T(8,128)S(1)} %concatenate.7.own_small, f32[128,2]{1,0:T(8,128)S(1)} %collective-permute-done.1.other_small, ...), custom_call_target="tpu_custom_call" | custom-call | flops 1 | bytes 1 | tf_op jit(solution)/shard_map/pallas_call | solution.py:230
  33.3 1.3 %collective-permute-done.9.rest_3_ = bf16[64,2048]{1,0:T(8,128)(2,1)} collective-permute-done((bf16[64,2048]{1,0:T(8,128)(2,1)}, bf16[64,2048]{1,0:T(8,128)(2,1)}, u32[]{:S(2)}, u32[]{:S(2)}) %collective-permute-start.9) | collective-permute-done | bytes 262176 | tf_op jit(solution)/shard_map/ppermute | solution.py:214
  34.9 1.7 %collective-permute-start.11 = (bf16[64,2048]{1,0:T(8,128)(2,1)}, bf16[64,2048]{1,0:T(8,128)(2,1)S(1)}, u32[]{:S(2)}, u32[]{:S(2)}) collective-permute-start(bf16[64,2048]{1,0:T(8,128)(2,1)} %collective-permute-done.9.rest_3_), channel_id=1, source_target_pairs={{0,4},{4,8},{8,12},{12,14},{14,10},{10,6},{6,2},{2,0},{1,5},{5,9},... | collective-permute-start | bytes 786440 | tf_op jit(solution)/shard_map/ppermute | solution.py:214
  37.0 3.5 %collective-permute-done.14.rest_11_ = bf16[32,4096]{1,0:T(8,128)(2,1)S(1)} collective-permute-done((bf16[32,4096]{1,0:T(8,128)(2,1)}, bf16[32,4096]{1,0:T(8,128)(2,1)S(1)}, u32[]{:S(2)}, u32[]{:S(2)}) %collective-permute-start.14) | collective-permute-done | bytes 262176 | tf_op jit(solution)/shard_map/ppermute | solution.py:214
  40.4 1.6 %collective-permute-start.24 = (bf16[32,4096]{1,0:T(8,128)(2,1)S(1)}, bf16[32,4096]{1,0:T(8,128)(2,1)S(1)}, u32[]{:S(2)}, u32[]{:S(2)}) collective-permute-start(bf16[32,4096]{1,0:T(8,128)(2,1)S(1)} %collective-permute-done.14.rest_11_), channel_id=1, source_target_pairs={{0,16},{16,0},{1,17},{17,1},{2,18},{18,2},{3,19},{19,3},{4,20},{20... | collective-permute-start | bytes 786440 | tf_op jit(solution)/shard_map/ppermute | solution.py:260
  42.1 1.5 %collective-permute-start.16 = (bf16[32,4096]{1,0:T(8,128)(2,1)S(1)}, bf16[32,4096]{1,0:T(8,128)(2,1)S(1)}, u32[]{:S(2)}, u32[]{:S(2)}) collective-permute-start(bf16[32,4096]{1,0:T(8,128)(2,1)S(1)} %collective-permute-done.14.rest_11_), channel_id=1, source_target_pairs={{0,2},{4,0},{8,4},{12,8},{14,12},{10,14},{6,10},{2,6},{1,3},{5,1},... | collective-permute-start | bytes 786440 | tf_op jit(solution)/shard_map/ppermute | solution.py:214
  44.7 1.4 %collective-permute-done.12.rest_6_ = bf16[64,2048]{1,0:T(8,128)(2,1)S(1)} collective-permute-done((bf16[64,2048]{1,0:T(8,128)(2,1)}, bf16[64,2048]{1,0:T(8,128)(2,1)S(1)}, u32[]{:S(2)}, u32[]{:S(2)}) %collective-permute-start.12) | collective-permute-done | bytes 262176 | tf_op jit(solution)/shard_map/ppermute | solution.py:214
  46.1 1.6 %collective-permute-start.23 = (bf16[32,4096]{1,0:T(8,128)(2,1)S(1)}, bf16[32,4096]{1,0:T(8,128)(2,1)S(1)}, u32[]{:S(2)}, u32[]{:S(2)}) collective-permute-start(bf16[32,4096]{1,0:T(8,128)(2,1)S(1)} %collective-permute-done.15.rest_9_), channel_id=1, source_target_pairs={{0,16},{16,0},{1,17},{17,1},{2,18},{18,2},{3,19},{19,3},{4,20},{20... | collective-permute-start | bytes 786440 | tf_op jit(solution)/shard_map/ppermute | solution.py:260
  48.1 2.3 %collective-permute-start.22 = (bf16[32,4096]{1,0:T(8,128)(2,1)S(1)}, bf16[32,4096]{1,0:T(8,128)(2,1)S(1)}, u32[]{:S(2)}, u32[]{:S(2)}) collective-permute-start(bf16[32,4096]{1,0:T(8,128)(2,1)S(1)} %copy-done.3), channel_id=1, source_target_pairs={{0,2},{4,0},{8,4},{12,8},{14,12},{10,14},{6,10},{2,6},{1,3},{5,1},... | collective-permute-start | bytes 786440 | tf_op jit(solution)/shard_map/ppermute | solution.py:214
  50.4 1.3 %collective-permute-done.16.rest_13_ = bf16[32,4096]{1,0:T(8,128)(2,1)S(1)} collective-permute-done((bf16[32,4096]{1,0:T(8,128)(2,1)S(1)}, bf16[32,4096]{1,0:T(8,128)(2,1)S(1)}, u32[]{:S(2)}, u32[]{:S(2)}) %collective-permute-start.16) | collective-permute-done | bytes 262176 | tf_op jit(solution)/shard_map/ppermute | solution.py:214
  51.7 1.7 %collective-permute-start.13 = (bf16[64,2048]{1,0:T(8,128)(2,1)S(1)}, bf16[64,2048]{1,0:T(8,128)(2,1)S(1)}, u32[]{:S(2)}, u32[]{:S(2)}) collective-permute-start(bf16[64,2048]{1,0:T(8,128)(2,1)S(1)} %collective-permute-done.11.rest_5_), channel_id=1, source_target_pairs={{0,4},{4,8},{8,12},{12,14},{14,10},{10,6},{6,2},{2,0},{1,5},{5,9},... | collective-permute-start | bytes 786440 | tf_op jit(solution)/shard_map/ppermute | solution.py:214
  53.4 1.5 %collective-permute-start.17 = (bf16[32,4096]{1,0:T(8,128)(2,1)S(1)}, bf16[32,4096]{1,0:T(8,128)(2,1)S(1)}, u32[]{:S(2)}, u32[]{:S(2)}) collective-permute-start(bf16[32,4096]{1,0:T(8,128)(2,1)S(1)} %collective-permute-done.16.rest_13_), channel_id=1, source_target_pairs={{0,16},{16,0},{1,17},{17,1},{2,18},{18,2},{3,19},{19,3},{4,20},{20... | collective-permute-start | bytes 786440 | tf_op jit(solution)/shard_map/ppermute | solution.py:269
  54.9 1.6 %collective-permute-start.25 = (bf16[32,4096]{1,0:T(8,128)(2,1)S(1)}, bf16[32,4096]{1,0:T(8,128)(2,1)S(1)}, u32[]{:S(2)}, u32[]{:S(2)}) collective-permute-start(bf16[32,4096]{1,0:T(8,128)(2,1)S(1)} %collective-permute-done.21.rest_2_), channel_id=1, source_target_pairs={{0,4},{4,8},{8,12},{12,14},{14,10},{10,6},{6,2},{2,0},{1,5},{5,9},... | collective-permute-start | bytes 786440 | tf_op jit(solution)/shard_map/ppermute | solution.py:214
  57.0 2.5 %collective-permute-done.13.rest_7_ = bf16[64,2048]{1,0:T(8,128)(2,1)S(1)} collective-permute-done((bf16[64,2048]{1,0:T(8,128)(2,1)S(1)}, bf16[64,2048]{1,0:T(8,128)(2,1)S(1)}, u32[]{:S(2)}, u32[]{:S(2)}) %collective-permute-start.13) | collective-permute-done | bytes 262176 | tf_op jit(solution)/shard_map/ppermute | solution.py:214
  59.5 2.8 %shard_map.97 = (f32[256,128]{1,0:T(8,128)S(1)}, f32[256,128]{1,0:T(8,128)S(1)}) custom-call(bf16[256,2176]{1,0:T(8,128)(2,1)S(1)} %shard_map.96.here.mine, bf16[256,2176]{1,0:T(8,128)(2,1)} %collective-permute-done.8.across, f32[1,512]{1,0:T(1,128)S(1)} %convert_element_type.41.ids, bf16[64,2048]{1,0:T(8,128)(2,1)S(1)} %dynamic-slice_bitcast_fusion.1.rest_0_, ...), custom_call_target="tpu_custom_call" | custom-call | flops 1 | bytes 1 | tf_op jit(solution)/shard_map/pallas_call | solution.py:263
  62.3 1.5 %collective-permute-start.18 = (f32[256,128]{1,0:T(8,128)S(1)}, f32[256,128]{1,0:T(8,128)S(1)}, u32[]{:S(2)}, u32[]{:S(2)}) collective-permute-start(f32[256,128]{1,0:T(8,128)S(1)} %get-tuple-element.42), channel_id=1, source_target_pairs={{0,16},{16,0},{1,17},{17,1},{2,18},{18,2},{3,19},{19,3},{4,20},{20... | collective-permute-start | bytes 393224 | tf_op jit(solution)/shard_map/ppermute | solution.py:270
  63.8 3.6 %collective-permute-done.18.crossed = f32[256,128]{1,0:T(8,128)S(1)} collective-permute-done((f32[256,128]{1,0:T(8,128)S(1)}, f32[256,128]{1,0:T(8,128)S(1)}, u32[]{:S(2)}, u32[]{:S(2)}) %collective-permute-start.18) | collective-permute-done | bytes 131104 | tf_op jit(solution)/shard_map/ppermute | solution.py:270
  67.4 1.3 %collective-permute-done.20.beyond = f32[256,128]{1,0:T(8,128)S(1)} collective-permute-done((f32[256,128]{1,0:T(8,128)S(1)}, f32[256,128]{1,0:T(8,128)S(1)}, u32[]{:S(2)}, u32[]{:S(2)}) %collective-permute-start.20) | collective-permute-done | bytes 131104 | tf_op jit(solution)/shard_map/ppermute | solution.py:272
  68.7 5.3 %shard_map.98 = (bf16[120,8192]{1,0:T(8,128)(2,1)}, bf16[120,4096]{1,0:T(8,128)(2,1)S(1)}, f32[1,128]{1,0:T(1,128)S(1)}, f32[1,128]{1,0:T(1,128)S(1)}) custom-call(s32[2]{0:T(128)S(1)} %pad_add_fusion.place, bf16[256,2176]{1,0:T(8,128)(2,1)S(1)} %shard_map.96.here.mine, bf16[256,2176]{1,0:T(8,128)(2,1)} %shard_map.95.theirs, ...), custom_call_target="tpu_custom_call" | custom-call | flops 1 | bytes 1 | tf_op jit(solution)/shard_map/pallas_call | solution.py:278
  74.5 2.1 %collective-permute-done.28 = f32[128]{0:T(128)S(1)} collective-permute-done((f32[128]{0:T(128)S(1)}, f32[128]{0:T(128)S(1)}, u32[]{:S(2)}, u32[]{:S(2)}) %collective-permute-start.28) | collective-permute-done | bytes 544 | tf_op jit(solution)/shard_map/ppermute | solution.py:307
  77.1 1.0 %constant_dynamic-update-slice_fusion = bf16[120,8192]{1,0:T(8,128)(2,1)} fusion(bf16[120,8192]{1,0:T(8,128)(2,1)} %get-tuple-element.48, bf16[120,4096]{1,0:T(8,128)(2,1)S(1)} %collective-permute-done.27, s32[]{:T(128)S(6)} %select_n.21), kind=kLoop, calls=%fused_computation.6 | loop fusion | bytes 1966084 | tf_op jit(solution)/shard_map/dynamic_update_slice | solution.py:308
  (59 shorter events, 9.9 us)
Async XLA Ops:
  0.6 10.5 %copy-start.1 = (bf16[120,8192]{1,0:T(8,128)(2,1)S(1)}, bf16[120,8192]{1,0:T(8,128)(2,1)}, u32[]{:S(2)}) copy-start(bf16[120,8192]{1,0:T(8,128)(2,1)} %hidden.3) | copy-start | bytes 5898244
  0.7 10.5 %collective-permute-start = (bf16[120,8192]{1,0:T(8,128)(2,1)}, bf16[120,8192]{1,0:T(8,128)(2,1)}, u32[]{:S(2)}, u32[]{:S(2)}) collective-permute-start(bf16[120,8192]{1,0:T(8,128)(2,1)} %hidden.3), channel_id=1, source_target_pairs={{0,1},{1,0},{2,3},{3,2},{4,5},{5,4},{6,7},{7,6},{8,9},{9,8},{10,11... | collective-permute-start | bytes 5898248 | tf_op jit(solution)/shard_map/ppermute | solution.py:219
  1.7 12.4 %collective-permute-start.7 = (bf16[64,2048]{1,0:T(8,128)(2,1)S(1)}, bf16[64,2048]{1,0:T(8,128)(2,1)}, u32[]{:S(2)}, u32[]{:S(2)}) collective-permute-start(bf16[64,2048]{1,0:T(8,128)(2,1)S(1)} %dynamic-slice_bitcast_fusion.1.rest_0_), channel_id=1, source_target_pairs={{0,2},{4,0},{8,4},{12,8},{14,12},{10,14},{6,10},{2,6},{1,3},{5,1},... | collective-permute-start | bytes 786440 | tf_op jit(solution)/shard_map/ppermute | solution.py:214
  4.7 9.4 %collective-permute-start.6 = (bf16[64,2048]{1,0:T(8,128)(2,1)S(1)}, bf16[64,2048]{1,0:T(8,128)(2,1)}, u32[]{:S(2)}, u32[]{:S(2)}) collective-permute-start(bf16[64,2048]{1,0:T(8,128)(2,1)S(1)} %dynamic-slice_bitcast_fusion.1.rest_0_), channel_id=1, source_target_pairs={{0,4},{4,8},{8,12},{12,14},{14,10},{10,6},{6,2},{2,0},{1,5},{5,9},... | collective-permute-start | bytes 786440 | tf_op jit(solution)/shard_map/ppermute | solution.py:214
  7.8 2.8 %collective-permute-start.1 = (f32[128,2]{1,0:T(8,128)S(1)}, f32[128,2]{1,0:T(8,128)S(1)}, u32[]{:S(2)}, u32[]{:S(2)}) collective-permute-start(f32[128,2]{1,0:T(8,128)S(1)} %concatenate.7.own_small), channel_id=1, source_target_pairs={{0,1},{1,0},{2,3},{3,2},{4,5},{5,4},{6,7},{7,6},{8,9},{9,8},{10,11... | collective-permute-start | bytes 3080 | tf_op jit(solution)/shard_map/ppermute | solution.py:224
  8.7 9.2 %collective-permute-start.3 = (bf16[32,4096]{1,0:T(8,128)(2,1)}, bf16[32,4096]{1,0:T(8,128)(2,1)}, u32[]{:S(2)}, u32[]{:S(2)}) collective-permute-start(bf16[32,4096]{1,0:T(8,128)(2,1)} %get-tuple-element.53), channel_id=1, source_target_pairs={{0,2},{4,0},{8,4},{12,8},{14,12},{10,14},{6,10},{2,6},{1,3},{5,1},... | collective-permute-start | bytes 786440 | tf_op jit(solution)/shard_map/ppermute | solution.py:214
  10.6 8.7 %collective-permute-start.2 = (bf16[32,4096]{1,0:T(8,128)(2,1)}, bf16[32,4096]{1,0:T(8,128)(2,1)}, u32[]{:S(2)}, u32[]{:S(2)}) collective-permute-start(bf16[32,4096]{1,0:T(8,128)(2,1)} %get-tuple-element.53), channel_id=1, source_target_pairs={{0,4},{4,8},{8,12},{12,14},{14,10},{10,6},{6,2},{2,0},{1,5},{5,9},... | collective-permute-start | bytes 786440 | tf_op jit(solution)/shard_map/ppermute | solution.py:214
  11.2 13.1 %copy-start.5 = (bf16[4096]{0:T(1024)(128)(2,1)S(1)}, bf16[4096]{0:T(1024)(128)(2,1)}, u32[]{:S(2)}) copy-start(bf16[4096]{0:T(1024)(128)(2,1)} %param.14) | copy-start | bytes 24580
  14.1 45.4 %collective-permute-start.8 = (bf16[256,2176]{1,0:T(8,128)(2,1)}, bf16[256,2176]{1,0:T(8,128)(2,1)}, u32[]{:S(2)}, u32[]{:S(2)}) collective-permute-start(bf16[256,2176]{1,0:T(8,128)(2,1)} %shard_map.95.theirs), channel_id=1, source_target_pairs={{0,16},{16,0},{1,17},{17,1},{2,18},{18,2},{3,19},{19,3},{4,20},{20... | collective-permute-start | bytes 3342344 | tf_op jit(solution)/shard_map/ppermute | solution.py:250
  19.3 9.6 %collective-permute-start.4 = (bf16[32,4096]{1,0:T(8,128)(2,1)}, bf16[32,4096]{1,0:T(8,128)(2,1)}, u32[]{:S(2)}, u32[]{:S(2)}) collective-permute-start(bf16[32,4096]{1,0:T(8,128)(2,1)} %collective-permute-done.2.rest_1_), channel_id=1, source_target_pairs={{0,4},{4,8},{8,12},{12,14},{14,10},{10,6},{6,2},{2,0},{1,5},{5,9},... | collective-permute-start | bytes 786440 | tf_op jit(solution)/shard_map/ppermute | solution.py:214
  19.8 9.6 %collective-permute-start.5 = (bf16[32,4096]{1,0:T(8,128)(2,1)}, bf16[32,4096]{1,0:T(8,128)(2,1)}, u32[]{:S(2)}, u32[]{:S(2)}) collective-permute-start(bf16[32,4096]{1,0:T(8,128)(2,1)} %collective-permute-done.3.rest_3_), channel_id=1, source_target_pairs={{0,2},{4,0},{8,4},{12,8},{14,12},{10,14},{6,10},{2,6},{1,3},{5,1},... | collective-permute-start | bytes 786440 | tf_op jit(solution)/shard_map/ppermute | solution.py:214
  21.4 13.1 %collective-permute-start.9 = (bf16[64,2048]{1,0:T(8,128)(2,1)}, bf16[64,2048]{1,0:T(8,128)(2,1)}, u32[]{:S(2)}, u32[]{:S(2)}) collective-permute-start(bf16[64,2048]{1,0:T(8,128)(2,1)} %collective-permute-done.6.rest_1_), channel_id=1, source_target_pairs={{0,4},{4,8},{8,12},{12,14},{14,10},{10,6},{6,2},{2,0},{1,5},{5,9},... | collective-permute-start | bytes 786440 | tf_op jit(solution)/shard_map/ppermute | solution.py:214
  21.8 13.2 %collective-permute-start.10 = (bf16[64,2048]{1,0:T(8,128)(2,1)}, bf16[64,2048]{1,0:T(8,128)(2,1)}, u32[]{:S(2)}, u32[]{:S(2)}) collective-permute-start(bf16[64,2048]{1,0:T(8,128)(2,1)} %collective-permute-done.7.rest_2_), channel_id=1, source_target_pairs={{0,2},{4,0},{8,4},{12,8},{14,12},{10,14},{6,10},{2,6},{1,3},{5,1},... | collective-permute-start | bytes 786440 | tf_op jit(solution)/shard_map/ppermute | solution.py:214
  24.3 19.7 %copy-start.3 = (bf16[32,4096]{1,0:T(8,128)(2,1)S(1)}, bf16[32,4096]{1,0:T(8,128)(2,1)}, u32[]{:S(2)}) copy-start(bf16[32,4096]{1,0:T(8,128)(2,1)} %get-tuple-element.45) | copy-start | bytes 786436
  29.3 11.1 %collective-permute-start.14 = (bf16[32,4096]{1,0:T(8,128)(2,1)}, bf16[32,4096]{1,0:T(8,128)(2,1)S(1)}, u32[]{:S(2)}, u32[]{:S(2)}) collective-permute-start(bf16[32,4096]{1,0:T(8,128)(2,1)} %collective-permute-done.5.rest_7_), channel_id=1, source_target_pairs={{0,2},{4,0},{8,4},{12,8},{14,12},{10,14},{6,10},{2,6},{1,3},{5,1},... | collective-permute-start | bytes 786440 | tf_op jit(solution)/shard_map/ppermute | solution.py:214
  30.9 11.2 %collective-permute-start.15 = (bf16[32,4096]{1,0:T(8,128)(2,1)}, bf16[32,4096]{1,0:T(8,128)(2,1)S(1)}, u32[]{:S(2)}, u32[]{:S(2)}) collective-permute-start(bf16[32,4096]{1,0:T(8,128)(2,1)} %collective-permute-done.4.rest_5_), channel_id=1, source_target_pairs={{0,4},{4,8},{8,12},{12,14},{14,10},{10,6},{6,2},{2,0},{1,5},{5,9},... | collective-permute-start | bytes 786440 | tf_op jit(solution)/shard_map/ppermute | solution.py:214
  34.9 9.1 %collective-permute-start.11 = (bf16[64,2048]{1,0:T(8,128)(2,1)}, bf16[64,2048]{1,0:T(8,128)(2,1)S(1)}, u32[]{:S(2)}, u32[]{:S(2)}) collective-permute-start(bf16[64,2048]{1,0:T(8,128)(2,1)} %collective-permute-done.9.rest_3_), channel_id=1, source_target_pairs={{0,4},{4,8},{8,12},{12,14},{14,10},{10,6},{6,2},{2,0},{1,5},{5,9},... | collective-permute-start | bytes 786440 | tf_op jit(solution)/shard_map/ppermute | solution.py:214
  36.6 9.4 %collective-permute-start.12 = (bf16[64,2048]{1,0:T(8,128)(2,1)}, bf16[64,2048]{1,0:T(8,128)(2,1)S(1)}, u32[]{:S(2)}, u32[]{:S(2)}) collective-permute-start(bf16[64,2048]{1,0:T(8,128)(2,1)} %collective-permute-done.10.rest_4_), channel_id=1, source_target_pairs={{0,2},{4,0},{8,4},{12,8},{14,12},{10,14},{6,10},{2,6},{1,3},{5,1},... | collective-permute-start | bytes 786440 | tf_op jit(solution)/shard_map/ppermute | solution.py:214
  40.4 7.7 %collective-permute-start.24 = (bf16[32,4096]{1,0:T(8,128)(2,1)S(1)}, bf16[32,4096]{1,0:T(8,128)(2,1)S(1)}, u32[]{:S(2)}, u32[]{:S(2)}) collective-permute-start(bf16[32,4096]{1,0:T(8,128)(2,1)S(1)} %collective-permute-done.14.rest_11_), channel_id=1, source_target_pairs={{0,16},{16,0},{1,17},{17,1},{2,18},{18,2},{3,19},{19,3},{4,20},{20... | collective-permute-start | bytes 786440 | tf_op jit(solution)/shard_map/ppermute | solution.py:260
  42.1 9.6 %collective-permute-start.16 = (bf16[32,4096]{1,0:T(8,128)(2,1)S(1)}, bf16[32,4096]{1,0:T(8,128)(2,1)S(1)}, u32[]{:S(2)}, u32[]{:S(2)}) collective-permute-start(bf16[32,4096]{1,0:T(8,128)(2,1)S(1)} %collective-permute-done.14.rest_11_), channel_id=1, source_target_pairs={{0,2},{4,0},{8,4},{12,8},{14,12},{10,14},{6,10},{2,6},{1,3},{5,1},... | collective-permute-start | bytes 786440 | tf_op jit(solution)/shard_map/ppermute | solution.py:214
  44.0 9.4 %collective-permute-start.21 = (bf16[32,4096]{1,0:T(8,128)(2,1)S(1)}, bf16[32,4096]{1,0:T(8,128)(2,1)S(1)}, u32[]{:S(2)}, u32[]{:S(2)}) collective-permute-start(bf16[32,4096]{1,0:T(8,128)(2,1)S(1)} %copy-done.3), channel_id=1, source_target_pairs={{0,4},{4,8},{8,12},{12,14},{14,10},{10,6},{6,2},{2,0},{1,5},{5,9},... | collective-permute-start | bytes 786440 | tf_op jit(solution)/shard_map/ppermute | solution.py:214
  46.1 8.8 %collective-permute-start.23 = (bf16[32,4096]{1,0:T(8,128)(2,1)S(1)}, bf16[32,4096]{1,0:T(8,128)(2,1)S(1)}, u32[]{:S(2)}, u32[]{:S(2)}) collective-permute-start(bf16[32,4096]{1,0:T(8,128)(2,1)S(1)} %collective-permute-done.15.rest_9_), channel_id=1, source_target_pairs={{0,16},{16,0},{1,17},{17,1},{2,18},{18,2},{3,19},{19,3},{4,20},{20... | collective-permute-start | bytes 786440 | tf_op jit(solution)/shard_map/ppermute | solution.py:260
  48.1 8.4 %collective-permute-start.22 = (bf16[32,4096]{1,0:T(8,128)(2,1)S(1)}, bf16[32,4096]{1,0:T(8,128)(2,1)S(1)}, u32[]{:S(2)}, u32[]{:S(2)}) collective-permute-start(bf16[32,4096]{1,0:T(8,128)(2,1)S(1)} %copy-done.3), channel_id=1, source_target_pairs={{0,2},{4,0},{8,4},{12,8},{14,12},{10,14},{6,10},{2,6},{1,3},{5,1},... | collective-permute-start | bytes 786440 | tf_op jit(solution)/shard_map/ppermute | solution.py:214
  51.7 7.8 %collective-permute-start.13 = (bf16[64,2048]{1,0:T(8,128)(2,1)S(1)}, bf16[64,2048]{1,0:T(8,128)(2,1)S(1)}, u32[]{:S(2)}, u32[]{:S(2)}) collective-permute-start(bf16[64,2048]{1,0:T(8,128)(2,1)S(1)} %collective-permute-done.11.rest_5_), channel_id=1, source_target_pairs={{0,4},{4,8},{8,12},{12,14},{14,10},{10,6},{6,2},{2,0},{1,5},{5,9},... | collective-permute-start | bytes 786440 | tf_op jit(solution)/shard_map/ppermute | solution.py:214
  53.4 8.9 %collective-permute-start.17 = (bf16[32,4096]{1,0:T(8,128)(2,1)S(1)}, bf16[32,4096]{1,0:T(8,128)(2,1)S(1)}, u32[]{:S(2)}, u32[]{:S(2)}) collective-permute-start(bf16[32,4096]{1,0:T(8,128)(2,1)S(1)} %collective-permute-done.16.rest_13_), channel_id=1, source_target_pairs={{0,16},{16,0},{1,17},{17,1},{2,18},{18,2},{3,19},{19,3},{4,20},{20... | collective-permute-start | bytes 786440 | tf_op jit(solution)/shard_map/ppermute | solution.py:269
  54.9 12.4 %collective-permute-start.25 = (bf16[32,4096]{1,0:T(8,128)(2,1)S(1)}, bf16[32,4096]{1,0:T(8,128)(2,1)S(1)}, u32[]{:S(2)}, u32[]{:S(2)}) collective-permute-start(bf16[32,4096]{1,0:T(8,128)(2,1)S(1)} %collective-permute-done.21.rest_2_), channel_id=1, source_target_pairs={{0,4},{4,8},{8,12},{12,14},{14,10},{10,6},{6,2},{2,0},{1,5},{5,9},... | collective-permute-start | bytes 786440 | tf_op jit(solution)/shard_map/ppermute | solution.py:214
  56.5 10.9 %collective-permute-start.26 = (bf16[32,4096]{1,0:T(8,128)(2,1)S(1)}, bf16[32,4096]{1,0:T(8,128)(2,1)S(1)}, u32[]{:S(2)}, u32[]{:S(2)}) collective-permute-start(bf16[32,4096]{1,0:T(8,128)(2,1)S(1)} %collective-permute-done.22.rest_4_), channel_id=1, source_target_pairs={{0,2},{4,0},{8,4},{12,8},{14,12},{10,14},{6,10},{2,6},{1,3},{5,1},... | collective-permute-start | bytes 786440 | tf_op jit(solution)/shard_map/ppermute | solution.py:214
  62.3 5.0 %collective-permute-start.18 = (f32[256,128]{1,0:T(8,128)S(1)}, f32[256,128]{1,0:T(8,128)S(1)}, u32[]{:S(2)}, u32[]{:S(2)}) collective-permute-start(f32[256,128]{1,0:T(8,128)S(1)} %get-tuple-element.42), channel_id=1, source_target_pairs={{0,16},{16,0},{1,17},{17,1},{2,18},{18,2},{3,19},{19,3},{4,20},{20... | collective-permute-start | bytes 393224 | tf_op jit(solution)/shard_map/ppermute | solution.py:270
  63.8 3.6 %collective-permute-start.19 = (f32[256,128]{1,0:T(8,128)S(1)}, f32[256,128]{1,0:T(8,128)S(1)}, u32[]{:S(2)}, u32[]{:S(2)}) collective-permute-start(f32[256,128]{1,0:T(8,128)S(1)} %get-tuple-element.37.here), channel_id=1, source_target_pairs={{0,1},{1,0},{2,3},{3,2},{4,5},{5,4},{6,7},{7,6},{8,9},{9,8},{10,11... | collective-permute-start | bytes 393224 | tf_op jit(solution)/shard_map/ppermute | solution.py:271
  67.3 1.3 %collective-permute-start.20 = (f32[256,128]{1,0:T(8,128)S(1)}, f32[256,128]{1,0:T(8,128)S(1)}, u32[]{:S(2)}, u32[]{:S(2)}) collective-permute-start(f32[256,128]{1,0:T(8,128)S(1)} %collective-permute-done.18.crossed), channel_id=1, source_target_pairs={{0,1},{1,0},{2,3},{3,2},{4,5},{5,4},{6,7},{7,6},{8,9},{9,8},{10,11... | collective-permute-start | bytes 393224 | tf_op jit(solution)/shard_map/ppermute | solution.py:272
  74.0 3.1 %collective-permute-start.27 = (bf16[120,4096]{1,0:T(8,128)(2,1)S(1)}, bf16[120,4096]{1,0:T(8,128)(2,1)S(1)}, u32[]{:S(2)}, u32[]{:S(2)}) collective-permute-start(bf16[120,4096]{1,0:T(8,128)(2,1)S(1)} %get-tuple-element.49), channel_id=1, source_target_pairs={{0,1},{1,0},{2,3},{3,2},{4,5},{5,4},{6,7},{7,6},{8,9},{9,8},{10,11... | collective-permute-start | bytes 2949128 | tf_op jit(solution)/shard_map/ppermute | solution.py:306
  74.2 2.4 %collective-permute-start.28 = (f32[128]{0:T(128)S(1)}, f32[128]{0:T(128)S(1)}, u32[]{:S(2)}, u32[]{:S(2)}) collective-permute-start(f32[128]{0:T(128)S(1)} %bitcast.23), channel_id=1, source_target_pairs={{0,1},{1,0},{2,3},{3,2},{4,5},{5,4},{6,7},{7,6},{8,9},{9,8},{10,11... | collective-permute-start | bytes 1544 | tf_op jit(solution)/shard_map/ppermute | solution.py:307
  (3 other events, 18.7 us)

commit v5 on v4

--- a/solution.py
+++ b/solution.py
@@ -194,6 +194,10 @@
     near = far // 2
     lengths = {1: (far, count - 1 - far, near), -1: (count - 1 - far, far, near)}
     slots = {way: slots_of(lengths[way], (1, 0, 2)) for way in (1, -1)}
+    if count == 8:
+        for way, chains in ((1, (1, 0, 2, 1, 0, 1, 0, 0, 2)), (-1, (1, 0, 2, 1, 0, 1, 0, 1, 2))):
+            left = {c: iter(range(1, n + 1)) for c, n in enumerate(lengths[way])}
+            slots[way] = [(c, next(left[c])) for c in chains]
     held = {}
     for way in (1, -1):
         held[0, 0, way] = down_own
@@ -208,7 +212,7 @@
                 continue
             chain, distance = slots[way][k]
             piece = held[chain, distance - 1, way]
-            wait = list(gates) + (arrived[k - 2] if k >= 2 else [])
+            wait = list(gates) + (arrived[k - 2] if k >= 3 else [])
             if wait:
                 piece = after(piece, *wait)
             held[chain, distance, way] = lax.ppermute(piece, "adapter", perms[way])
@@ -259,7 +263,7 @@
         if near < d < far:
             across_far[d, w] = lax.ppermute(held[1, d, w], "groups", swap)
     for k in range(last_down + 1, max(len(slots[1]), len(slots[-1]))):
-        send_slot(k, *across_far.values())
+        send_slot(k, across_far[far - 1, 1])
     here, there = pl.pallas_call(
         codes_kernel,
         out_shape=[fl(2 * full, 128), fl(2 * full, 128)],

time: 78.4 us -> 77.4 us (0.987)
  starting transfers between devices: 30.7 us -> 28.3 us
  waiting for transfers between devices: 26.8 us -> 28.4 us
    ppermute x18, starting transfers between devices: 21.8 us -> 19.8 us  [send_slot(): held[chain, distance, way] = lax.ppermute(piece, 'adapter', perms[way])]
    ppermute x18, waiting for transfers between devices: 19.5 us -> 21.1 us  [send_slot(): held[chain, distance, way] = lax.ppermute(piece, 'adapter', perms[way])]
  transfers between devices with their start and end apart: 29 -> 29, of which waited for: 15 -> 13; matrix products, arithmetic and copies ran while one was open for 7% -> 7% of each run, Pallas kernels for 10% -> 10%
where the time goes in v5:
time: 77.4 us; the launch traced here: 77.1 us
  waiting for transfers between devices  28.4 us (37%)
  starting transfers between devices  28.3 us (37%)
  Pallas kernels  12.9 us (17%)
  other arithmetic  4.08 us (5%)
  local copies, waits for them, and re-layouts  2.67 us (3%)
  between operations  0.8 us (1%)
    ppermute x18, waiting for transfers between devices, send_slot(): held[chain, distance, way] = lax.ppermute(piece, 'adapter', perms[way])  21.1 us
    ppermute x18, starting transfers between devices, send_slot(): held[chain, distance, way] = lax.ppermute(piece, 'adapter', perms[way])  19.8 us
    pallas_call x1, Pallas kernels, gathered_matrices(): pl.pallas_call(delta_kernel, grid_spec=pltpu.PrefetchScalarGridSpec(num_s...  5.41 us
    pallas_call x2, Pallas kernels, normed(): pl.pallas_call(norm_kernel, grid_spec=pltpu.PrefetchScalarGridSpec(num_sc...  4.83 us
    ppermute x1, waiting for transfers between devices, gathered_matrices(): crossed = lax.ppermute(after(there, across_far[far, 1]), 'groups', swap)  3.85 us
    ppermute x2, starting transfers between devices, gathered_matrices(): across_far[d, w] = lax.ppermute(held[1, d, w], 'groups', swap)  2.67 us
    pallas_call x1, Pallas kernels, gathered_matrices(): pl.pallas_call(codes_kernel, out_shape=[fl(2 * full, 128), fl(2 * full, 1...  2.65 us
    ppermute x1, waiting for transfers between devices, gathered_matrices(): part_back = lax.ppermute(other_part.reshape(-1), 'fsdp', swap)  2.06 us
  transfers between devices with their start and end apart: 29, of which 13 were waited for; matrix products, arithmetic and copies ran while one was open for 7% of the time, Pallas kernels for 10%

profile of v5, /device:TPU:0, one launch (start us, length us, event | category | flops | bytes accessed | tf_op | source)
XLA Modules:
  0.0 77.1 jit_solution(9592970735072081951)
XLA Ops:
  1.7 3.0 %collective-permute-start.5 = (bf16[64,2048]{1,0:T(8,128)(2,1)S(1)}, bf16[64,2048]{1,0:T(8,128)(2,1)}, u32[]{:S(2)}, u32[]{:S(2)}) collective-permute-start(bf16[64,2048]{1,0:T(8,128)(2,1)S(1)} %dynamic-slice_bitcast_fusion.1.rest_0_), channel_id=1, source_target_pairs={{0,2},{4,0},{8,4},{12,8},{14,12},{10,14},{6,10},{2,6},{1,3},{5,1},... | collective-permute-start | bytes 786440 | tf_op jit(solution)/shard_map/ppermute | solution.py:218
  4.8 0.8 select_reduce_fusion
  5.6 2.0 %multiply_reduce_fusion = f32[120]{0:T(128)S(1)} fusion(bf16[120,8192]{1,0:T(8,128)(2,1)} %hidden.3), kind=kLoop, calls=%fused_computation | loop fusion | flops 2949000 | bytes 1966560 | tf_op jit(solution)/shard_map/reduce_sum | solution.py:225
  7.9 0.8 %dynamic-slice_bitcast_fusion = (bf16[32,4096]{1,0:T(8,128)(2,1)}, bf16[32,4096]{1,0:T(8,128)(2,1)}) fusion(bf16[1,64,4096]{2,1,0:T(8,128)(2,1)S(1)} %copy-done.2, s32[]{:T(128)S(6)} %select_n.20, s32[]{:T(128)S(6)} %select_n.18), kind=kLoop, calls=%fused_computation.1 | loop fusion | bytes 1048584 | tf_op jit(solution)/shard_map/dynamic_slice | solution.py:205
  8.7 1.9 %collective-permute-start.13 = (bf16[32,4096]{1,0:T(8,128)(2,1)}, bf16[32,4096]{1,0:T(8,128)(2,1)}, u32[]{:S(2)}, u32[]{:S(2)}) collective-permute-start(bf16[32,4096]{1,0:T(8,128)(2,1)} %get-tuple-element.48), channel_id=1, source_target_pairs={{0,2},{4,0},{8,4},{12,8},{14,12},{10,14},{6,10},{2,6},{1,3},{5,1},... | collective-permute-start | bytes 786440 | tf_op jit(solution)/shard_map/ppermute | solution.py:218
  11.2 2.9 %shard_map.95.theirs = bf16[256,2176]{1,0:T(8,128)(2,1)} custom-call(s32[2]{0:T(128)S(1)} %pad_add_fusion.place, bf16[120,8192]{1,0:T(8,128)(2,1)S(1)} %copy-done.1, bf16[120,8192]{1,0:T(8,128)(2,1)} %collective-permute-done.other, f32[128,2]{1,0:T(8,128)S(1)} %concatenate.7.own_small, f32[128,2]{1,0:T(8,128)S(1)} %collective-permute-done.1.other_small, ...), custom_call_target="tpu_custom_call" | custom-call | flops 1 | bytes 1 | tf_op jit(solution)/shard_map/pallas_call | solution.py:234
  14.1 1.6 %collective-permute-start.6 = (bf16[256,2176]{1,0:T(8,128)(2,1)}, bf16[256,2176]{1,0:T(8,128)(2,1)}, u32[]{:S(2)}, u32[]{:S(2)}) collective-permute-start(bf16[256,2176]{1,0:T(8,128)(2,1)} %shard_map.95.theirs), channel_id=1, source_target_pairs={{0,16},{16,0},{1,17},{17,1},{2,18},{18,2},{3,19},{19,3},{4,20},{20... | collective-permute-start | bytes 3342344 | tf_op jit(solution)/shard_map/ppermute | solution.py:254
  15.7 1.5 %collective-permute-start.3 = (bf16[32,4096]{1,0:T(8,128)(2,1)}, bf16[32,4096]{1,0:T(8,128)(2,1)}, u32[]{:S(2)}, u32[]{:S(2)}) collective-permute-start(bf16[32,4096]{1,0:T(8,128)(2,1)} %get-tuple-element.49), channel_id=1, source_target_pairs={{0,2},{4,0},{8,4},{12,8},{14,12},{10,14},{6,10},{2,6},{1,3},{5,1},... | collective-permute-start | bytes 786440 | tf_op jit(solution)/shard_map/ppermute | solution.py:218
  18.0 1.7 %collective-permute-start.14 = (bf16[32,4096]{1,0:T(8,128)(2,1)}, bf16[32,4096]{1,0:T(8,128)(2,1)}, u32[]{:S(2)}, u32[]{:S(2)}) collective-permute-start(bf16[32,4096]{1,0:T(8,128)(2,1)} %collective-permute-done.13.rest_3_), channel_id=1, source_target_pairs={{0,2},{4,0},{8,4},{12,8},{14,12},{10,14},{6,10},{2,6},{1,3},{5,1},... | collective-permute-start | bytes 786440 | tf_op jit(solution)/shard_map/ppermute | solution.py:218
  20.0 0.7 fusion.1
  20.8 4.4 %collective-permute-done.3.rest_4_ = bf16[32,4096]{1,0:T(8,128)(2,1)} collective-permute-done((bf16[32,4096]{1,0:T(8,128)(2,1)}, bf16[32,4096]{1,0:T(8,128)(2,1)}, u32[]{:S(2)}, u32[]{:S(2)}) %collective-permute-start.3) | collective-permute-done | bytes 262176 | tf_op jit(solution)/shard_map/ppermute | solution.py:218
  25.2 1.5 %collective-permute-done.2.rest_2_ = bf16[32,4096]{1,0:T(8,128)(2,1)} collective-permute-done((bf16[32,4096]{1,0:T(8,128)(2,1)}, bf16[32,4096]{1,0:T(8,128)(2,1)}, u32[]{:S(2)}, u32[]{:S(2)}) %collective-permute-start.2) | collective-permute-done | bytes 262176 | tf_op jit(solution)/shard_map/ppermute | solution.py:218
  27.3 1.5 %collective-permute-start.8 = (bf16[64,2048]{1,0:T(8,128)(2,1)}, bf16[64,2048]{1,0:T(8,128)(2,1)S(1)}, u32[]{:S(2)}, u32[]{:S(2)}) collective-permute-start(bf16[64,2048]{1,0:T(8,128)(2,1)} %collective-permute-done.5.rest_2_), channel_id=1, source_target_pairs={{0,2},{4,0},{8,4},{12,8},{14,12},{10,14},{6,10},{2,6},{1,3},{5,1},... | collective-permute-start | bytes 786440 | tf_op jit(solution)/shard_map/ppermute | solution.py:218
  28.8 1.9 %shard_map.96.here.mine = bf16[256,2176]{1,0:T(8,128)(2,1)S(1)} custom-call(s32[2]{0:T(128)S(1)} %pad_add_fusion.place, bf16[120,8192]{1,0:T(8,128)(2,1)S(1)} %copy-done.1, bf16[120,8192]{1,0:T(8,128)(2,1)} %collective-permute-done.other, f32[128,2]{1,0:T(8,128)S(1)} %concatenate.7.own_small, f32[128,2]{1,0:T(8,128)S(1)} %collective-permute-done.1.other_small, ...), custom_call_target="tpu_custom_call" | custom-call | flops 1 | bytes 1 | tf_op jit(solution)/shard_map/pallas_call | solution.py:234
  30.9 1.5 %collective-permute-done.12.rest_5_ = bf16[32,4096]{1,0:T(8,128)(2,1)} collective-permute-done((bf16[32,4096]{1,0:T(8,128)(2,1)}, bf16[32,4096]{1,0:T(8,128)(2,1)}, u32[]{:S(2)}, u32[]{:S(2)}) %collective-permute-start.12) | collective-permute-done | bytes 262176 | tf_op jit(solution)/shard_map/ppermute | solution.py:218
  32.9 1.5 %collective-permute-start.16 = (bf16[32,4096]{1,0:T(8,128)(2,1)}, bf16[32,4096]{1,0:T(8,128)(2,1)S(1)}, u32[]{:S(2)}, u32[]{:S(2)}) collective-permute-start(bf16[32,4096]{1,0:T(8,128)(2,1)} %collective-permute-done.14.rest_7_), channel_id=1, source_target_pairs={{0,2},{4,0},{8,4},{12,8},{14,12},{10,14},{6,10},{2,6},{1,3},{5,1},... | collective-permute-start | bytes 786440 | tf_op jit(solution)/shard_map/ppermute | solution.py:218
  34.4 3.5 %collective-permute-done.7.rest_3_ = bf16[64,2048]{1,0:T(8,128)(2,1)S(1)} collective-permute-done((bf16[64,2048]{1,0:T(8,128)(2,1)}, bf16[64,2048]{1,0:T(8,128)(2,1)S(1)}, u32[]{:S(2)}, u32[]{:S(2)}) %collective-permute-start.7) | collective-permute-done | bytes 262176 | tf_op jit(solution)/shard_map/ppermute | solution.py:218
  38.4 5.1 %collective-permute-done.15.rest_9_ = bf16[32,4096]{1,0:T(8,128)(2,1)S(1)} collective-permute-done((bf16[32,4096]{1,0:T(8,128)(2,1)}, bf16[32,4096]{1,0:T(8,128)(2,1)S(1)}, u32[]{:S(2)}, u32[]{:S(2)}) %collective-permute-start.15) | collective-permute-done | bytes 262176 | tf_op jit(solution)/shard_map/ppermute | solution.py:218
  43.5 1.6 %collective-permute-start.18 = (bf16[32,4096]{1,0:T(8,128)(2,1)S(1)}, bf16[32,4096]{1,0:T(8,128)(2,1)S(1)}, u32[]{:S(2)}, u32[]{:S(2)}) collective-permute-start(bf16[32,4096]{1,0:T(8,128)(2,1)S(1)} %collective-permute-done.16.rest_11_), channel_id=1, source_target_pairs={{0,2},{4,0},{8,4},{12,8},{14,12},{10,14},{6,10},{2,6},{1,3},{5,1},... | collective-permute-start | bytes 786440 | tf_op jit(solution)/shard_map/ppermute | solution.py:218
  45.1 1.6 %collective-permute-start.10 = (bf16[64,2048]{1,0:T(8,128)(2,1)S(1)}, bf16[64,2048]{1,0:T(8,128)(2,1)S(1)}, u32[]{:S(2)}, u32[]{:S(2)}) collective-permute-start(bf16[64,2048]{1,0:T(8,128)(2,1)S(1)} %collective-permute-done.8.rest_4_), channel_id=1, source_target_pairs={{0,2},{4,0},{8,4},{12,8},{14,12},{10,14},{6,10},{2,6},{1,3},{5,1},... | collective-permute-start | bytes 786440 | tf_op jit(solution)/shard_map/ppermute | solution.py:218
  48.0 3.4 %collective-permute-done.18.rest_13_ = bf16[32,4096]{1,0:T(8,128)(2,1)S(1)} collective-permute-done((bf16[32,4096]{1,0:T(8,128)(2,1)S(1)}, bf16[32,4096]{1,0:T(8,128)(2,1)S(1)}, u32[]{:S(2)}, u32[]{:S(2)}) %collective-permute-start.18) | collective-permute-done | bytes 262176 | tf_op jit(solution)/shard_map/ppermute | solution.py:218
  51.4 1.8 %collective-permute-start.19 = (bf16[32,4096]{1,0:T(8,128)(2,1)S(1)}, bf16[32,4096]{1,0:T(8,128)(2,1)S(1)}, u32[]{:S(2)}, u32[]{:S(2)}) collective-permute-start(bf16[32,4096]{1,0:T(8,128)(2,1)S(1)} %collective-permute-done.18.rest_13_), channel_id=1, source_target_pairs={{0,16},{16,0},{1,17},{17,1},{2,18},{18,2},{3,19},{19,3},{4,20},{20... | collective-permute-start | bytes 786440 | tf_op jit(solution)/shard_map/ppermute | solution.py:273
  53.2 1.0 %collective-permute-done.10.rest_6_ = bf16[64,2048]{1,0:T(8,128)(2,1)S(1)} collective-permute-done((bf16[64,2048]{1,0:T(8,128)(2,1)S(1)}, bf16[64,2048]{1,0:T(8,128)(2,1)S(1)}, u32[]{:S(2)}, u32[]{:S(2)}) %collective-permute-start.10) | collective-permute-done | bytes 262176 | tf_op jit(solution)/shard_map/ppermute | solution.py:218
  54.2 2.2 %collective-permute-start.26 = (bf16[32,4096]{1,0:T(8,128)(2,1)S(1)}, bf16[32,4096]{1,0:T(8,128)(2,1)S(1)}, u32[]{:S(2)}, u32[]{:S(2)}) collective-permute-start(bf16[32,4096]{1,0:T(8,128)(2,1)S(1)} %collective-permute-done.16.rest_11_), channel_id=1, source_target_pairs={{0,16},{16,0},{1,17},{17,1},{2,18},{18,2},{3,19},{19,3},{4,20},{20... | collective-permute-start | bytes 786440 | tf_op jit(solution)/shard_map/ppermute | solution.py:264
  57.1 1.4 %collective-permute-start.25 = (bf16[32,4096]{1,0:T(8,128)(2,1)}, bf16[32,4096]{1,0:T(8,128)(2,1)S(1)}, u32[]{:S(2)}, u32[]{:S(2)}) collective-permute-start(bf16[32,4096]{1,0:T(8,128)(2,1)} %collective-permute-done.3.rest_4_), channel_id=1, source_target_pairs={{0,2},{4,0},{8,4},{12,8},{14,12},{10,14},{6,10},{2,6},{1,3},{5,1},... | collective-permute-start | bytes 786440 | tf_op jit(solution)/shard_map/ppermute | solution.py:218
  58.5 2.6 %shard_map.97 = (f32[256,128]{1,0:T(8,128)S(1)}, f32[256,128]{1,0:T(8,128)S(1)}) custom-call(bf16[256,2176]{1,0:T(8,128)(2,1)S(1)} %shard_map.96.here.mine, bf16[256,2176]{1,0:T(8,128)(2,1)} %collective-permute-done.6.across, f32[1,512]{1,0:T(1,128)S(1)} %convert_element_type.41.ids, bf16[64,2048]{1,0:T(8,128)(2,1)S(1)} %dynamic-slice_bitcast_fusion.1.rest_0_, ...), custom_call_target="tpu_custom_call" | custom-call | flops 1 | bytes 1 | tf_op jit(solution)/shard_map/pallas_call | solution.py:267
  61.1 1.2 %collective-permute-start.20 = (f32[256,128]{1,0:T(8,128)S(1)}, f32[256,128]{1,0:T(8,128)S(1)}, u32[]{:S(2)}, u32[]{:S(2)}) collective-permute-start(f32[256,128]{1,0:T(8,128)S(1)} %get-tuple-element.40), channel_id=1, source_target_pairs={{0,16},{16,0},{1,17},{17,1},{2,18},{18,2},{3,19},{19,3},{4,20},{20... | collective-permute-start | bytes 393224 | tf_op jit(solution)/shard_map/ppermute | solution.py:274
  62.4 3.8 %collective-permute-done.20.crossed = f32[256,128]{1,0:T(8,128)S(1)} collective-permute-done((f32[256,128]{1,0:T(8,128)S(1)}, f32[256,128]{1,0:T(8,128)S(1)}, u32[]{:S(2)}, u32[]{:S(2)}) %collective-permute-start.20) | collective-permute-done | bytes 131104 | tf_op jit(solution)/shard_map/ppermute | solution.py:274
  66.3 1.3 %collective-permute-done.22.beyond = f32[256,128]{1,0:T(8,128)S(1)} collective-permute-done((f32[256,128]{1,0:T(8,128)S(1)}, f32[256,128]{1,0:T(8,128)S(1)}, u32[]{:S(2)}, u32[]{:S(2)}) %collective-permute-start.22) | collective-permute-done | bytes 131104 | tf_op jit(solution)/shard_map/ppermute | solution.py:276
  67.6 5.4 %shard_map.98 = (bf16[120,8192]{1,0:T(8,128)(2,1)}, bf16[120,4096]{1,0:T(8,128)(2,1)S(1)}, f32[1,128]{1,0:T(1,128)S(1)}, f32[1,128]{1,0:T(1,128)S(1)}) custom-call(s32[2]{0:T(128)S(1)} %pad_add_fusion.place, bf16[256,2176]{1,0:T(8,128)(2,1)S(1)} %shard_map.96.here.mine, bf16[256,2176]{1,0:T(8,128)(2,1)} %shard_map.95.theirs, ...), custom_call_target="tpu_custom_call" | custom-call | flops 1 | bytes 1 | tf_op jit(solution)/shard_map/pallas_call | solution.py:282
  73.5 2.1 %collective-permute-done.28 = f32[128]{0:T(128)S(1)} collective-permute-done((f32[128]{0:T(128)S(1)}, f32[128]{0:T(128)S(1)}, u32[]{:S(2)}, u32[]{:S(2)}) %collective-permute-start.28) | collective-permute-done | bytes 544 | tf_op jit(solution)/shard_map/ppermute | solution.py:311
  76.1 1.0 %constant_dynamic-update-slice_fusion = bf16[120,8192]{1,0:T(8,128)(2,1)} fusion(bf16[120,8192]{1,0:T(8,128)(2,1)} %get-tuple-element.44, bf16[120,4096]{1,0:T(8,128)(2,1)S(1)} %collective-permute-done.27, s32[]{:T(128)S(6)} %select_n.21), kind=kLoop, calls=%fused_computation.6 | loop fusion | bytes 1966084 | tf_op jit(solution)/shard_map/dynamic_update_slice | solution.py:312
  (57 shorter events, 8.0 us)
Async XLA Ops:
  0.6 10.5 %copy-start.1 = (bf16[120,8192]{1,0:T(8,128)(2,1)S(1)}, bf16[120,8192]{1,0:T(8,128)(2,1)}, u32[]{:S(2)}) copy-start(bf16[120,8192]{1,0:T(8,128)(2,1)} %hidden.3) | copy-start | bytes 5898244
  0.7 10.4 %copy-start.3 = (bf16[4096]{0:T(1024)(128)(2,1)S(1)}, bf16[4096]{0:T(1024)(128)(2,1)}, u32[]{:S(2)}) copy-start(bf16[4096]{0:T(1024)(128)(2,1)} %param.13) | copy-start | bytes 24580
  0.7 10.5 %collective-permute-start = (bf16[120,8192]{1,0:T(8,128)(2,1)}, bf16[120,8192]{1,0:T(8,128)(2,1)}, u32[]{:S(2)}, u32[]{:S(2)}) collective-permute-start(bf16[120,8192]{1,0:T(8,128)(2,1)} %hidden.3), channel_id=1, source_target_pairs={{0,1},{1,0},{2,3},{3,2},{4,5},{5,4},{6,7},{7,6},{8,9},{9,8},{10,11... | collective-permute-start | bytes 5898248 | tf_op jit(solution)/shard_map/ppermute | solution.py:223
  1.7 12.4 %collective-permute-start.5 = (bf16[64,2048]{1,0:T(8,128)(2,1)S(1)}, bf16[64,2048]{1,0:T(8,128)(2,1)}, u32[]{:S(2)}, u32[]{:S(2)}) collective-permute-start(bf16[64,2048]{1,0:T(8,128)(2,1)S(1)} %dynamic-slice_bitcast_fusion.1.rest_0_), channel_id=1, source_target_pairs={{0,2},{4,0},{8,4},{12,8},{14,12},{10,14},{6,10},{2,6},{1,3},{5,1},... | collective-permute-start | bytes 786440 | tf_op jit(solution)/shard_map/ppermute | solution.py:218
  4.7 9.4 %collective-permute-start.4 = (bf16[64,2048]{1,0:T(8,128)(2,1)S(1)}, bf16[64,2048]{1,0:T(8,128)(2,1)}, u32[]{:S(2)}, u32[]{:S(2)}) collective-permute-start(bf16[64,2048]{1,0:T(8,128)(2,1)S(1)} %dynamic-slice_bitcast_fusion.1.rest_0_), channel_id=1, source_target_pairs={{0,4},{4,8},{8,12},{12,14},{14,10},{10,6},{6,2},{2,0},{1,5},{5,9},... | collective-permute-start | bytes 786440 | tf_op jit(solution)/shard_map/ppermute | solution.py:218
  7.8 2.8 %collective-permute-start.1 = (f32[128,2]{1,0:T(8,128)S(1)}, f32[128,2]{1,0:T(8,128)S(1)}, u32[]{:S(2)}, u32[]{:S(2)}) collective-permute-start(f32[128,2]{1,0:T(8,128)S(1)} %concatenate.7.own_small), channel_id=1, source_target_pairs={{0,1},{1,0},{2,3},{3,2},{4,5},{5,4},{6,7},{7,6},{8,9},{9,8},{10,11... | collective-permute-start | bytes 3080 | tf_op jit(solution)/shard_map/ppermute | solution.py:228
  8.7 9.2 %collective-permute-start.13 = (bf16[32,4096]{1,0:T(8,128)(2,1)}, bf16[32,4096]{1,0:T(8,128)(2,1)}, u32[]{:S(2)}, u32[]{:S(2)}) collective-permute-start(bf16[32,4096]{1,0:T(8,128)(2,1)} %get-tuple-element.48), channel_id=1, source_target_pairs={{0,2},{4,0},{8,4},{12,8},{14,12},{10,14},{6,10},{2,6},{1,3},{5,1},... | collective-permute-start | bytes 786440 | tf_op jit(solution)/shard_map/ppermute | solution.py:218
  10.6 9.0 %collective-permute-start.11 = (bf16[32,4096]{1,0:T(8,128)(2,1)}, bf16[32,4096]{1,0:T(8,128)(2,1)}, u32[]{:S(2)}, u32[]{:S(2)}) collective-permute-start(bf16[32,4096]{1,0:T(8,128)(2,1)} %get-tuple-element.48), channel_id=1, source_target_pairs={{0,4},{4,8},{8,12},{12,14},{14,10},{10,6},{6,2},{2,0},{1,5},{5,9},... | collective-permute-start | bytes 786440 | tf_op jit(solution)/shard_map/ppermute | solution.py:218
  11.2 9.7 %copy-start.4 = (bf16[4096]{0:T(1024)(128)(2,1)S(1)}, bf16[4096]{0:T(1024)(128)(2,1)}, u32[]{:S(2)}) copy-start(bf16[4096]{0:T(1024)(128)(2,1)} %param.14) | copy-start | bytes 24580
  14.1 44.4 %collective-permute-start.6 = (bf16[256,2176]{1,0:T(8,128)(2,1)}, bf16[256,2176]{1,0:T(8,128)(2,1)}, u32[]{:S(2)}, u32[]{:S(2)}) collective-permute-start(bf16[256,2176]{1,0:T(8,128)(2,1)} %shard_map.95.theirs), channel_id=1, source_target_pairs={{0,16},{16,0},{1,17},{17,1},{2,18},{18,2},{3,19},{19,3},{4,20},{20... | collective-permute-start | bytes 3342344 | tf_op jit(solution)/shard_map/ppermute | solution.py:254
  15.7 9.5 %collective-permute-start.3 = (bf16[32,4096]{1,0:T(8,128)(2,1)}, bf16[32,4096]{1,0:T(8,128)(2,1)}, u32[]{:S(2)}, u32[]{:S(2)}) collective-permute-start(bf16[32,4096]{1,0:T(8,128)(2,1)} %get-tuple-element.49), channel_id=1, source_target_pairs={{0,2},{4,0},{8,4},{12,8},{14,12},{10,14},{6,10},{2,6},{1,3},{5,1},... | collective-permute-start | bytes 786440 | tf_op jit(solution)/shard_map/ppermute | solution.py:218
  17.2 9.6 %collective-permute-start.2 = (bf16[32,4096]{1,0:T(8,128)(2,1)}, bf16[32,4096]{1,0:T(8,128)(2,1)}, u32[]{:S(2)}, u32[]{:S(2)}) collective-permute-start(bf16[32,4096]{1,0:T(8,128)(2,1)} %get-tuple-element.49), channel_id=1, source_target_pairs={{0,4},{4,8},{8,12},{12,14},{14,10},{10,6},{6,2},{2,0},{1,5},{5,9},... | collective-permute-start | bytes 786440 | tf_op jit(solution)/shard_map/ppermute | solution.py:218
  18.0 12.9 %collective-permute-start.14 = (bf16[32,4096]{1,0:T(8,128)(2,1)}, bf16[32,4096]{1,0:T(8,128)(2,1)}, u32[]{:S(2)}, u32[]{:S(2)}) collective-permute-start(bf16[32,4096]{1,0:T(8,128)(2,1)} %collective-permute-done.13.rest_3_), channel_id=1, source_target_pairs={{0,2},{4,0},{8,4},{12,8},{14,12},{10,14},{6,10},{2,6},{1,3},{5,1},... | collective-permute-start | bytes 786440 | tf_op jit(solution)/shard_map/ppermute | solution.py:218
  19.6 12.8 %collective-permute-start.12 = (bf16[32,4096]{1,0:T(8,128)(2,1)}, bf16[32,4096]{1,0:T(8,128)(2,1)}, u32[]{:S(2)}, u32[]{:S(2)}) collective-permute-start(bf16[32,4096]{1,0:T(8,128)(2,1)} %collective-permute-done.11.rest_1_), channel_id=1, source_target_pairs={{0,4},{4,8},{8,12},{12,14},{14,10},{10,6},{6,2},{2,0},{1,5},{5,9},... | collective-permute-start | bytes 786440 | tf_op jit(solution)/shard_map/ppermute | solution.py:218
  26.8 11.1 %collective-permute-start.7 = (bf16[64,2048]{1,0:T(8,128)(2,1)}, bf16[64,2048]{1,0:T(8,128)(2,1)S(1)}, u32[]{:S(2)}, u32[]{:S(2)}) collective-permute-start(bf16[64,2048]{1,0:T(8,128)(2,1)} %collective-permute-done.4.rest_1_), channel_id=1, source_target_pairs={{0,4},{4,8},{8,12},{12,14},{14,10},{10,6},{6,2},{2,0},{1,5},{5,9},... | collective-permute-start | bytes 786440 | tf_op jit(solution)/shard_map/ppermute | solution.py:218
  27.3 10.6 %collective-permute-start.8 = (bf16[64,2048]{1,0:T(8,128)(2,1)}, bf16[64,2048]{1,0:T(8,128)(2,1)S(1)}, u32[]{:S(2)}, u32[]{:S(2)}) collective-permute-start(bf16[64,2048]{1,0:T(8,128)(2,1)} %collective-permute-done.5.rest_2_), channel_id=1, source_target_pairs={{0,2},{4,0},{8,4},{12,8},{14,12},{10,14},{6,10},{2,6},{1,3},{5,1},... | collective-permute-start | bytes 786440 | tf_op jit(solution)/shard_map/ppermute | solution.py:218
  32.4 11.1 %collective-permute-start.15 = (bf16[32,4096]{1,0:T(8,128)(2,1)}, bf16[32,4096]{1,0:T(8,128)(2,1)S(1)}, u32[]{:S(2)}, u32[]{:S(2)}) collective-permute-start(bf16[32,4096]{1,0:T(8,128)(2,1)} %collective-permute-done.12.rest_5_), channel_id=1, source_target_pairs={{0,4},{4,8},{8,12},{12,14},{14,10},{10,6},{6,2},{2,0},{1,5},{5,9},... | collective-permute-start | bytes 786440 | tf_op jit(solution)/shard_map/ppermute | solution.py:218
  32.9 10.6 %collective-permute-start.16 = (bf16[32,4096]{1,0:T(8,128)(2,1)}, bf16[32,4096]{1,0:T(8,128)(2,1)S(1)}, u32[]{:S(2)}, u32[]{:S(2)}) collective-permute-start(bf16[32,4096]{1,0:T(8,128)(2,1)} %collective-permute-done.14.rest_7_), channel_id=1, source_target_pairs={{0,2},{4,0},{8,4},{12,8},{14,12},{10,14},{6,10},{2,6},{1,3},{5,1},... | collective-permute-start | bytes 786440 | tf_op jit(solution)/shard_map/ppermute | solution.py:218
  37.9 9.6 %collective-permute-start.9 = (bf16[64,2048]{1,0:T(8,128)(2,1)S(1)}, bf16[64,2048]{1,0:T(8,128)(2,1)S(1)}, u32[]{:S(2)}, u32[]{:S(2)}) collective-permute-start(bf16[64,2048]{1,0:T(8,128)(2,1)S(1)} %collective-permute-done.7.rest_3_), channel_id=1, source_target_pairs={{0,4},{4,8},{8,12},{12,14},{14,10},{10,6},{6,2},{2,0},{1,5},{5,9},... | collective-permute-start | bytes 786440 | tf_op jit(solution)/shard_map/ppermute | solution.py:218
  43.5 7.9 %collective-permute-start.18 = (bf16[32,4096]{1,0:T(8,128)(2,1)S(1)}, bf16[32,4096]{1,0:T(8,128)(2,1)S(1)}, u32[]{:S(2)}, u32[]{:S(2)}) collective-permute-start(bf16[32,4096]{1,0:T(8,128)(2,1)S(1)} %collective-permute-done.16.rest_11_), channel_id=1, source_target_pairs={{0,2},{4,0},{8,4},{12,8},{14,12},{10,14},{6,10},{2,6},{1,3},{5,1},... | collective-permute-start | bytes 786440 | tf_op jit(solution)/shard_map/ppermute | solution.py:218
  45.1 9.1 %collective-permute-start.10 = (bf16[64,2048]{1,0:T(8,128)(2,1)S(1)}, bf16[64,2048]{1,0:T(8,128)(2,1)S(1)}, u32[]{:S(2)}, u32[]{:S(2)}) collective-permute-start(bf16[64,2048]{1,0:T(8,128)(2,1)S(1)} %collective-permute-done.8.rest_4_), channel_id=1, source_target_pairs={{0,2},{4,0},{8,4},{12,8},{14,12},{10,14},{6,10},{2,6},{1,3},{5,1},... | collective-permute-start | bytes 786440 | tf_op jit(solution)/shard_map/ppermute | solution.py:218
  46.7 9.8 %collective-permute-start.23 = (bf16[32,4096]{1,0:T(8,128)(2,1)S(1)}, bf16[32,4096]{1,0:T(8,128)(2,1)S(1)}, u32[]{:S(2)}, u32[]{:S(2)}) collective-permute-start(bf16[32,4096]{1,0:T(8,128)(2,1)S(1)} %collective-permute-done.15.rest_9_), channel_id=1, source_target_pairs={{0,16},{16,0},{1,17},{17,1},{2,18},{18,2},{3,19},{19,3},{4,20},{20... | collective-permute-start | bytes 786440 | tf_op jit(solution)/shard_map/ppermute | solution.py:264
  47.4 9.6 %collective-permute-start.17 = (bf16[64,2048]{1,0:T(8,128)(2,1)S(1)}, bf16[64,2048]{1,0:T(8,128)(2,1)S(1)}, u32[]{:S(2)}, u32[]{:S(2)}) collective-permute-start(bf16[64,2048]{1,0:T(8,128)(2,1)S(1)} %collective-permute-done.9.rest_5_), channel_id=1, source_target_pairs={{0,4},{4,8},{8,12},{12,14},{14,10},{10,6},{6,2},{2,0},{1,5},{5,9},... | collective-permute-start | bytes 786440 | tf_op jit(solution)/shard_map/ppermute | solution.py:218
  51.4 9.7 %collective-permute-start.19 = (bf16[32,4096]{1,0:T(8,128)(2,1)S(1)}, bf16[32,4096]{1,0:T(8,128)(2,1)S(1)}, u32[]{:S(2)}, u32[]{:S(2)}) collective-permute-start(bf16[32,4096]{1,0:T(8,128)(2,1)S(1)} %collective-permute-done.18.rest_13_), channel_id=1, source_target_pairs={{0,16},{16,0},{1,17},{17,1},{2,18},{18,2},{3,19},{19,3},{4,20},{20... | collective-permute-start | bytes 786440 | tf_op jit(solution)/shard_map/ppermute | solution.py:273
  54.2 12.0 %collective-permute-start.26 = (bf16[32,4096]{1,0:T(8,128)(2,1)S(1)}, bf16[32,4096]{1,0:T(8,128)(2,1)S(1)}, u32[]{:S(2)}, u32[]{:S(2)}) collective-permute-start(bf16[32,4096]{1,0:T(8,128)(2,1)S(1)} %collective-permute-done.16.rest_11_), channel_id=1, source_target_pairs={{0,16},{16,0},{1,17},{17,1},{2,18},{18,2},{3,19},{19,3},{4,20},{20... | collective-permute-start | bytes 786440 | tf_op jit(solution)/shard_map/ppermute | solution.py:264
  56.4 9.8 %collective-permute-start.24 = (bf16[32,4096]{1,0:T(8,128)(2,1)}, bf16[32,4096]{1,0:T(8,128)(2,1)S(1)}, u32[]{:S(2)}, u32[]{:S(2)}) collective-permute-start(bf16[32,4096]{1,0:T(8,128)(2,1)} %collective-permute-done.2.rest_2_), channel_id=1, source_target_pairs={{0,4},{4,8},{8,12},{12,14},{14,10},{10,6},{6,2},{2,0},{1,5},{5,9},... | collective-permute-start | bytes 786440 | tf_op jit(solution)/shard_map/ppermute | solution.py:218
  57.1 9.2 %collective-permute-start.25 = (bf16[32,4096]{1,0:T(8,128)(2,1)}, bf16[32,4096]{1,0:T(8,128)(2,1)S(1)}, u32[]{:S(2)}, u32[]{:S(2)}) collective-permute-start(bf16[32,4096]{1,0:T(8,128)(2,1)} %collective-permute-done.3.rest_4_), channel_id=1, source_target_pairs={{0,2},{4,0},{8,4},{12,8},{14,12},{10,14},{6,10},{2,6},{1,3},{5,1},... | collective-permute-start | bytes 786440 | tf_op jit(solution)/shard_map/ppermute | solution.py:218
  61.1 5.1 %collective-permute-start.20 = (f32[256,128]{1,0:T(8,128)S(1)}, f32[256,128]{1,0:T(8,128)S(1)}, u32[]{:S(2)}, u32[]{:S(2)}) collective-permute-start(f32[256,128]{1,0:T(8,128)S(1)} %get-tuple-element.40), channel_id=1, source_target_pairs={{0,16},{16,0},{1,17},{17,1},{2,18},{18,2},{3,19},{19,3},{4,20},{20... | collective-permute-start | bytes 393224 | tf_op jit(solution)/shard_map/ppermute | solution.py:274
  62.4 3.9 %collective-permute-start.21 = (f32[256,128]{1,0:T(8,128)S(1)}, f32[256,128]{1,0:T(8,128)S(1)}, u32[]{:S(2)}, u32[]{:S(2)}) collective-permute-start(f32[256,128]{1,0:T(8,128)S(1)} %get-tuple-element.37.here), channel_id=1, source_target_pairs={{0,1},{1,0},{2,3},{3,2},{4,5},{5,4},{6,7},{7,6},{8,9},{9,8},{10,11... | collective-permute-start | bytes 393224 | tf_op jit(solution)/shard_map/ppermute | solution.py:275
  66.2 1.3 %collective-permute-start.22 = (f32[256,128]{1,0:T(8,128)S(1)}, f32[256,128]{1,0:T(8,128)S(1)}, u32[]{:S(2)}, u32[]{:S(2)}) collective-permute-start(f32[256,128]{1,0:T(8,128)S(1)} %collective-permute-done.20.crossed), channel_id=1, source_target_pairs={{0,1},{1,0},{2,3},{3,2},{4,5},{5,4},{6,7},{7,6},{8,9},{9,8},{10,11... | collective-permute-start | bytes 393224 | tf_op jit(solution)/shard_map/ppermute | solution.py:276
  73.0 3.1 %collective-permute-start.27 = (bf16[120,4096]{1,0:T(8,128)(2,1)S(1)}, bf16[120,4096]{1,0:T(8,128)(2,1)S(1)}, u32[]{:S(2)}, u32[]{:S(2)}) collective-permute-start(bf16[120,4096]{1,0:T(8,128)(2,1)S(1)} %get-tuple-element.45), channel_id=1, source_target_pairs={{0,1},{1,0},{2,3},{3,2},{4,5},{5,4},{6,7},{7,6},{8,9},{9,8},{10,11... | collective-permute-start | bytes 2949128 | tf_op jit(solution)/shard_map/ppermute | solution.py:310
  73.1 2.4 %collective-permute-start.28 = (f32[128]{0:T(128)S(1)}, f32[128]{0:T(128)S(1)}, u32[]{:S(2)}, u32[]{:S(2)}) collective-permute-start(f32[128]{0:T(128)S(1)} %bitcast.23), channel_id=1, source_target_pairs={{0,1},{1,0},{2,3},{3,2},{4,5},{5,4},{6,7},{7,6},{8,9},{9,8},{10,11... | collective-permute-start | bytes 1544 | tf_op jit(solution)/shard_map/ppermute | solution.py:311
  (2 other events, 8.3 us)

commit v6 on v5

--- a/solution.py
+++ b/solution.py
@@ -258,7 +258,7 @@
     last_down = max(k for way in (1, -1) for k, (c, _) in enumerate(slots[way]) if c == 0)
     across_far = {}
     for k in range(3, last_down + 1):
-        send_slot(k, *([mine] if k == 5 else []))
+        send_slot(k, *([mine] if k == 6 else []))
     for d, w in hops:
         if near < d < far:
             across_far[d, w] = lax.ppermute(held[1, d, w], "groups", swap)

time: 77.4 us -> 76.9 us (level)
  starting transfers between devices: 28.3 us -> 26.6 us
  waiting for transfers between devices: 28.4 us -> 29.2 us
    ppermute x2, starting transfers between devices: 2.67 us -> 1.31 us  [gathered_matrices(): across_far[d, w] = lax.ppermute(held[1, d, w], 'groups', swap)]
where the time goes in v6:
time: 76.9 us; the launch traced here: 76.6 us
  waiting for transfers between devices  29.2 us (38%)
  starting transfers between devices  26.6 us (35%)
  Pallas kernels  13.1 us (17%)
  other arithmetic  4.08 us (5%)
  local copies, waits for them, and re-layouts  2.69 us (3%)
  between operations  0.8 us (1%)
    ppermute x18, waiting for transfers between devices, send_slot(): held[chain, distance, way] = lax.ppermute(piece, 'adapter', perms[way])  21.9 us
    ppermute x18, starting transfers between devices, send_slot(): held[chain, distance, way] = lax.ppermute(piece, 'adapter', perms[way])  19.7 us
    pallas_call x1, Pallas kernels, gathered_matrices(): pl.pallas_call(delta_kernel, grid_spec=pltpu.PrefetchScalarGridSpec(num_s...  5.5 us
    pallas_call x2, Pallas kernels, normed(): pl.pallas_call(norm_kernel, grid_spec=pltpu.PrefetchScalarGridSpec(num_sc...  4.83 us
    ppermute x1, waiting for transfers between devices, gathered_matrices(): crossed = lax.ppermute(after(there, across_far[far, 1]), 'groups', swap)  3.94 us
    pallas_call x1, Pallas kernels, gathered_matrices(): pl.pallas_call(codes_kernel, out_shape=[fl(2 * full, 128), fl(2 * full, 1...  2.81 us
    ppermute x1, waiting for transfers between devices, gathered_matrices(): part_back = lax.ppermute(other_part.reshape(-1), 'fsdp', swap)  2.06 us
    reduce_sum x1, other arithmetic, gathered_matrices(): jnp.mean(values * values, axis=-1, keepdims=True) + 1e-05  2.02 us
  transfers between devices with their start and end apart: 29, of which 13 were waited for; matrix products, arithmetic and copies ran while one was open for 7% of the time, Pallas kernels for 10%

profile of v6, /device:TPU:0, one launch (start us, length us, event | category | flops | bytes accessed | tf_op | source)
XLA Modules:
  0.0 76.6 jit_solution(9133274349317360400)
XLA Ops:
  1.7 3.0 %collective-permute-start.5 = (bf16[64,2048]{1,0:T(8,128)(2,1)S(1)}, bf16[64,2048]{1,0:T(8,128)(2,1)}, u32[]{:S(2)}, u32[]{:S(2)}) collective-permute-start(bf16[64,2048]{1,0:T(8,128)(2,1)S(1)} %dynamic-slice_bitcast_fusion.1.rest_0_), channel_id=1, source_target_pairs={{0,2},{4,0},{8,4},{12,8},{14,12},{10,14},{6,10},{2,6},{1,3},{5,1},... | collective-permute-start | bytes 786440 | tf_op jit(solution)/shard_map/ppermute | solution.py:218
  4.8 0.8 select_reduce_fusion
  5.6 2.0 %multiply_reduce_fusion = f32[120]{0:T(128)S(1)} fusion(bf16[120,8192]{1,0:T(8,128)(2,1)} %hidden.3), kind=kLoop, calls=%fused_computation | loop fusion | flops 2949000 | bytes 1966560 | tf_op jit(solution)/shard_map/reduce_sum | solution.py:225
  7.9 0.9 %dynamic-slice_bitcast_fusion = (bf16[32,4096]{1,0:T(8,128)(2,1)}, bf16[32,4096]{1,0:T(8,128)(2,1)}) fusion(bf16[1,64,4096]{2,1,0:T(8,128)(2,1)S(1)} %copy-done.2, s32[]{:T(128)S(6)} %select_n.20, s32[]{:T(128)S(6)} %select_n.18), kind=kLoop, calls=%fused_computation.1 | loop fusion | bytes 1048584 | tf_op jit(solution)/shard_map/dynamic_slice | solution.py:205
  8.7 1.9 %collective-permute-start.13 = (bf16[32,4096]{1,0:T(8,128)(2,1)}, bf16[32,4096]{1,0:T(8,128)(2,1)}, u32[]{:S(2)}, u32[]{:S(2)}) collective-permute-start(bf16[32,4096]{1,0:T(8,128)(2,1)} %get-tuple-element.48), channel_id=1, source_target_pairs={{0,2},{4,0},{8,4},{12,8},{14,12},{10,14},{6,10},{2,6},{1,3},{5,1},... | collective-permute-start | bytes 786440 | tf_op jit(solution)/shard_map/ppermute | solution.py:218
  11.2 2.9 %shard_map.95.theirs = bf16[256,2176]{1,0:T(8,128)(2,1)} custom-call(s32[2]{0:T(128)S(1)} %pad_add_fusion.place, bf16[120,8192]{1,0:T(8,128)(2,1)S(1)} %copy-done.1, bf16[120,8192]{1,0:T(8,128)(2,1)} %collective-permute-done.other, f32[128,2]{1,0:T(8,128)S(1)} %concatenate.7.own_small, f32[128,2]{1,0:T(8,128)S(1)} %collective-permute-done.1.other_small, ...), custom_call_target="tpu_custom_call" | custom-call | flops 1 | bytes 1 | tf_op jit(solution)/shard_map/pallas_call | solution.py:234
  14.1 1.6 %collective-permute-start.6 = (bf16[256,2176]{1,0:T(8,128)(2,1)}, bf16[256,2176]{1,0:T(8,128)(2,1)}, u32[]{:S(2)}, u32[]{:S(2)}) collective-permute-start(bf16[256,2176]{1,0:T(8,128)(2,1)} %shard_map.95.theirs), channel_id=1, source_target_pairs={{0,16},{16,0},{1,17},{17,1},{2,18},{18,2},{3,19},{19,3},{4,20},{20... | collective-permute-start | bytes 3342344 | tf_op jit(solution)/shard_map/ppermute | solution.py:254
  15.7 1.5 %collective-permute-start.3 = (bf16[32,4096]{1,0:T(8,128)(2,1)S(1)}, bf16[32,4096]{1,0:T(8,128)(2,1)}, u32[]{:S(2)}, u32[]{:S(2)}) collective-permute-start(bf16[32,4096]{1,0:T(8,128)(2,1)S(1)} %copy-done.3), channel_id=1, source_target_pairs={{0,2},{4,0},{8,4},{12,8},{14,12},{10,14},{6,10},{2,6},{1,3},{5,1},... | collective-permute-start | bytes 786440 | tf_op jit(solution)/shard_map/ppermute | solution.py:218
  18.0 1.7 %collective-permute-start.14 = (bf16[32,4096]{1,0:T(8,128)(2,1)}, bf16[32,4096]{1,0:T(8,128)(2,1)}, u32[]{:S(2)}, u32[]{:S(2)}) collective-permute-start(bf16[32,4096]{1,0:T(8,128)(2,1)} %collective-permute-done.13.rest_3_), channel_id=1, source_target_pairs={{0,2},{4,0},{8,4},{12,8},{14,12},{10,14},{6,10},{2,6},{1,3},{5,1},... | collective-permute-start | bytes 786440 | tf_op jit(solution)/shard_map/ppermute | solution.py:218
  20.0 5.1 %collective-permute-done.3.rest_4_ = bf16[32,4096]{1,0:T(8,128)(2,1)} collective-permute-done((bf16[32,4096]{1,0:T(8,128)(2,1)S(1)}, bf16[32,4096]{1,0:T(8,128)(2,1)}, u32[]{:S(2)}, u32[]{:S(2)}) %collective-permute-start.3) | collective-permute-done | bytes 262176 | tf_op jit(solution)/shard_map/ppermute | solution.py:218
  25.0 1.5 %collective-permute-done.2.rest_2_ = bf16[32,4096]{1,0:T(8,128)(2,1)} collective-permute-done((bf16[32,4096]{1,0:T(8,128)(2,1)S(1)}, bf16[32,4096]{1,0:T(8,128)(2,1)}, u32[]{:S(2)}, u32[]{:S(2)}) %collective-permute-start.2) | collective-permute-done | bytes 262176 | tf_op jit(solution)/shard_map/ppermute | solution.py:218
  27.1 1.5 %collective-permute-start.8 = (bf16[64,2048]{1,0:T(8,128)(2,1)}, bf16[64,2048]{1,0:T(8,128)(2,1)}, u32[]{:S(2)}, u32[]{:S(2)}) collective-permute-start(bf16[64,2048]{1,0:T(8,128)(2,1)} %collective-permute-done.5.rest_2_), channel_id=1, source_target_pairs={{0,2},{4,0},{8,4},{12,8},{14,12},{10,14},{6,10},{2,6},{1,3},{5,1},... | collective-permute-start | bytes 786440 | tf_op jit(solution)/shard_map/ppermute | solution.py:218
  28.6 2.1 %collective-permute-done.14.rest_7_ = bf16[32,4096]{1,0:T(8,128)(2,1)} collective-permute-done((bf16[32,4096]{1,0:T(8,128)(2,1)}, bf16[32,4096]{1,0:T(8,128)(2,1)}, u32[]{:S(2)}, u32[]{:S(2)}) %collective-permute-start.14) | collective-permute-done | bytes 262176 | tf_op jit(solution)/shard_map/ppermute | solution.py:218
  30.7 1.5 %collective-permute-done.12.rest_5_ = bf16[32,4096]{1,0:T(8,128)(2,1)} collective-permute-done((bf16[32,4096]{1,0:T(8,128)(2,1)}, bf16[32,4096]{1,0:T(8,128)(2,1)}, u32[]{:S(2)}, u32[]{:S(2)}) %collective-permute-start.12) | collective-permute-done | bytes 262176 | tf_op jit(solution)/shard_map/ppermute | solution.py:218
  32.7 1.5 %collective-permute-start.16 = (bf16[32,4096]{1,0:T(8,128)(2,1)}, bf16[32,4096]{1,0:T(8,128)(2,1)}, u32[]{:S(2)}, u32[]{:S(2)}) collective-permute-start(bf16[32,4096]{1,0:T(8,128)(2,1)} %collective-permute-done.14.rest_7_), channel_id=1, source_target_pairs={{0,2},{4,0},{8,4},{12,8},{14,12},{10,14},{6,10},{2,6},{1,3},{5,1},... | collective-permute-start | bytes 786440 | tf_op jit(solution)/shard_map/ppermute | solution.py:218
  34.2 0.7 fusion.1
  35.1 1.9 %shard_map.96.here.mine = bf16[256,2176]{1,0:T(8,128)(2,1)S(1)} custom-call(s32[2]{0:T(128)S(1)} %pad_add_fusion.place, bf16[120,8192]{1,0:T(8,128)(2,1)S(1)} %copy-done.1, bf16[120,8192]{1,0:T(8,128)(2,1)} %collective-permute-done.other, f32[128,2]{1,0:T(8,128)S(1)} %concatenate.7.own_small, f32[128,2]{1,0:T(8,128)S(1)} %collective-permute-done.1.other_small, ...), custom_call_target="tpu_custom_call" | custom-call | flops 1 | bytes 1 | tf_op jit(solution)/shard_map/pallas_call | solution.py:234
  37.0 0.8 %collective-permute-done.7.rest_3_ = bf16[64,2048]{1,0:T(8,128)(2,1)} collective-permute-done((bf16[64,2048]{1,0:T(8,128)(2,1)}, bf16[64,2048]{1,0:T(8,128)(2,1)}, u32[]{:S(2)}, u32[]{:S(2)}) %collective-permute-start.7) | collective-permute-done | bytes 262176 | tf_op jit(solution)/shard_map/ppermute | solution.py:218
  38.3 5.1 %collective-permute-done.15.rest_9_ = bf16[32,4096]{1,0:T(8,128)(2,1)} collective-permute-done((bf16[32,4096]{1,0:T(8,128)(2,1)}, bf16[32,4096]{1,0:T(8,128)(2,1)}, u32[]{:S(2)}, u32[]{:S(2)}) %collective-permute-start.15) | collective-permute-done | bytes 262176 | tf_op jit(solution)/shard_map/ppermute | solution.py:218
  43.4 1.6 %collective-permute-start.18 = (bf16[32,4096]{1,0:T(8,128)(2,1)}, bf16[32,4096]{1,0:T(8,128)(2,1)S(1)}, u32[]{:S(2)}, u32[]{:S(2)}) collective-permute-start(bf16[32,4096]{1,0:T(8,128)(2,1)} %collective-permute-done.16.rest_11_), channel_id=1, source_target_pairs={{0,2},{4,0},{8,4},{12,8},{14,12},{10,14},{6,10},{2,6},{1,3},{5,1},... | collective-permute-start | bytes 786440 | tf_op jit(solution)/shard_map/ppermute | solution.py:218
  45.7 1.6 %collective-permute-start.10 = (bf16[64,2048]{1,0:T(8,128)(2,1)}, bf16[64,2048]{1,0:T(8,128)(2,1)S(1)}, u32[]{:S(2)}, u32[]{:S(2)}) collective-permute-start(bf16[64,2048]{1,0:T(8,128)(2,1)} %collective-permute-done.8.rest_4_), channel_id=1, source_target_pairs={{0,2},{4,0},{8,4},{12,8},{14,12},{10,14},{6,10},{2,6},{1,3},{5,1},... | collective-permute-start | bytes 786440 | tf_op jit(solution)/shard_map/ppermute | solution.py:218
  47.8 4.4 %collective-permute-done.18.rest_13_ = bf16[32,4096]{1,0:T(8,128)(2,1)S(1)} collective-permute-done((bf16[32,4096]{1,0:T(8,128)(2,1)}, bf16[32,4096]{1,0:T(8,128)(2,1)S(1)}, u32[]{:S(2)}, u32[]{:S(2)}) %collective-permute-start.18) | collective-permute-done | bytes 262176 | tf_op jit(solution)/shard_map/ppermute | solution.py:218
  52.2 1.4 %collective-permute-start.19 = (bf16[32,4096]{1,0:T(8,128)(2,1)S(1)}, bf16[32,4096]{1,0:T(8,128)(2,1)S(1)}, u32[]{:S(2)}, u32[]{:S(2)}) collective-permute-start(bf16[32,4096]{1,0:T(8,128)(2,1)S(1)} %collective-permute-done.18.rest_13_), channel_id=1, source_target_pairs={{0,16},{16,0},{1,17},{17,1},{2,18},{18,2},{3,19},{19,3},{4,20},{20... | collective-permute-start | bytes 786440 | tf_op jit(solution)/shard_map/ppermute | solution.py:273
  54.2 1.1 %collective-permute-done.10.rest_6_ = bf16[64,2048]{1,0:T(8,128)(2,1)S(1)} collective-permute-done((bf16[64,2048]{1,0:T(8,128)(2,1)}, bf16[64,2048]{1,0:T(8,128)(2,1)S(1)}, u32[]{:S(2)}, u32[]{:S(2)}) %collective-permute-start.10) | collective-permute-done | bytes 262176 | tf_op jit(solution)/shard_map/ppermute | solution.py:218
  55.7 1.6 %collective-permute-start.25 = (bf16[32,4096]{1,0:T(8,128)(2,1)}, bf16[32,4096]{1,0:T(8,128)(2,1)S(1)}, u32[]{:S(2)}, u32[]{:S(2)}) collective-permute-start(bf16[32,4096]{1,0:T(8,128)(2,1)} %collective-permute-done.3.rest_4_), channel_id=1, source_target_pairs={{0,2},{4,0},{8,4},{12,8},{14,12},{10,14},{6,10},{2,6},{1,3},{5,1},... | collective-permute-start | bytes 786440 | tf_op jit(solution)/shard_map/ppermute | solution.py:218
  57.3 2.8 %shard_map.97 = (f32[256,128]{1,0:T(8,128)S(1)}, f32[256,128]{1,0:T(8,128)S(1)}) custom-call(bf16[256,2176]{1,0:T(8,128)(2,1)S(1)} %shard_map.96.here.mine, bf16[256,2176]{1,0:T(8,128)(2,1)} %collective-permute-done.6.across, f32[1,512]{1,0:T(1,128)S(1)} %convert_element_type.41.ids, bf16[64,2048]{1,0:T(8,128)(2,1)S(1)} %dynamic-slice_bitcast_fusion.1.rest_0_, ...), custom_call_target="tpu_custom_call" | custom-call | flops 1 | bytes 1 | tf_op jit(solution)/shard_map/pallas_call | solution.py:267
  60.2 1.5 %collective-permute-start.20 = (f32[256,128]{1,0:T(8,128)S(1)}, f32[256,128]{1,0:T(8,128)S(1)}, u32[]{:S(2)}, u32[]{:S(2)}) collective-permute-start(f32[256,128]{1,0:T(8,128)S(1)} %get-tuple-element.40), channel_id=1, source_target_pairs={{0,16},{16,0},{1,17},{17,1},{2,18},{18,2},{3,19},{19,3},{4,20},{20... | collective-permute-start | bytes 393224 | tf_op jit(solution)/shard_map/ppermute | solution.py:274
  61.7 3.9 %collective-permute-done.20.crossed = f32[256,128]{1,0:T(8,128)S(1)} collective-permute-done((f32[256,128]{1,0:T(8,128)S(1)}, f32[256,128]{1,0:T(8,128)S(1)}, u32[]{:S(2)}, u32[]{:S(2)}) %collective-permute-start.20) | collective-permute-done | bytes 131104 | tf_op jit(solution)/shard_map/ppermute | solution.py:274
  65.7 1.3 %collective-permute-done.22.beyond = f32[256,128]{1,0:T(8,128)S(1)} collective-permute-done((f32[256,128]{1,0:T(8,128)S(1)}, f32[256,128]{1,0:T(8,128)S(1)}, u32[]{:S(2)}, u32[]{:S(2)}) %collective-permute-start.22) | collective-permute-done | bytes 131104 | tf_op jit(solution)/shard_map/ppermute | solution.py:276
  67.0 5.5 %shard_map.98 = (bf16[120,8192]{1,0:T(8,128)(2,1)}, bf16[120,4096]{1,0:T(8,128)(2,1)S(1)}, f32[1,128]{1,0:T(1,128)S(1)}, f32[1,128]{1,0:T(1,128)S(1)}) custom-call(s32[2]{0:T(128)S(1)} %pad_add_fusion.place, bf16[256,2176]{1,0:T(8,128)(2,1)S(1)} %shard_map.96.here.mine, bf16[256,2176]{1,0:T(8,128)(2,1)} %shard_map.95.theirs, ...), custom_call_target="tpu_custom_call" | custom-call | flops 1 | bytes 1 | tf_op jit(solution)/shard_map/pallas_call | solution.py:282
  73.0 2.1 %collective-permute-done.28 = f32[128]{0:T(128)S(1)} collective-permute-done((f32[128]{0:T(128)S(1)}, f32[128]{0:T(128)S(1)}, u32[]{:S(2)}, u32[]{:S(2)}) %collective-permute-start.28) | collective-permute-done | bytes 544 | tf_op jit(solution)/shard_map/ppermute | solution.py:311
  75.6 1.0 %constant_dynamic-update-slice_fusion = bf16[120,8192]{1,0:T(8,128)(2,1)} fusion(bf16[120,8192]{1,0:T(8,128)(2,1)} %get-tuple-element.44, bf16[120,4096]{1,0:T(8,128)(2,1)S(1)} %collective-permute-done.27, s32[]{:T(128)S(6)} %select_n.21), kind=kLoop, calls=%fused_computation.6 | loop fusion | bytes 1966084 | tf_op jit(solution)/shard_map/dynamic_update_slice | solution.py:312
  (59 shorter events, 8.2 us)
Async XLA Ops:
  0.6 10.5 %copy-start.1 = (bf16[120,8192]{1,0:T(8,128)(2,1)S(1)}, bf16[120,8192]{1,0:T(8,128)(2,1)}, u32[]{:S(2)}) copy-start(bf16[120,8192]{1,0:T(8,128)(2,1)} %hidden.3) | copy-start | bytes 5898244
  0.7 10.4 %copy-start.4 = (bf16[4096]{0:T(1024)(128)(2,1)S(1)}, bf16[4096]{0:T(1024)(128)(2,1)}, u32[]{:S(2)}) copy-start(bf16[4096]{0:T(1024)(128)(2,1)} %param.13) | copy-start | bytes 24580
  0.7 10.5 %collective-permute-start = (bf16[120,8192]{1,0:T(8,128)(2,1)}, bf16[120,8192]{1,0:T(8,128)(2,1)}, u32[]{:S(2)}, u32[]{:S(2)}) collective-permute-start(bf16[120,8192]{1,0:T(8,128)(2,1)} %hidden.3), channel_id=1, source_target_pairs={{0,1},{1,0},{2,3},{3,2},{4,5},{5,4},{6,7},{7,6},{8,9},{9,8},{10,11... | collective-permute-start | bytes 5898248 | tf_op jit(solution)/shard_map/ppermute | solution.py:223
  1.7 12.4 %collective-permute-start.5 = (bf16[64,2048]{1,0:T(8,128)(2,1)S(1)}, bf16[64,2048]{1,0:T(8,128)(2,1)}, u32[]{:S(2)}, u32[]{:S(2)}) collective-permute-start(bf16[64,2048]{1,0:T(8,128)(2,1)S(1)} %dynamic-slice_bitcast_fusion.1.rest_0_), channel_id=1, source_target_pairs={{0,2},{4,0},{8,4},{12,8},{14,12},{10,14},{6,10},{2,6},{1,3},{5,1},... | collective-permute-start | bytes 786440 | tf_op jit(solution)/shard_map/ppermute | solution.py:218
  4.7 9.4 %collective-permute-start.4 = (bf16[64,2048]{1,0:T(8,128)(2,1)S(1)}, bf16[64,2048]{1,0:T(8,128)(2,1)}, u32[]{:S(2)}, u32[]{:S(2)}) collective-permute-start(bf16[64,2048]{1,0:T(8,128)(2,1)S(1)} %dynamic-slice_bitcast_fusion.1.rest_0_), channel_id=1, source_target_pairs={{0,4},{4,8},{8,12},{12,14},{14,10},{10,6},{6,2},{2,0},{1,5},{5,9},... | collective-permute-start | bytes 786440 | tf_op jit(solution)/shard_map/ppermute | solution.py:218
  7.8 2.8 %collective-permute-start.1 = (f32[128,2]{1,0:T(8,128)S(1)}, f32[128,2]{1,0:T(8,128)S(1)}, u32[]{:S(2)}, u32[]{:S(2)}) collective-permute-start(f32[128,2]{1,0:T(8,128)S(1)} %concatenate.7.own_small), channel_id=1, source_target_pairs={{0,1},{1,0},{2,3},{3,2},{4,5},{5,4},{6,7},{7,6},{8,9},{9,8},{10,11... | collective-permute-start | bytes 3080 | tf_op jit(solution)/shard_map/ppermute | solution.py:228
  8.7 9.2 %collective-permute-start.13 = (bf16[32,4096]{1,0:T(8,128)(2,1)}, bf16[32,4096]{1,0:T(8,128)(2,1)}, u32[]{:S(2)}, u32[]{:S(2)}) collective-permute-start(bf16[32,4096]{1,0:T(8,128)(2,1)} %get-tuple-element.48), channel_id=1, source_target_pairs={{0,2},{4,0},{8,4},{12,8},{14,12},{10,14},{6,10},{2,6},{1,3},{5,1},... | collective-permute-start | bytes 786440 | tf_op jit(solution)/shard_map/ppermute | solution.py:218
  10.6 9.0 %collective-permute-start.11 = (bf16[32,4096]{1,0:T(8,128)(2,1)}, bf16[32,4096]{1,0:T(8,128)(2,1)}, u32[]{:S(2)}, u32[]{:S(2)}) collective-permute-start(bf16[32,4096]{1,0:T(8,128)(2,1)} %get-tuple-element.48), channel_id=1, source_target_pairs={{0,4},{4,8},{8,12},{12,14},{14,10},{10,6},{6,2},{2,0},{1,5},{5,9},... | collective-permute-start | bytes 786440 | tf_op jit(solution)/shard_map/ppermute | solution.py:218
  11.2 23.9 %copy-start.5 = (bf16[4096]{0:T(1024)(128)(2,1)S(1)}, bf16[4096]{0:T(1024)(128)(2,1)}, u32[]{:S(2)}) copy-start(bf16[4096]{0:T(1024)(128)(2,1)} %param.14) | copy-start | bytes 24580
  14.1 43.2 %collective-permute-start.6 = (bf16[256,2176]{1,0:T(8,128)(2,1)}, bf16[256,2176]{1,0:T(8,128)(2,1)}, u32[]{:S(2)}, u32[]{:S(2)}) collective-permute-start(bf16[256,2176]{1,0:T(8,128)(2,1)} %shard_map.95.theirs), channel_id=1, source_target_pairs={{0,16},{16,0},{1,17},{17,1},{2,18},{18,2},{3,19},{19,3},{4,20},{20... | collective-permute-start | bytes 3342344 | tf_op jit(solution)/shard_map/ppermute | solution.py:254
  15.7 9.3 %collective-permute-start.3 = (bf16[32,4096]{1,0:T(8,128)(2,1)S(1)}, bf16[32,4096]{1,0:T(8,128)(2,1)}, u32[]{:S(2)}, u32[]{:S(2)}) collective-permute-start(bf16[32,4096]{1,0:T(8,128)(2,1)S(1)} %copy-done.3), channel_id=1, source_target_pairs={{0,2},{4,0},{8,4},{12,8},{14,12},{10,14},{6,10},{2,6},{1,3},{5,1},... | collective-permute-start | bytes 786440 | tf_op jit(solution)/shard_map/ppermute | solution.py:218
  17.2 9.3 %collective-permute-start.2 = (bf16[32,4096]{1,0:T(8,128)(2,1)S(1)}, bf16[32,4096]{1,0:T(8,128)(2,1)}, u32[]{:S(2)}, u32[]{:S(2)}) collective-permute-start(bf16[32,4096]{1,0:T(8,128)(2,1)S(1)} %copy-done.3), channel_id=1, source_target_pairs={{0,4},{4,8},{8,12},{12,14},{14,10},{10,6},{6,2},{2,0},{1,5},{5,9},... | collective-permute-start | bytes 786440 | tf_op jit(solution)/shard_map/ppermute | solution.py:218
  18.0 12.7 %collective-permute-start.14 = (bf16[32,4096]{1,0:T(8,128)(2,1)}, bf16[32,4096]{1,0:T(8,128)(2,1)}, u32[]{:S(2)}, u32[]{:S(2)}) collective-permute-start(bf16[32,4096]{1,0:T(8,128)(2,1)} %collective-permute-done.13.rest_3_), channel_id=1, source_target_pairs={{0,2},{4,0},{8,4},{12,8},{14,12},{10,14},{6,10},{2,6},{1,3},{5,1},... | collective-permute-start | bytes 786440 | tf_op jit(solution)/shard_map/ppermute | solution.py:218
  19.6 12.5 %collective-permute-start.12 = (bf16[32,4096]{1,0:T(8,128)(2,1)}, bf16[32,4096]{1,0:T(8,128)(2,1)}, u32[]{:S(2)}, u32[]{:S(2)}) collective-permute-start(bf16[32,4096]{1,0:T(8,128)(2,1)} %collective-permute-done.11.rest_1_), channel_id=1, source_target_pairs={{0,4},{4,8},{8,12},{12,14},{14,10},{10,6},{6,2},{2,0},{1,5},{5,9},... | collective-permute-start | bytes 786440 | tf_op jit(solution)/shard_map/ppermute | solution.py:218
  26.6 11.2 %collective-permute-start.7 = (bf16[64,2048]{1,0:T(8,128)(2,1)}, bf16[64,2048]{1,0:T(8,128)(2,1)}, u32[]{:S(2)}, u32[]{:S(2)}) collective-permute-start(bf16[64,2048]{1,0:T(8,128)(2,1)} %collective-permute-done.4.rest_1_), channel_id=1, source_target_pairs={{0,4},{4,8},{8,12},{12,14},{14,10},{10,6},{6,2},{2,0},{1,5},{5,9},... | collective-permute-start | bytes 786440 | tf_op jit(solution)/shard_map/ppermute | solution.py:218
  27.1 10.7 %collective-permute-start.8 = (bf16[64,2048]{1,0:T(8,128)(2,1)}, bf16[64,2048]{1,0:T(8,128)(2,1)}, u32[]{:S(2)}, u32[]{:S(2)}) collective-permute-start(bf16[64,2048]{1,0:T(8,128)(2,1)} %collective-permute-done.5.rest_2_), channel_id=1, source_target_pairs={{0,2},{4,0},{8,4},{12,8},{14,12},{10,14},{6,10},{2,6},{1,3},{5,1},... | collective-permute-start | bytes 786440 | tf_op jit(solution)/shard_map/ppermute | solution.py:218
  32.2 11.2 %collective-permute-start.15 = (bf16[32,4096]{1,0:T(8,128)(2,1)}, bf16[32,4096]{1,0:T(8,128)(2,1)}, u32[]{:S(2)}, u32[]{:S(2)}) collective-permute-start(bf16[32,4096]{1,0:T(8,128)(2,1)} %collective-permute-done.12.rest_5_), channel_id=1, source_target_pairs={{0,4},{4,8},{8,12},{12,14},{14,10},{10,6},{6,2},{2,0},{1,5},{5,9},... | collective-permute-start | bytes 786440 | tf_op jit(solution)/shard_map/ppermute | solution.py:218
  32.7 10.7 %collective-permute-start.16 = (bf16[32,4096]{1,0:T(8,128)(2,1)}, bf16[32,4096]{1,0:T(8,128)(2,1)}, u32[]{:S(2)}, u32[]{:S(2)}) collective-permute-start(bf16[32,4096]{1,0:T(8,128)(2,1)} %collective-permute-done.14.rest_7_), channel_id=1, source_target_pairs={{0,2},{4,0},{8,4},{12,8},{14,12},{10,14},{6,10},{2,6},{1,3},{5,1},... | collective-permute-start | bytes 786440 | tf_op jit(solution)/shard_map/ppermute | solution.py:218
  37.8 9.5 %collective-permute-start.9 = (bf16[64,2048]{1,0:T(8,128)(2,1)}, bf16[64,2048]{1,0:T(8,128)(2,1)S(1)}, u32[]{:S(2)}, u32[]{:S(2)}) collective-permute-start(bf16[64,2048]{1,0:T(8,128)(2,1)} %collective-permute-done.7.rest_3_), channel_id=1, source_target_pairs={{0,4},{4,8},{8,12},{12,14},{14,10},{10,6},{6,2},{2,0},{1,5},{5,9},... | collective-permute-start | bytes 786440 | tf_op jit(solution)/shard_map/ppermute | solution.py:218
  43.4 8.7 %collective-permute-start.18 = (bf16[32,4096]{1,0:T(8,128)(2,1)}, bf16[32,4096]{1,0:T(8,128)(2,1)S(1)}, u32[]{:S(2)}, u32[]{:S(2)}) collective-permute-start(bf16[32,4096]{1,0:T(8,128)(2,1)} %collective-permute-done.16.rest_11_), channel_id=1, source_target_pairs={{0,2},{4,0},{8,4},{12,8},{14,12},{10,14},{6,10},{2,6},{1,3},{5,1},... | collective-permute-start | bytes 786440 | tf_op jit(solution)/shard_map/ppermute | solution.py:218
  45.0 8.5 %collective-permute-start.23 = (bf16[32,4096]{1,0:T(8,128)(2,1)}, bf16[32,4096]{1,0:T(8,128)(2,1)S(1)}, u32[]{:S(2)}, u32[]{:S(2)}) collective-permute-start(bf16[32,4096]{1,0:T(8,128)(2,1)} %collective-permute-done.15.rest_9_), channel_id=1, source_target_pairs={{0,16},{16,0},{1,17},{17,1},{2,18},{18,2},{3,19},{19,3},{4,20},{20... | collective-permute-start | bytes 786440 | tf_op jit(solution)/shard_map/ppermute | solution.py:264
  45.7 9.7 %collective-permute-start.10 = (bf16[64,2048]{1,0:T(8,128)(2,1)}, bf16[64,2048]{1,0:T(8,128)(2,1)S(1)}, u32[]{:S(2)}, u32[]{:S(2)}) collective-permute-start(bf16[64,2048]{1,0:T(8,128)(2,1)} %collective-permute-done.8.rest_4_), channel_id=1, source_target_pairs={{0,2},{4,0},{8,4},{12,8},{14,12},{10,14},{6,10},{2,6},{1,3},{5,1},... | collective-permute-start | bytes 786440 | tf_op jit(solution)/shard_map/ppermute | solution.py:218
  47.3 8.4 %collective-permute-start.17 = (bf16[64,2048]{1,0:T(8,128)(2,1)S(1)}, bf16[64,2048]{1,0:T(8,128)(2,1)S(1)}, u32[]{:S(2)}, u32[]{:S(2)}) collective-permute-start(bf16[64,2048]{1,0:T(8,128)(2,1)S(1)} %collective-permute-done.9.rest_5_), channel_id=1, source_target_pairs={{0,4},{4,8},{8,12},{12,14},{14,10},{10,6},{6,2},{2,0},{1,5},{5,9},... | collective-permute-start | bytes 786440 | tf_op jit(solution)/shard_map/ppermute | solution.py:218
  52.2 8.0 %collective-permute-start.19 = (bf16[32,4096]{1,0:T(8,128)(2,1)S(1)}, bf16[32,4096]{1,0:T(8,128)(2,1)S(1)}, u32[]{:S(2)}, u32[]{:S(2)}) collective-permute-start(bf16[32,4096]{1,0:T(8,128)(2,1)S(1)} %collective-permute-done.18.rest_13_), channel_id=1, source_target_pairs={{0,16},{16,0},{1,17},{17,1},{2,18},{18,2},{3,19},{19,3},{4,20},{20... | collective-permute-start | bytes 786440 | tf_op jit(solution)/shard_map/ppermute | solution.py:273
  53.5 12.1 %collective-permute-start.26 = (bf16[32,4096]{1,0:T(8,128)(2,1)}, bf16[32,4096]{1,0:T(8,128)(2,1)S(1)}, u32[]{:S(2)}, u32[]{:S(2)}) collective-permute-start(bf16[32,4096]{1,0:T(8,128)(2,1)} %collective-permute-done.16.rest_11_), channel_id=1, source_target_pairs={{0,16},{16,0},{1,17},{17,1},{2,18},{18,2},{3,19},{19,3},{4,20},{20... | collective-permute-start | bytes 786440 | tf_op jit(solution)/shard_map/ppermute | solution.py:264
  55.3 10.3 %collective-permute-start.24 = (bf16[32,4096]{1,0:T(8,128)(2,1)}, bf16[32,4096]{1,0:T(8,128)(2,1)S(1)}, u32[]{:S(2)}, u32[]{:S(2)}) collective-permute-start(bf16[32,4096]{1,0:T(8,128)(2,1)} %collective-permute-done.2.rest_2_), channel_id=1, source_target_pairs={{0,4},{4,8},{8,12},{12,14},{14,10},{10,6},{6,2},{2,0},{1,5},{5,9},... | collective-permute-start | bytes 786440 | tf_op jit(solution)/shard_map/ppermute | solution.py:218
  55.7 9.9 %collective-permute-start.25 = (bf16[32,4096]{1,0:T(8,128)(2,1)}, bf16[32,4096]{1,0:T(8,128)(2,1)S(1)}, u32[]{:S(2)}, u32[]{:S(2)}) collective-permute-start(bf16[32,4096]{1,0:T(8,128)(2,1)} %collective-permute-done.3.rest_4_), channel_id=1, source_target_pairs={{0,2},{4,0},{8,4},{12,8},{14,12},{10,14},{6,10},{2,6},{1,3},{5,1},... | collective-permute-start | bytes 786440 | tf_op jit(solution)/shard_map/ppermute | solution.py:218
  60.2 5.4 %collective-permute-start.20 = (f32[256,128]{1,0:T(8,128)S(1)}, f32[256,128]{1,0:T(8,128)S(1)}, u32[]{:S(2)}, u32[]{:S(2)}) collective-permute-start(f32[256,128]{1,0:T(8,128)S(1)} %get-tuple-element.40), channel_id=1, source_target_pairs={{0,16},{16,0},{1,17},{17,1},{2,18},{18,2},{3,19},{19,3},{4,20},{20... | collective-permute-start | bytes 393224 | tf_op jit(solution)/shard_map/ppermute | solution.py:274
  61.7 4.0 %collective-permute-start.21 = (f32[256,128]{1,0:T(8,128)S(1)}, f32[256,128]{1,0:T(8,128)S(1)}, u32[]{:S(2)}, u32[]{:S(2)}) collective-permute-start(f32[256,128]{1,0:T(8,128)S(1)} %get-tuple-element.37.here), channel_id=1, source_target_pairs={{0,1},{1,0},{2,3},{3,2},{4,5},{5,4},{6,7},{7,6},{8,9},{9,8},{10,11... | collective-permute-start | bytes 393224 | tf_op jit(solution)/shard_map/ppermute | solution.py:275
  65.6 1.3 %collective-permute-start.22 = (f32[256,128]{1,0:T(8,128)S(1)}, f32[256,128]{1,0:T(8,128)S(1)}, u32[]{:S(2)}, u32[]{:S(2)}) collective-permute-start(f32[256,128]{1,0:T(8,128)S(1)} %collective-permute-done.20.crossed), channel_id=1, source_target_pairs={{0,1},{1,0},{2,3},{3,2},{4,5},{5,4},{6,7},{7,6},{8,9},{9,8},{10,11... | collective-permute-start | bytes 393224 | tf_op jit(solution)/shard_map/ppermute | solution.py:276
  72.5 3.1 %collective-permute-start.27 = (bf16[120,4096]{1,0:T(8,128)(2,1)S(1)}, bf16[120,4096]{1,0:T(8,128)(2,1)S(1)}, u32[]{:S(2)}, u32[]{:S(2)}) collective-permute-start(bf16[120,4096]{1,0:T(8,128)(2,1)S(1)} %get-tuple-element.45), channel_id=1, source_target_pairs={{0,1},{1,0},{2,3},{3,2},{4,5},{5,4},{6,7},{7,6},{8,9},{9,8},{10,11... | collective-permute-start | bytes 2949128 | tf_op jit(solution)/shard_map/ppermute | solution.py:310
  72.6 2.4 %collective-permute-start.28 = (f32[128]{0:T(128)S(1)}, f32[128]{0:T(128)S(1)}, u32[]{:S(2)}, u32[]{:S(2)}) collective-permute-start(f32[128]{0:T(128)S(1)} %bitcast.23), channel_id=1, source_target_pairs={{0,1},{1,0},{2,3},{3,2},{4,5},{5,4},{6,7},{7,6},{8,9},{9,8},{10,11... | collective-permute-start | bytes 1544 | tf_op jit(solution)/shard_map/ppermute | solution.py:311
  (3 other events, 12.8 us)

commit v7 on v6

--- a/solution.py
+++ b/solution.py
@@ -252,7 +252,7 @@
 
     theirs = normed(gain, lambda y: 1 - y)
     across = lax.ppermute(after(theirs, *arrived[1]), "groups", swap)
-    gain, head, ids, *_ = lax.optimization_barrier((gain, head, ids, theirs, *arrived[2]))
+    gain, head, ids, *_ = lax.optimization_barrier((gain, head, ids, theirs, *arrived[1]))
     mine = normed(gain, lambda y: y)
 
     last_down = max(k for way in (1, -1) for k, (c, _) in enumerate(slots[way]) if c == 0)

time: 76.9 us -> 76.9 us (level)
  no operation moved by 1% of the time
where the time goes in v7:
time: 76.9 us; the launch traced here: 76.6 us
  waiting for transfers between devices  29.2 us (38%)
  starting transfers between devices  26.6 us (35%)
  Pallas kernels  13.1 us (17%)
  other arithmetic  4.08 us (5%)
  local copies, waits for them, and re-layouts  2.69 us (3%)
  between operations  0.8 us (1%)
    ppermute x18, waiting for transfers between devices, send_slot(): held[chain, distance, way] = lax.ppermute(piece, 'adapter', perms[way])  21.9 us
    ppermute x18, starting transfers between devices, send_slot(): held[chain, distance, way] = lax.ppermute(piece, 'adapter', perms[way])  19.7 us
    pallas_call x1, Pallas kernels, gathered_matrices(): pl.pallas_call(delta_kernel, grid_spec=pltpu.PrefetchScalarGridSpec(num_s...  5.5 us
    pallas_call x2, Pallas kernels, normed(): pl.pallas_call(norm_kernel, grid_spec=pltpu.PrefetchScalarGridSpec(num_sc...  4.83 us
    ppermute x1, waiting for transfers between devices, gathered_matrices(): crossed = lax.ppermute(after(there, across_far[far, 1]), 'groups', swap)  3.94 us
    pallas_call x1, Pallas kernels, gathered_matrices(): pl.pallas_call(codes_kernel, out_shape=[fl(2 * full, 128), fl(2 * full, 1...  2.81 us
    ppermute x1, waiting for transfers between devices, gathered_matrices(): part_back = lax.ppermute(other_part.reshape(-1), 'fsdp', swap)  2.06 us
    reduce_sum x1, other arithmetic, gathered_matrices(): jnp.mean(values * values, axis=-1, keepdims=True) + 1e-05  2.02 us
  transfers between devices with their start and end apart: 29, of which 13 were waited for; matrix products, arithmetic and copies ran while one was open for 7% of the time, Pallas kernels for 10%

profile of v7, /device:TPU:0, one launch (start us, length us, event | category | flops | bytes accessed | tf_op | source)
XLA Modules:
  0.0 76.6 jit_solution(9133274349317360400)
XLA Ops:
  1.7 3.0 %collective-permute-start.3 = (bf16[64,2048]{1,0:T(8,128)(2,1)S(1)}, bf16[64,2048]{1,0:T(8,128)(2,1)}, u32[]{:S(2)}, u32[]{:S(2)}) collective-permute-start(bf16[64,2048]{1,0:T(8,128)(2,1)S(1)} %dynamic-slice_bitcast_fusion.2.rest_0_), channel_id=1, source_target_pairs={{0,2},{4,0},{8,4},{12,8},{14,12},{10,14},{6,10},{2,6},{1,3},{5,1},... | collective-permute-start | bytes 786440 | tf_op jit(solution)/shard_map/ppermute | solution.py:218
  4.8 0.8 select_reduce_fusion
  5.6 2.0 %multiply_reduce_fusion = f32[120]{0:T(128)S(1)} fusion(bf16[120,8192]{1,0:T(8,128)(2,1)} %hidden.3), kind=kLoop, calls=%fused_computation | loop fusion | flops 2949000 | bytes 1966560 | tf_op jit(solution)/shard_map/reduce_sum | solution.py:225
  7.9 0.9 %dynamic-slice_bitcast_fusion = (bf16[32,4096]{1,0:T(8,128)(2,1)}, bf16[32,4096]{1,0:T(8,128)(2,1)}) fusion(bf16[1,64,4096]{2,1,0:T(8,128)(2,1)S(1)} %copy-done.2, s32[]{:T(128)S(6)} %select_n.20, s32[]{:T(128)S(6)} %select_n.19), kind=kLoop, calls=%fused_computation.1 | loop fusion | bytes 1048584 | tf_op jit(solution)/shard_map/dynamic_slice | solution.py:205
  8.7 1.9 %collective-permute-start.13 = (bf16[32,4096]{1,0:T(8,128)(2,1)}, bf16[32,4096]{1,0:T(8,128)(2,1)}, u32[]{:S(2)}, u32[]{:S(2)}) collective-permute-start(bf16[32,4096]{1,0:T(8,128)(2,1)} %get-tuple-element.48), channel_id=1, source_target_pairs={{0,2},{4,0},{8,4},{12,8},{14,12},{10,14},{6,10},{2,6},{1,3},{5,1},... | collective-permute-start | bytes 786440 | tf_op jit(solution)/shard_map/ppermute | solution.py:218
  11.2 2.9 %shard_map.95.theirs = bf16[256,2176]{1,0:T(8,128)(2,1)} custom-call(s32[2]{0:T(128)S(1)} %pad_add_fusion.place, bf16[120,8192]{1,0:T(8,128)(2,1)S(1)} %copy-done.1, bf16[120,8192]{1,0:T(8,128)(2,1)} %collective-permute-done.other, f32[128,2]{1,0:T(8,128)S(1)} %concatenate.7.own_small, f32[128,2]{1,0:T(8,128)S(1)} %collective-permute-done.1.other_small, ...), custom_call_target="tpu_custom_call" | custom-call | flops 1 | bytes 1 | tf_op jit(solution)/shard_map/pallas_call | solution.py:234
  14.1 1.6 %collective-permute-start.4 = (bf16[256,2176]{1,0:T(8,128)(2,1)}, bf16[256,2176]{1,0:T(8,128)(2,1)}, u32[]{:S(2)}, u32[]{:S(2)}) collective-permute-start(bf16[256,2176]{1,0:T(8,128)(2,1)} %shard_map.95.theirs), channel_id=1, source_target_pairs={{0,16},{16,0},{1,17},{17,1},{2,18},{18,2},{3,19},{19,3},{4,20},{20... | collective-permute-start | bytes 3342344 | tf_op jit(solution)/shard_map/ppermute | solution.py:254
  15.7 1.5 %collective-permute-start.6 = (bf16[32,4096]{1,0:T(8,128)(2,1)S(1)}, bf16[32,4096]{1,0:T(8,128)(2,1)}, u32[]{:S(2)}, u32[]{:S(2)}) collective-permute-start(bf16[32,4096]{1,0:T(8,128)(2,1)S(1)} %copy-done.3), channel_id=1, source_target_pairs={{0,2},{4,0},{8,4},{12,8},{14,12},{10,14},{6,10},{2,6},{1,3},{5,1},... | collective-permute-start | bytes 786440 | tf_op jit(solution)/shard_map/ppermute | solution.py:218
  18.0 1.7 %collective-permute-start.14 = (bf16[32,4096]{1,0:T(8,128)(2,1)}, bf16[32,4096]{1,0:T(8,128)(2,1)}, u32[]{:S(2)}, u32[]{:S(2)}) collective-permute-start(bf16[32,4096]{1,0:T(8,128)(2,1)} %collective-permute-done.13.rest_3_), channel_id=1, source_target_pairs={{0,2},{4,0},{8,4},{12,8},{14,12},{10,14},{6,10},{2,6},{1,3},{5,1},... | collective-permute-start | bytes 786440 | tf_op jit(solution)/shard_map/ppermute | solution.py:218
  20.0 5.1 %collective-permute-done.6.rest_4_ = bf16[32,4096]{1,0:T(8,128)(2,1)} collective-permute-done((bf16[32,4096]{1,0:T(8,128)(2,1)S(1)}, bf16[32,4096]{1,0:T(8,128)(2,1)}, u32[]{:S(2)}, u32[]{:S(2)}) %collective-permute-start.6) | collective-permute-done | bytes 262176 | tf_op jit(solution)/shard_map/ppermute | solution.py:218
  25.0 1.5 %collective-permute-done.5.rest_2_ = bf16[32,4096]{1,0:T(8,128)(2,1)} collective-permute-done((bf16[32,4096]{1,0:T(8,128)(2,1)S(1)}, bf16[32,4096]{1,0:T(8,128)(2,1)}, u32[]{:S(2)}, u32[]{:S(2)}) %collective-permute-start.5) | collective-permute-done | bytes 262176 | tf_op jit(solution)/shard_map/ppermute | solution.py:218
  27.1 1.5 %collective-permute-start.8 = (bf16[64,2048]{1,0:T(8,128)(2,1)}, bf16[64,2048]{1,0:T(8,128)(2,1)}, u32[]{:S(2)}, u32[]{:S(2)}) collective-permute-start(bf16[64,2048]{1,0:T(8,128)(2,1)} %collective-permute-done.3.rest_2_), channel_id=1, source_target_pairs={{0,2},{4,0},{8,4},{12,8},{14,12},{10,14},{6,10},{2,6},{1,3},{5,1},... | collective-permute-start | bytes 786440 | tf_op jit(solution)/shard_map/ppermute | solution.py:218
  28.6 2.1 %collective-permute-done.14.rest_7_ = bf16[32,4096]{1,0:T(8,128)(2,1)} collective-permute-done((bf16[32,4096]{1,0:T(8,128)(2,1)}, bf16[32,4096]{1,0:T(8,128)(2,1)}, u32[]{:S(2)}, u32[]{:S(2)}) %collective-permute-start.14) | collective-permute-done | bytes 262176 | tf_op jit(solution)/shard_map/ppermute | solution.py:218
  30.7 1.5 %collective-permute-done.12.rest_5_ = bf16[32,4096]{1,0:T(8,128)(2,1)} collective-permute-done((bf16[32,4096]{1,0:T(8,128)(2,1)}, bf16[32,4096]{1,0:T(8,128)(2,1)}, u32[]{:S(2)}, u32[]{:S(2)}) %collective-permute-start.12) | collective-permute-done | bytes 262176 | tf_op jit(solution)/shard_map/ppermute | solution.py:218
  32.7 1.5 %collective-permute-start.16 = (bf16[32,4096]{1,0:T(8,128)(2,1)}, bf16[32,4096]{1,0:T(8,128)(2,1)}, u32[]{:S(2)}, u32[]{:S(2)}) collective-permute-start(bf16[32,4096]{1,0:T(8,128)(2,1)} %collective-permute-done.14.rest_7_), channel_id=1, source_target_pairs={{0,2},{4,0},{8,4},{12,8},{14,12},{10,14},{6,10},{2,6},{1,3},{5,1},... | collective-permute-start | bytes 786440 | tf_op jit(solution)/shard_map/ppermute | solution.py:218
  34.2 0.7 fusion.1
  35.1 1.9 %shard_map.96.here.mine = bf16[256,2176]{1,0:T(8,128)(2,1)S(1)} custom-call(s32[2]{0:T(128)S(1)} %pad_add_fusion.place, bf16[120,8192]{1,0:T(8,128)(2,1)S(1)} %copy-done.1, bf16[120,8192]{1,0:T(8,128)(2,1)} %collective-permute-done.other, f32[128,2]{1,0:T(8,128)S(1)} %concatenate.7.own_small, f32[128,2]{1,0:T(8,128)S(1)} %collective-permute-done.1.other_small, ...), custom_call_target="tpu_custom_call" | custom-call | flops 1 | bytes 1 | tf_op jit(solution)/shard_map/pallas_call | solution.py:234
  37.0 0.8 %collective-permute-done.7.rest_3_ = bf16[64,2048]{1,0:T(8,128)(2,1)} collective-permute-done((bf16[64,2048]{1,0:T(8,128)(2,1)}, bf16[64,2048]{1,0:T(8,128)(2,1)}, u32[]{:S(2)}, u32[]{:S(2)}) %collective-permute-start.7) | collective-permute-done | bytes 262176 | tf_op jit(solution)/shard_map/ppermute | solution.py:218
  38.3 5.1 %collective-permute-done.15.rest_9_ = bf16[32,4096]{1,0:T(8,128)(2,1)} collective-permute-done((bf16[32,4096]{1,0:T(8,128)(2,1)}, bf16[32,4096]{1,0:T(8,128)(2,1)}, u32[]{:S(2)}, u32[]{:S(2)}) %collective-permute-start.15) | collective-permute-done | bytes 262176 | tf_op jit(solution)/shard_map/ppermute | solution.py:218
  43.4 1.6 %collective-permute-start.18 = (bf16[32,4096]{1,0:T(8,128)(2,1)}, bf16[32,4096]{1,0:T(8,128)(2,1)S(1)}, u32[]{:S(2)}, u32[]{:S(2)}) collective-permute-start(bf16[32,4096]{1,0:T(8,128)(2,1)} %collective-permute-done.16.rest_11_), channel_id=1, source_target_pairs={{0,2},{4,0},{8,4},{12,8},{14,12},{10,14},{6,10},{2,6},{1,3},{5,1},... | collective-permute-start | bytes 786440 | tf_op jit(solution)/shard_map/ppermute | solution.py:218
  45.7 1.6 %collective-permute-start.10 = (bf16[64,2048]{1,0:T(8,128)(2,1)}, bf16[64,2048]{1,0:T(8,128)(2,1)S(1)}, u32[]{:S(2)}, u32[]{:S(2)}) collective-permute-start(bf16[64,2048]{1,0:T(8,128)(2,1)} %collective-permute-done.8.rest_4_), channel_id=1, source_target_pairs={{0,2},{4,0},{8,4},{12,8},{14,12},{10,14},{6,10},{2,6},{1,3},{5,1},... | collective-permute-start | bytes 786440 | tf_op jit(solution)/shard_map/ppermute | solution.py:218
  47.8 4.4 %collective-permute-done.18.rest_13_ = bf16[32,4096]{1,0:T(8,128)(2,1)S(1)} collective-permute-done((bf16[32,4096]{1,0:T(8,128)(2,1)}, bf16[32,4096]{1,0:T(8,128)(2,1)S(1)}, u32[]{:S(2)}, u32[]{:S(2)}) %collective-permute-start.18) | collective-permute-done | bytes 262176 | tf_op jit(solution)/shard_map/ppermute | solution.py:218
  52.2 1.4 %collective-permute-start.19 = (bf16[32,4096]{1,0:T(8,128)(2,1)S(1)}, bf16[32,4096]{1,0:T(8,128)(2,1)S(1)}, u32[]{:S(2)}, u32[]{:S(2)}) collective-permute-start(bf16[32,4096]{1,0:T(8,128)(2,1)S(1)} %collective-permute-done.18.rest_13_), channel_id=1, source_target_pairs={{0,16},{16,0},{1,17},{17,1},{2,18},{18,2},{3,19},{19,3},{4,20},{20... | collective-permute-start | bytes 786440 | tf_op jit(solution)/shard_map/ppermute | solution.py:273
  54.2 1.1 %collective-permute-done.10.rest_6_ = bf16[64,2048]{1,0:T(8,128)(2,1)S(1)} collective-permute-done((bf16[64,2048]{1,0:T(8,128)(2,1)}, bf16[64,2048]{1,0:T(8,128)(2,1)S(1)}, u32[]{:S(2)}, u32[]{:S(2)}) %collective-permute-start.10) | collective-permute-done | bytes 262176 | tf_op jit(solution)/shard_map/ppermute | solution.py:218
  55.7 1.6 %collective-permute-start.25 = (bf16[32,4096]{1,0:T(8,128)(2,1)}, bf16[32,4096]{1,0:T(8,128)(2,1)S(1)}, u32[]{:S(2)}, u32[]{:S(2)}) collective-permute-start(bf16[32,4096]{1,0:T(8,128)(2,1)} %collective-permute-done.6.rest_4_), channel_id=1, source_target_pairs={{0,2},{4,0},{8,4},{12,8},{14,12},{10,14},{6,10},{2,6},{1,3},{5,1},... | collective-permute-start | bytes 786440 | tf_op jit(solution)/shard_map/ppermute | solution.py:218
  57.3 2.8 %shard_map.97 = (f32[256,128]{1,0:T(8,128)S(1)}, f32[256,128]{1,0:T(8,128)S(1)}) custom-call(bf16[256,2176]{1,0:T(8,128)(2,1)S(1)} %shard_map.96.here.mine, bf16[256,2176]{1,0:T(8,128)(2,1)} %collective-permute-done.4.across, f32[1,512]{1,0:T(1,128)S(1)} %convert_element_type.41.ids, bf16[64,2048]{1,0:T(8,128)(2,1)S(1)} %dynamic-slice_bitcast_fusion.2.rest_0_, ...), custom_call_target="tpu_custom_call" | custom-call | flops 1 | bytes 1 | tf_op jit(solution)/shard_map/pallas_call | solution.py:267
  60.2 1.5 %collective-permute-start.20 = (f32[256,128]{1,0:T(8,128)S(1)}, f32[256,128]{1,0:T(8,128)S(1)}, u32[]{:S(2)}, u32[]{:S(2)}) collective-permute-start(f32[256,128]{1,0:T(8,128)S(1)} %get-tuple-element.40), channel_id=1, source_target_pairs={{0,16},{16,0},{1,17},{17,1},{2,18},{18,2},{3,19},{19,3},{4,20},{20... | collective-permute-start | bytes 393224 | tf_op jit(solution)/shard_map/ppermute | solution.py:274
  61.7 3.9 %collective-permute-done.20.crossed = f32[256,128]{1,0:T(8,128)S(1)} collective-permute-done((f32[256,128]{1,0:T(8,128)S(1)}, f32[256,128]{1,0:T(8,128)S(1)}, u32[]{:S(2)}, u32[]{:S(2)}) %collective-permute-start.20) | collective-permute-done | bytes 131104 | tf_op jit(solution)/shard_map/ppermute | solution.py:274
  65.7 1.3 %collective-permute-done.22.beyond = f32[256,128]{1,0:T(8,128)S(1)} collective-permute-done((f32[256,128]{1,0:T(8,128)S(1)}, f32[256,128]{1,0:T(8,128)S(1)}, u32[]{:S(2)}, u32[]{:S(2)}) %collective-permute-start.22) | collective-permute-done | bytes 131104 | tf_op jit(solution)/shard_map/ppermute | solution.py:276
  67.0 5.5 %shard_map.98 = (bf16[120,8192]{1,0:T(8,128)(2,1)}, bf16[120,4096]{1,0:T(8,128)(2,1)S(1)}, f32[1,128]{1,0:T(1,128)S(1)}, f32[1,128]{1,0:T(1,128)S(1)}) custom-call(s32[2]{0:T(128)S(1)} %pad_add_fusion.place, bf16[256,2176]{1,0:T(8,128)(2,1)S(1)} %shard_map.96.here.mine, bf16[256,2176]{1,0:T(8,128)(2,1)} %shard_map.95.theirs, ...), custom_call_target="tpu_custom_call" | custom-call | flops 1 | bytes 1 | tf_op jit(solution)/shard_map/pallas_call | solution.py:282
  73.0 2.1 %collective-permute-done.28 = f32[128]{0:T(128)S(1)} collective-permute-done((f32[128]{0:T(128)S(1)}, f32[128]{0:T(128)S(1)}, u32[]{:S(2)}, u32[]{:S(2)}) %collective-permute-start.28) | collective-permute-done | bytes 544 | tf_op jit(solution)/shard_map/ppermute | solution.py:311
  75.6 1.0 %constant_dynamic-update-slice_fusion = bf16[120,8192]{1,0:T(8,128)(2,1)} fusion(bf16[120,8192]{1,0:T(8,128)(2,1)} %get-tuple-element.44, bf16[120,4096]{1,0:T(8,128)(2,1)S(1)} %collective-permute-done.27, s32[]{:T(128)S(6)} %select_n.21), kind=kLoop, calls=%fused_computation.6 | loop fusion | bytes 1966084 | tf_op jit(solution)/shard_map/dynamic_update_slice | solution.py:312
  (59 shorter events, 8.2 us)
Async XLA Ops:
  0.6 10.5 %copy-start.1 = (bf16[120,8192]{1,0:T(8,128)(2,1)S(1)}, bf16[120,8192]{1,0:T(8,128)(2,1)}, u32[]{:S(2)}) copy-start(bf16[120,8192]{1,0:T(8,128)(2,1)} %hidden.3) | copy-start | bytes 5898244
  0.7 10.4 %copy-start.4 = (bf16[4096]{0:T(1024)(128)(2,1)S(1)}, bf16[4096]{0:T(1024)(128)(2,1)}, u32[]{:S(2)}) copy-start(bf16[4096]{0:T(1024)(128)(2,1)} %param.13) | copy-start | bytes 24580
  0.7 10.5 %collective-permute-start = (bf16[120,8192]{1,0:T(8,128)(2,1)}, bf16[120,8192]{1,0:T(8,128)(2,1)}, u32[]{:S(2)}, u32[]{:S(2)}) collective-permute-start(bf16[120,8192]{1,0:T(8,128)(2,1)} %hidden.3), channel_id=1, source_target_pairs={{0,1},{1,0},{2,3},{3,2},{4,5},{5,4},{6,7},{7,6},{8,9},{9,8},{10,11... | collective-permute-start | bytes 5898248 | tf_op jit(solution)/shard_map/ppermute | solution.py:223
  1.7 12.4 %collective-permute-start.3 = (bf16[64,2048]{1,0:T(8,128)(2,1)S(1)}, bf16[64,2048]{1,0:T(8,128)(2,1)}, u32[]{:S(2)}, u32[]{:S(2)}) collective-permute-start(bf16[64,2048]{1,0:T(8,128)(2,1)S(1)} %dynamic-slice_bitcast_fusion.2.rest_0_), channel_id=1, source_target_pairs={{0,2},{4,0},{8,4},{12,8},{14,12},{10,14},{6,10},{2,6},{1,3},{5,1},... | collective-permute-start | bytes 786440 | tf_op jit(solution)/shard_map/ppermute | solution.py:218
  4.7 9.4 %collective-permute-start.2 = (bf16[64,2048]{1,0:T(8,128)(2,1)S(1)}, bf16[64,2048]{1,0:T(8,128)(2,1)}, u32[]{:S(2)}, u32[]{:S(2)}) collective-permute-start(bf16[64,2048]{1,0:T(8,128)(2,1)S(1)} %dynamic-slice_bitcast_fusion.2.rest_0_), channel_id=1, source_target_pairs={{0,4},{4,8},{8,12},{12,14},{14,10},{10,6},{6,2},{2,0},{1,5},{5,9},... | collective-permute-start | bytes 786440 | tf_op jit(solution)/shard_map/ppermute | solution.py:218
  7.8 2.8 %collective-permute-start.1 = (f32[128,2]{1,0:T(8,128)S(1)}, f32[128,2]{1,0:T(8,128)S(1)}, u32[]{:S(2)}, u32[]{:S(2)}) collective-permute-start(f32[128,2]{1,0:T(8,128)S(1)} %concatenate.7.own_small), channel_id=1, source_target_pairs={{0,1},{1,0},{2,3},{3,2},{4,5},{5,4},{6,7},{7,6},{8,9},{9,8},{10,11... | collective-permute-start | bytes 3080 | tf_op jit(solution)/shard_map/ppermute | solution.py:228
  8.7 9.2 %collective-permute-start.13 = (bf16[32,4096]{1,0:T(8,128)(2,1)}, bf16[32,4096]{1,0:T(8,128)(2,1)}, u32[]{:S(2)}, u32[]{:S(2)}) collective-permute-start(bf16[32,4096]{1,0:T(8,128)(2,1)} %get-tuple-element.48), channel_id=1, source_target_pairs={{0,2},{4,0},{8,4},{12,8},{14,12},{10,14},{6,10},{2,6},{1,3},{5,1},... | collective-permute-start | bytes 786440 | tf_op jit(solution)/shard_map/ppermute | solution.py:218
  10.6 9.0 %collective-permute-start.11 = (bf16[32,4096]{1,0:T(8,128)(2,1)}, bf16[32,4096]{1,0:T(8,128)(2,1)}, u32[]{:S(2)}, u32[]{:S(2)}) collective-permute-start(bf16[32,4096]{1,0:T(8,128)(2,1)} %get-tuple-element.48), channel_id=1, source_target_pairs={{0,4},{4,8},{8,12},{12,14},{14,10},{10,6},{6,2},{2,0},{1,5},{5,9},... | collective-permute-start | bytes 786440 | tf_op jit(solution)/shard_map/ppermute | solution.py:218
  11.2 23.9 %copy-start.5 = (bf16[4096]{0:T(1024)(128)(2,1)S(1)}, bf16[4096]{0:T(1024)(128)(2,1)}, u32[]{:S(2)}) copy-start(bf16[4096]{0:T(1024)(128)(2,1)} %param.14) | copy-start | bytes 24580
  14.1 43.2 %collective-permute-start.4 = (bf16[256,2176]{1,0:T(8,128)(2,1)}, bf16[256,2176]{1,0:T(8,128)(2,1)}, u32[]{:S(2)}, u32[]{:S(2)}) collective-permute-start(bf16[256,2176]{1,0:T(8,128)(2,1)} %shard_map.95.theirs), channel_id=1, source_target_pairs={{0,16},{16,0},{1,17},{17,1},{2,18},{18,2},{3,19},{19,3},{4,20},{20... | collective-permute-start | bytes 3342344 | tf_op jit(solution)/shard_map/ppermute | solution.py:254
  15.7 9.3 %collective-permute-start.6 = (bf16[32,4096]{1,0:T(8,128)(2,1)S(1)}, bf16[32,4096]{1,0:T(8,128)(2,1)}, u32[]{:S(2)}, u32[]{:S(2)}) collective-permute-start(bf16[32,4096]{1,0:T(8,128)(2,1)S(1)} %copy-done.3), channel_id=1, source_target_pairs={{0,2},{4,0},{8,4},{12,8},{14,12},{10,14},{6,10},{2,6},{1,3},{5,1},... | collective-permute-start | bytes 786440 | tf_op jit(solution)/shard_map/ppermute | solution.py:218
  17.2 9.3 %collective-permute-start.5 = (bf16[32,4096]{1,0:T(8,128)(2,1)S(1)}, bf16[32,4096]{1,0:T(8,128)(2,1)}, u32[]{:S(2)}, u32[]{:S(2)}) collective-permute-start(bf16[32,4096]{1,0:T(8,128)(2,1)S(1)} %copy-done.3), channel_id=1, source_target_pairs={{0,4},{4,8},{8,12},{12,14},{14,10},{10,6},{6,2},{2,0},{1,5},{5,9},... | collective-permute-start | bytes 786440 | tf_op jit(solution)/shard_map/ppermute | solution.py:218
  18.0 12.7 %collective-permute-start.14 = (bf16[32,4096]{1,0:T(8,128)(2,1)}, bf16[32,4096]{1,0:T(8,128)(2,1)}, u32[]{:S(2)}, u32[]{:S(2)}) collective-permute-start(bf16[32,4096]{1,0:T(8,128)(2,1)} %collective-permute-done.13.rest_3_), channel_id=1, source_target_pairs={{0,2},{4,0},{8,4},{12,8},{14,12},{10,14},{6,10},{2,6},{1,3},{5,1},... | collective-permute-start | bytes 786440 | tf_op jit(solution)/shard_map/ppermute | solution.py:218
  19.6 12.5 %collective-permute-start.12 = (bf16[32,4096]{1,0:T(8,128)(2,1)}, bf16[32,4096]{1,0:T(8,128)(2,1)}, u32[]{:S(2)}, u32[]{:S(2)}) collective-permute-start(bf16[32,4096]{1,0:T(8,128)(2,1)} %collective-permute-done.11.rest_1_), channel_id=1, source_target_pairs={{0,4},{4,8},{8,12},{12,14},{14,10},{10,6},{6,2},{2,0},{1,5},{5,9},... | collective-permute-start | bytes 786440 | tf_op jit(solution)/shard_map/ppermute | solution.py:218
  26.6 11.2 %collective-permute-start.7 = (bf16[64,2048]{1,0:T(8,128)(2,1)}, bf16[64,2048]{1,0:T(8,128)(2,1)}, u32[]{:S(2)}, u32[]{:S(2)}) collective-permute-start(bf16[64,2048]{1,0:T(8,128)(2,1)} %collective-permute-done.2.rest_1_), channel_id=1, source_target_pairs={{0,4},{4,8},{8,12},{12,14},{14,10},{10,6},{6,2},{2,0},{1,5},{5,9},... | collective-permute-start | bytes 786440 | tf_op jit(solution)/shard_map/ppermute | solution.py:218
  27.1 10.7 %collective-permute-start.8 = (bf16[64,2048]{1,0:T(8,128)(2,1)}, bf16[64,2048]{1,0:T(8,128)(2,1)}, u32[]{:S(2)}, u32[]{:S(2)}) collective-permute-start(bf16[64,2048]{1,0:T(8,128)(2,1)} %collective-permute-done.3.rest_2_), channel_id=1, source_target_pairs={{0,2},{4,0},{8,4},{12,8},{14,12},{10,14},{6,10},{2,6},{1,3},{5,1},... | collective-permute-start | bytes 786440 | tf_op jit(solution)/shard_map/ppermute | solution.py:218
  32.2 11.2 %collective-permute-start.15 = (bf16[32,4096]{1,0:T(8,128)(2,1)}, bf16[32,4096]{1,0:T(8,128)(2,1)}, u32[]{:S(2)}, u32[]{:S(2)}) collective-permute-start(bf16[32,4096]{1,0:T(8,128)(2,1)} %collective-permute-done.12.rest_5_), channel_id=1, source_target_pairs={{0,4},{4,8},{8,12},{12,14},{14,10},{10,6},{6,2},{2,0},{1,5},{5,9},... | collective-permute-start | bytes 786440 | tf_op jit(solution)/shard_map/ppermute | solution.py:218
  32.7 10.7 %collective-permute-start.16 = (bf16[32,4096]{1,0:T(8,128)(2,1)}, bf16[32,4096]{1,0:T(8,128)(2,1)}, u32[]{:S(2)}, u32[]{:S(2)}) collective-permute-start(bf16[32,4096]{1,0:T(8,128)(2,1)} %collective-permute-done.14.rest_7_), channel_id=1, source_target_pairs={{0,2},{4,0},{8,4},{12,8},{14,12},{10,14},{6,10},{2,6},{1,3},{5,1},... | collective-permute-start | bytes 786440 | tf_op jit(solution)/shard_map/ppermute | solution.py:218
  37.8 9.5 %collective-permute-start.9 = (bf16[64,2048]{1,0:T(8,128)(2,1)}, bf16[64,2048]{1,0:T(8,128)(2,1)S(1)}, u32[]{:S(2)}, u32[]{:S(2)}) collective-permute-start(bf16[64,2048]{1,0:T(8,128)(2,1)} %collective-permute-done.7.rest_3_), channel_id=1, source_target_pairs={{0,4},{4,8},{8,12},{12,14},{14,10},{10,6},{6,2},{2,0},{1,5},{5,9},... | collective-permute-start | bytes 786440 | tf_op jit(solution)/shard_map/ppermute | solution.py:218
  43.4 8.7 %collective-permute-start.18 = (bf16[32,4096]{1,0:T(8,128)(2,1)}, bf16[32,4096]{1,0:T(8,128)(2,1)S(1)}, u32[]{:S(2)}, u32[]{:S(2)}) collective-permute-start(bf16[32,4096]{1,0:T(8,128)(2,1)} %collective-permute-done.16.rest_11_), channel_id=1, source_target_pairs={{0,2},{4,0},{8,4},{12,8},{14,12},{10,14},{6,10},{2,6},{1,3},{5,1},... | collective-permute-start | bytes 786440 | tf_op jit(solution)/shard_map/ppermute | solution.py:218
  45.0 8.5 %collective-permute-start.23 = (bf16[32,4096]{1,0:T(8,128)(2,1)}, bf16[32,4096]{1,0:T(8,128)(2,1)S(1)}, u32[]{:S(2)}, u32[]{:S(2)}) collective-permute-start(bf16[32,4096]{1,0:T(8,128)(2,1)} %collective-permute-done.15.rest_9_), channel_id=1, source_target_pairs={{0,16},{16,0},{1,17},{17,1},{2,18},{18,2},{3,19},{19,3},{4,20},{20... | collective-permute-start | bytes 786440 | tf_op jit(solution)/shard_map/ppermute | solution.py:264
  45.7 9.7 %collective-permute-start.10 = (bf16[64,2048]{1,0:T(8,128)(2,1)}, bf16[64,2048]{1,0:T(8,128)(2,1)S(1)}, u32[]{:S(2)}, u32[]{:S(2)}) collective-permute-start(bf16[64,2048]{1,0:T(8,128)(2,1)} %collective-permute-done.8.rest_4_), channel_id=1, source_target_pairs={{0,2},{4,0},{8,4},{12,8},{14,12},{10,14},{6,10},{2,6},{1,3},{5,1},... | collective-permute-start | bytes 786440 | tf_op jit(solution)/shard_map/ppermute | solution.py:218
  47.3 8.4 %collective-permute-start.17 = (bf16[64,2048]{1,0:T(8,128)(2,1)S(1)}, bf16[64,2048]{1,0:T(8,128)(2,1)S(1)}, u32[]{:S(2)}, u32[]{:S(2)}) collective-permute-start(bf16[64,2048]{1,0:T(8,128)(2,1)S(1)} %collective-permute-done.9.rest_5_), channel_id=1, source_target_pairs={{0,4},{4,8},{8,12},{12,14},{14,10},{10,6},{6,2},{2,0},{1,5},{5,9},... | collective-permute-start | bytes 786440 | tf_op jit(solution)/shard_map/ppermute | solution.py:218
  52.2 8.0 %collective-permute-start.19 = (bf16[32,4096]{1,0:T(8,128)(2,1)S(1)}, bf16[32,4096]{1,0:T(8,128)(2,1)S(1)}, u32[]{:S(2)}, u32[]{:S(2)}) collective-permute-start(bf16[32,4096]{1,0:T(8,128)(2,1)S(1)} %collective-permute-done.18.rest_13_), channel_id=1, source_target_pairs={{0,16},{16,0},{1,17},{17,1},{2,18},{18,2},{3,19},{19,3},{4,20},{20... | collective-permute-start | bytes 786440 | tf_op jit(solution)/shard_map/ppermute | solution.py:273
  53.5 12.1 %collective-permute-start.26 = (bf16[32,4096]{1,0:T(8,128)(2,1)}, bf16[32,4096]{1,0:T(8,128)(2,1)S(1)}, u32[]{:S(2)}, u32[]{:S(2)}) collective-permute-start(bf16[32,4096]{1,0:T(8,128)(2,1)} %collective-permute-done.16.rest_11_), channel_id=1, source_target_pairs={{0,16},{16,0},{1,17},{17,1},{2,18},{18,2},{3,19},{19,3},{4,20},{20... | collective-permute-start | bytes 786440 | tf_op jit(solution)/shard_map/ppermute | solution.py:264
  55.3 10.3 %collective-permute-start.24 = (bf16[32,4096]{1,0:T(8,128)(2,1)}, bf16[32,4096]{1,0:T(8,128)(2,1)S(1)}, u32[]{:S(2)}, u32[]{:S(2)}) collective-permute-start(bf16[32,4096]{1,0:T(8,128)(2,1)} %collective-permute-done.5.rest_2_), channel_id=1, source_target_pairs={{0,4},{4,8},{8,12},{12,14},{14,10},{10,6},{6,2},{2,0},{1,5},{5,9},... | collective-permute-start | bytes 786440 | tf_op jit(solution)/shard_map/ppermute | solution.py:218
  55.7 9.9 %collective-permute-start.25 = (bf16[32,4096]{1,0:T(8,128)(2,1)}, bf16[32,4096]{1,0:T(8,128)(2,1)S(1)}, u32[]{:S(2)}, u32[]{:S(2)}) collective-permute-start(bf16[32,4096]{1,0:T(8,128)(2,1)} %collective-permute-done.6.rest_4_), channel_id=1, source_target_pairs={{0,2},{4,0},{8,4},{12,8},{14,12},{10,14},{6,10},{2,6},{1,3},{5,1},... | collective-permute-start | bytes 786440 | tf_op jit(solution)/shard_map/ppermute | solution.py:218
  60.2 5.4 %collective-permute-start.20 = (f32[256,128]{1,0:T(8,128)S(1)}, f32[256,128]{1,0:T(8,128)S(1)}, u32[]{:S(2)}, u32[]{:S(2)}) collective-permute-start(f32[256,128]{1,0:T(8,128)S(1)} %get-tuple-element.40), channel_id=1, source_target_pairs={{0,16},{16,0},{1,17},{17,1},{2,18},{18,2},{3,19},{19,3},{4,20},{20... | collective-permute-start | bytes 393224 | tf_op jit(solution)/shard_map/ppermute | solution.py:274
  61.7 4.0 %collective-permute-start.21 = (f32[256,128]{1,0:T(8,128)S(1)}, f32[256,128]{1,0:T(8,128)S(1)}, u32[]{:S(2)}, u32[]{:S(2)}) collective-permute-start(f32[256,128]{1,0:T(8,128)S(1)} %get-tuple-element.37.here), channel_id=1, source_target_pairs={{0,1},{1,0},{2,3},{3,2},{4,5},{5,4},{6,7},{7,6},{8,9},{9,8},{10,11... | collective-permute-start | bytes 393224 | tf_op jit(solution)/shard_map/ppermute | solution.py:275
  65.6 1.3 %collective-permute-start.22 = (f32[256,128]{1,0:T(8,128)S(1)}, f32[256,128]{1,0:T(8,128)S(1)}, u32[]{:S(2)}, u32[]{:S(2)}) collective-permute-start(f32[256,128]{1,0:T(8,128)S(1)} %collective-permute-done.20.crossed), channel_id=1, source_target_pairs={{0,1},{1,0},{2,3},{3,2},{4,5},{5,4},{6,7},{7,6},{8,9},{9,8},{10,11... | collective-permute-start | bytes 393224 | tf_op jit(solution)/shard_map/ppermute | solution.py:276
  72.5 3.1 %collective-permute-start.27 = (bf16[120,4096]{1,0:T(8,128)(2,1)S(1)}, bf16[120,4096]{1,0:T(8,128)(2,1)S(1)}, u32[]{:S(2)}, u32[]{:S(2)}) collective-permute-start(bf16[120,4096]{1,0:T(8,128)(2,1)S(1)} %get-tuple-element.45), channel_id=1, source_target_pairs={{0,1},{1,0},{2,3},{3,2},{4,5},{5,4},{6,7},{7,6},{8,9},{9,8},{10,11... | collective-permute-start | bytes 2949128 | tf_op jit(solution)/shard_map/ppermute | solution.py:310
  72.6 2.4 %collective-permute-start.28 = (f32[128]{0:T(128)S(1)}, f32[128]{0:T(128)S(1)}, u32[]{:S(2)}, u32[]{:S(2)}) collective-permute-start(f32[128]{0:T(128)S(1)} %bitcast.23), channel_id=1, source_target_pairs={{0,1},{1,0},{2,3},{3,2},{4,5},{5,4},{6,7},{7,6},{8,9},{9,8},{10,11... | collective-permute-start | bytes 1544 | tf_op jit(solution)/shard_map/ppermute | solution.py:311
  (3 other events, 12.8 us)
